TPU v7x, 768 devices: a whole 4x8x12 slice. The times are simulated.
768 devices in a mesh: dp: 96 (over z, x, core), tensor: 8 (over y).
Axes of the slice: x: 4, y: 8, z: 12, core: 2. Of those that a mesh axis runs over, the one named last changes fastest.
Arguments:
- patches: bfloat16 [98304, 1280], P('dp'), may hold values from -30 to 30
- qkv_weight: bfloat16 [1280, 3840], P(None, 'tensor'), may hold values from -1 to 1
- patch_counts: int32 [1536], replicated, may hold values from 1 to 64
- lend_dest: int32 [96], replicated, may hold values from 0 to 95, as said below
- lend_slot: int32 [96], replicated, may hold values from 0 to 15
- attn_grad: bfloat16 [98304, 1280], P('dp', 'tensor'), may hold values from -6 to 6
Outputs:
- context: bfloat16 [98304, 1280], P('dp', 'tensor')
- input_grad: bfloat16 [98304, 1280], P('dp', 'tensor')
- weight_grad: float32 [3840, 1280], P(('tensor', 'dp'))
Inputs may be any that keep to these rules, and one draw needn't show every extreme that they name: `lend_dest`: a permutation of the data devices that maps every aligned group of 4 consecutive devices onto itself.
All inputs are finite; a program needn't handle non-finite values.
Results may differ from a plain program's by a relative error of at most 0.017.
Values may be sent and summed in bfloat16 or wider, within the bound.
No kernel may reach another device: no remote copies, remote signals or barrier semaphores. Data moves between devices by JAX's collectives and lax.ppermute only.
A program may use at most 64 MiB of HBM per device.

v0:
```python
import jax
import jax.numpy as jnp
from jax import lax
from jax.sharding import PartitionSpec as P

HEADS = 16
IMG_DEV = 16
GROUP = 4
HD = 80


def passed_along(value, axis, steps):
    count = lax.axis_size(axis)
    leading, last = (max(0, -steps), min(count, count - steps))
    return lax.ppermute(value, axis, [(source, source + steps) for source in range(leading, last)])


def attention_pass(full_rows, weight, live_counts, cotangent, head_count):
    row_count = full_rows.shape[0]
    image_count = live_counts.shape[0]
    block_rows = row_count // image_count
    scaling = HD ** (-0.5)
    qkv_half = jnp.dot(full_rows, weight, preferred_element_type=jnp.float32).astype(jnp.bfloat16)
    qkv_half = qkv_half.reshape(image_count, block_rows, head_count, 3, HD)
    queries = qkv_half[:, :, :, 0]
    keys_all = qkv_half[:, :, :, 1]
    values_all = qkv_half[:, :, :, 2]
    positions = jnp.arange(block_rows, dtype=jnp.int32)
    keep_rows = positions[None, :] < live_counts[:, None]
    scores = (
        jnp.einsum("ibhd,ijhd->ihbj", queries, keys_all, preferred_element_type=jnp.float32)
        * scaling
    )
    scores = jnp.where(keep_rows[:, None, None, :], scores, jnp.float32(-1e30))
    row_max = jnp.max(scores, axis=-1, keepdims=True)
    attn_prob = jnp.exp(scores - row_max)
    attn_prob = attn_prob / jnp.sum(attn_prob, axis=-1, keepdims=True)
    prob_half = attn_prob.astype(jnp.bfloat16)
    context = jnp.einsum(
        "ihbj,ijhd->ibhd", prob_half, values_all, preferred_element_type=jnp.float32
    )
    context = jnp.where(keep_rows[:, :, None, None], context, jnp.float32(0.0)).astype(jnp.bfloat16)
    grad_ctx = cotangent.reshape(image_count, block_rows, head_count, HD)
    grad_ctx = jnp.where(keep_rows[:, :, None, None], grad_ctx, jnp.zeros_like(grad_ctx))
    grad_value = jnp.einsum(
        "ihbj,ibhd->ijhd", prob_half, grad_ctx, preferred_element_type=jnp.float32
    ).astype(jnp.bfloat16)
    grad_prob = jnp.einsum(
        "ibhd,ijhd->ihbj", grad_ctx, values_all, preferred_element_type=jnp.float32
    )
    grad_score = attn_prob * (grad_prob - jnp.sum(grad_prob * attn_prob, axis=-1, keepdims=True))
    score_half = grad_score.astype(jnp.bfloat16)
    grad_query = (
        jnp.einsum("ihbj,ijhd->ibhd", score_half, keys_all, preferred_element_type=jnp.float32)
        * scaling
    ).astype(jnp.bfloat16)
    grad_key = (
        jnp.einsum("ihbj,ibhd->ijhd", score_half, queries, preferred_element_type=jnp.float32)
        * scaling
    ).astype(jnp.bfloat16)
    grad_qkv = jnp.stack([grad_query, grad_key, grad_value], axis=3).reshape(
        row_count, head_count * 3 * HD
    )
    return (context.reshape(row_count, head_count * HD), grad_qkv)


def shards(patches, qkv_weight, patch_counts, lend_dest, lend_slot, attn_grad):
    device_count = lax.axis_size("dp")
    my_rank = lax.axis_index("dp")
    tensor_rank = lax.axis_index("tensor")
    row_count = patches.shape[0]
    block_rows = row_count // IMG_DEV
    column_share = patches.shape[1] // lax.axis_size("tensor")
    head_count = HEADS // lax.axis_size("tensor")
    all_ranks = jnp.arange(device_count, dtype=jnp.int32)
    my_slot = lend_slot[my_rank]
    home_rank = lend_dest[my_rank]
    source = jnp.sum(jnp.where(lend_dest == my_rank, all_ranks, 0))
    lent_rows = lax.dynamic_slice_in_dim(patches, my_slot * block_rows, block_rows, 0)
    lent_block = lax.dynamic_slice_in_dim(lent_rows, tensor_rank * column_share, column_share, 1)
    empty_block = jnp.zeros_like(lent_block)
    hosted = jnp.where(source == my_rank, lent_block, empty_block)
    for offset in range(1 - GROUP, GROUP):
        if offset != 0:
            moved = passed_along(lent_block, "dp", offset)
            hosted = jnp.where(source == my_rank - offset, moved, hosted)
    hosted_full = lax.all_gather(hosted, "tensor", axis=1, tiled=True)
    full_rows = lax.dynamic_update_slice_in_dim(patches, hosted_full, my_slot * block_rows, 0)
    live_counts = lax.dynamic_slice_in_dim(patch_counts, my_rank * IMG_DEV, IMG_DEV, 0)
    live_counts = live_counts.at[my_slot].set(patch_counts[source * IMG_DEV + lend_slot[source]])
    context, grad_qkv = attention_pass(full_rows, qkv_weight, live_counts, attn_grad, head_count)
    product = lax.dot_general(
        grad_qkv, full_rows, (((0,), (0,)), ((), ())), preferred_element_type=jnp.float32
    )
    weight_grad = lax.psum_scatter(product / row_count, "dp", scatter_dimension=0, tiled=True)
    partial_value = lax.dot_general(
        grad_qkv, qkv_weight, (((1,), (1,)), ((), ())), preferred_element_type=jnp.float32
    )
    hosted_grad = lax.psum_scatter(
        partial_value.astype(jnp.bfloat16), "tensor", scatter_dimension=1, tiled=True
    )
    back_block = lax.dynamic_slice_in_dim(hosted_grad, my_slot * block_rows, block_rows, 0)
    empty_back = jnp.zeros_like(back_block)
    returned = jnp.where(home_rank == my_rank, back_block, empty_back)
    for offset in range(1 - GROUP, GROUP):
        if offset != 0:
            moved = passed_along(back_block, "dp", offset)
            returned = jnp.where(home_rank == my_rank - offset, moved, returned)
    input_grad = lax.dynamic_update_slice_in_dim(hosted_grad, returned, my_slot * block_rows, 0)
    return (context, input_grad, weight_grad)


def solution(mesh):
    return jax.shard_map(
        shards,
        mesh=mesh,
        in_specs=(P("dp", None), P(None, "tensor"), P(), P(), P(), P("dp", "tensor")),
        out_specs=(P("dp", "tensor"), P("dp", "tensor"), P(("tensor", "dp"), None)),
        check_vma=False,
    )
```

profile of v0, /device:TPU:6, one launch (start us, length us, event | category | flops | bytes accessed | tf_op | source)
XLA Modules:
  0.0 414.1 jit_solution(6171991571901429982)
XLA Ops:
  8.1 3.5 copy.62
  16.5 3.6 collective-permute-start
  20.1 3.4 collective-permute-start.1
  23.5 3.8 collective-permute-start.2
  27.4 1.9 collective-permute-start.3
  29.3 2.2 collective-permute-start.4
  37.0 5.3 %collective-permute-start.5 = (bf16[64,160]{0,1:T(8,128)(2,1)S(1)}, bf16[64,160]{0,1:T(8,128)(2,1)S(1)}, u32[]{:S(2)}, u32[]{:S(2)}) collective-permute-start(bf16[64,160]{0,1:T(8,128)(2,1)S(1)} %copy.53), channel_id=1, source_target_pairs={{24,0},{32,8},{40,16},{48,24},{56,32},{64,40},{72,48},{80,56},{88,... | collective-permute-start | bytes 61448 | tf_op jit(solution)/shard_map/ppermute | solution.py:15
  48.5 25.0 %all-gather = bf16[8,160,64]{1,2,0:T(8,128)(2,1)S(1)} all-gather(bf16[1,160,64]{1,2,0:T(8,128)(2,1)S(1)} %copy.40), channel_id=1, replica_groups=mesh['dp'=96,'tensor'=8] {'tensor'}, dimensions={0}, use_global_device_ids=true | all-gather | bytes 184320 | tf_op jit(solution)/shard_map/all_gather | solution.py:87
  74.5 4.1 %convolution_convert_fusion.1 = bf16[1024,480]{0,1:T(8,128)(2,1)} fusion(bf16[1024,1280]{1,0:T(8,128)(2,1)} %bitcast_dynamic-update-slice_fusion, bf16[1280,480]{0,1:T(8,128)(2,1)S(1)} %copy-done), kind=kOutput, calls=%fused_computation.5 | convolution fusion | flops 1258782720 | bytes 4833280 | tf_op jit(solution)/shard_map/dot_general | solution.py:23
  78.7 2.8 reshape.94
  82.9 2.5 copy.54
  89.6 2.2 fusion.10
  91.8 2.0 multiply_reduce_fusion
  96.4 3.2 copy.50
  99.6 2.2 reshape.97
  101.8 4.3 %convolution_convert_fusion = bf16[1024,1280]{0,1:T(8,128)(2,1)} fusion(bf16[1024,480]{0,1:T(8,128)(2,1)} %reshape.97, bf16[1280,480]{0,1:T(8,128)(2,1)S(1)} %copy-done), kind=kOutput, calls=%fused_computation.1 | convolution fusion | flops 1259601920 | bytes 4833280 | tf_op jit(solution)/shard_map/dot_general | solution.py:96
  107.3 4.6 %convolution_multiply_fusion = f32[480,1280]{1,0:T(8,128)} fusion(bf16[1024,480]{0,1:T(8,128)(2,1)S(1)} %copy-done.4, bf16[1024,1280]{1,0:T(8,128)(2,1)} %bitcast_dynamic-update-slice_fusion), kind=kOutput, calls=%fused_computation.2 | convolution fusion | flops 1258905600 | bytes 6062080 | tf_op jit(solution)/shard_map/dot_general | solution.py:92
  119.0 41.7 %reduce-scatter.2.cloned.1.call-done = bf16[1024,160]{0,1:T(8,128)(2,1)} async-done(((bf16[1024,1280]{0,1:T(8,128)(2,1)}), bf16[1024,160]{0,1:T(8,128)(2,1)}) %reduce-scatter.2.cloned.1.call-update) | async-done | bytes 327696 | tf_op jit(solution)/shard_map/reduce_scatter | solution.py:99
  163.4 2.2 fusion.9
  167.3 3.4 collective-permute-start.7
  170.7 4.7 %collective-permute-start.8 = (bf16[64,160]{0,1:T(8,128)(2,1)S(1)}, bf16[64,160]{0,1:T(8,128)(2,1)S(1)}, u32[]{:S(2)}, u32[]{:S(2)}) collective-permute-start(bf16[64,160]{0,1:T(8,128)(2,1)S(1)} %constant_dynamic-slice_fusion.1), channel_id=1, source_target_pairs={{0,8},{8,16},{16,24},{24,32},{32,40},{40,48},{48,56},{56,64},{64,7... | collective-permute-start | bytes 61448 | tf_op jit(solution)/shard_map/ppermute | solution.py:15
  175.5 1.9 collective-permute-start.9
  179.4 2.7 collective-permute-start.11
  182.1 220.7 %all-reduce.3.cloned.1.call-done = f32[480,1280]{1,0:T(8,128)} async-done(((f32[480,1280]{1,0:T(8,128)}), f32[480,1280]{1,0:T(8,128)}) %all-reduce.3.cloned.1.call-update) | async-done | bytes 2457616
  (70 shorter events, 28.4 us)
Async XLA Ops:
  8.0 66.5 %copy-start = (bf16[1280,480]{0,1:T(8,128)(2,1)S(1)}, bf16[1280,480]{0,1:T(8,128)(2,1)}, u32[]{:S(2)}) copy-start(bf16[1280,480]{0,1:T(8,128)(2,1)} %param.9) | copy-start | bytes 3686404
  8.0 3.6 copy-start.9
  8.0 6.2 %copy-start.8 = (s32[96]{0:T(128)S(1)}, s32[96]{0:T(128)}, u32[]{:S(2)}) copy-start(s32[96]{0:T(128)} %param.12) | copy-start | bytes 1156
  8.0 28.5 %copy-start.7 = (bf16[1024,160]{0,1:T(8,128)(2,1)S(1)}, bf16[1024,160]{0,1:T(8,128)(2,1)}, u32[]{:S(2)}) copy-start(bf16[1024,160]{0,1:T(8,128)(2,1)} %param.13) | copy-start | bytes 983044
  8.0 152.6 %reduce-scatter.2.cloned.1.call-start = ((), (), s32[]{:S(2)}) async-start(), calls=%async_computation.1 | async-start | bytes 2949120 | tf_op jit(solution)/shard_map/reduce_scatter | solution.py:99
  16.5 20.5 %collective-permute-start = (bf16[64,160]{0,1:T(8,128)(2,1)S(1)}, bf16[64,160]{0,1:T(8,128)(2,1)S(1)}, u32[]{:S(2)}, u32[]{:S(2)}) collective-permute-start(bf16[64,160]{0,1:T(8,128)(2,1)S(1)} %copy.53), channel_id=1, source_target_pairs={{0,24},{8,32},{16,40},{24,48},{32,56},{40,64},{48,72},{56,80},{64,... | collective-permute-start | bytes 61448 | tf_op jit(solution)/shard_map/ppermute | solution.py:15
  20.1 28.2 %collective-permute-start.1 = (bf16[64,160]{0,1:T(8,128)(2,1)S(1)}, bf16[64,160]{0,1:T(8,128)(2,1)S(1)}, u32[]{:S(2)}, u32[]{:S(2)}) collective-permute-start(bf16[64,160]{0,1:T(8,128)(2,1)S(1)} %copy.53), channel_id=1, source_target_pairs={{0,16},{8,24},{16,32},{24,40},{32,48},{40,56},{48,64},{56,72},{64,... | collective-permute-start | bytes 61448 | tf_op jit(solution)/shard_map/ppermute | solution.py:15
  23.5 24.8 %collective-permute-start.2 = (bf16[64,160]{0,1:T(8,128)(2,1)S(1)}, bf16[64,160]{0,1:T(8,128)(2,1)S(1)}, u32[]{:S(2)}, u32[]{:S(2)}) collective-permute-start(bf16[64,160]{0,1:T(8,128)(2,1)S(1)} %copy.53), channel_id=1, source_target_pairs={{0,8},{8,16},{16,24},{24,32},{32,40},{40,48},{48,56},{56,64},{64,7... | collective-permute-start | bytes 61448 | tf_op jit(solution)/shard_map/ppermute | solution.py:15
  27.4 20.9 %collective-permute-start.3 = (bf16[64,160]{0,1:T(8,128)(2,1)S(1)}, bf16[64,160]{0,1:T(8,128)(2,1)S(1)}, u32[]{:S(2)}, u32[]{:S(2)}) collective-permute-start(bf16[64,160]{0,1:T(8,128)(2,1)S(1)} %copy.53), channel_id=1, source_target_pairs={{8,0},{16,8},{24,16},{32,24},{40,32},{48,40},{56,48},{64,56},{72,6... | collective-permute-start | bytes 61448 | tf_op jit(solution)/shard_map/ppermute | solution.py:15
  29.3 19.0 %collective-permute-start.4 = (bf16[64,160]{0,1:T(8,128)(2,1)S(1)}, bf16[64,160]{0,1:T(8,128)(2,1)S(1)}, u32[]{:S(2)}, u32[]{:S(2)}) collective-permute-start(bf16[64,160]{0,1:T(8,128)(2,1)S(1)} %copy.53), channel_id=1, source_target_pairs={{16,0},{24,8},{32,16},{40,24},{48,32},{56,40},{64,48},{72,56},{80,... | collective-permute-start | bytes 61448 | tf_op jit(solution)/shard_map/ppermute | solution.py:15
  37.0 11.3 %collective-permute-start.5 = (bf16[64,160]{0,1:T(8,128)(2,1)S(1)}, bf16[64,160]{0,1:T(8,128)(2,1)S(1)}, u32[]{:S(2)}, u32[]{:S(2)}) collective-permute-start(bf16[64,160]{0,1:T(8,128)(2,1)S(1)} %copy.53), channel_id=1, source_target_pairs={{24,0},{32,8},{40,16},{48,24},{56,32},{64,40},{72,48},{80,56},{88,... | collective-permute-start | bytes 61448 | tf_op jit(solution)/shard_map/ppermute | solution.py:15
  82.9 4.2 %copy-start.3 = (bf16[16,64,2,1,80]{1,0,4,3,2:T(8,128)(2,1)S(1)}, bf16[16,64,2,1,80]{1,0,4,3,2:T(8,128)(2,1)}, u32[]{:S(2)}) copy-start(bf16[16,64,2,1,80]{1,0,4,3,2:T(8,128)(2,1)} %get-tuple-element.15) | copy-start | bytes 983044
  88.1 3.6 copy-start.1
  91.8 2.1 copy-start.2
  93.8 1.0 copy-start.6
  106.1 1.2 copy-start.4
  106.1 296.7 %all-reduce.3.cloned.1.call-start = ((), (), s32[]{:S(2)}) async-start(), calls=%async_computation.2 | async-start | bytes 4915200
  111.9 51.5 %copy-start.5 = (bf16[16,64,2,1,80]{4,1,2,0,3:T(8,128)(2,1)S(1)}, bf16[16,64,2,1,80]{4,1,2,0,3:T(8,128)(2,1)}, u32[]{:S(2)}) copy-start(bf16[16,64,2,1,80]{4,1,2,0,3:T(8,128)(2,1)} %copy.54) | copy-start | bytes 983044
  161.5 17.9 %collective-permute-start.6 = (bf16[64,160]{0,1:T(8,128)(2,1)S(1)}, bf16[64,160]{0,1:T(8,128)(2,1)S(1)}, u32[]{:S(2)}, u32[]{:S(2)}) collective-permute-start(bf16[64,160]{0,1:T(8,128)(2,1)S(1)} %constant_dynamic-slice_fusion.1), channel_id=1, source_target_pairs={{0,24},{8,32},{16,40},{24,48},{32,56},{40,64},{48,72},{56,80},{64,... | collective-permute-start | bytes 61448 | tf_op jit(solution)/shard_map/ppermute | solution.py:15
  167.3 237.0 %collective-permute-start.7 = (bf16[64,160]{0,1:T(8,128)(2,1)S(1)}, bf16[64,160]{0,1:T(8,128)(2,1)S(1)}, u32[]{:S(2)}, u32[]{:S(2)}) collective-permute-start(bf16[64,160]{0,1:T(8,128)(2,1)S(1)} %constant_dynamic-slice_fusion.1), channel_id=1, source_target_pairs={{0,16},{8,24},{16,32},{24,40},{32,48},{40,56},{48,64},{56,72},{64,... | collective-permute-start | bytes 61448 | tf_op jit(solution)/shard_map/ppermute | solution.py:15
  170.7 233.5 %collective-permute-start.8 = (bf16[64,160]{0,1:T(8,128)(2,1)S(1)}, bf16[64,160]{0,1:T(8,128)(2,1)S(1)}, u32[]{:S(2)}, u32[]{:S(2)}) collective-permute-start(bf16[64,160]{0,1:T(8,128)(2,1)S(1)} %constant_dynamic-slice_fusion.1), channel_id=1, source_target_pairs={{0,8},{8,16},{16,24},{24,32},{32,40},{40,48},{48,56},{56,64},{64,7... | collective-permute-start | bytes 61448 | tf_op jit(solution)/shard_map/ppermute | solution.py:15
  175.5 228.8 %collective-permute-start.9 = (bf16[64,160]{0,1:T(8,128)(2,1)S(1)}, bf16[64,160]{0,1:T(8,128)(2,1)S(1)}, u32[]{:S(2)}, u32[]{:S(2)}) collective-permute-start(bf16[64,160]{0,1:T(8,128)(2,1)S(1)} %constant_dynamic-slice_fusion.1), channel_id=1, source_target_pairs={{8,0},{16,8},{24,16},{32,24},{40,32},{48,40},{56,48},{64,56},{72,6... | collective-permute-start | bytes 61448 | tf_op jit(solution)/shard_map/ppermute | solution.py:15
  177.4 226.9 %collective-permute-start.10 = (bf16[64,160]{0,1:T(8,128)(2,1)S(1)}, bf16[64,160]{0,1:T(8,128)(2,1)S(1)}, u32[]{:S(2)}, u32[]{:S(2)}) collective-permute-start(bf16[64,160]{0,1:T(8,128)(2,1)S(1)} %constant_dynamic-slice_fusion.1), channel_id=1, source_target_pairs={{16,0},{24,8},{32,16},{40,24},{48,32},{56,40},{64,48},{72,56},{80,... | collective-permute-start | bytes 61448 | tf_op jit(solution)/shard_map/ppermute | solution.py:15
  179.4 224.9 %collective-permute-start.11 = (bf16[64,160]{0,1:T(8,128)(2,1)S(1)}, bf16[64,160]{0,1:T(8,128)(2,1)S(1)}, u32[]{:S(2)}, u32[]{:S(2)}) collective-permute-start(bf16[64,160]{0,1:T(8,128)(2,1)S(1)} %constant_dynamic-slice_fusion.1), channel_id=1, source_target_pairs={{24,0},{32,8},{40,16},{48,24},{56,32},{64,40},{72,48},{80,56},{88,... | collective-permute-start | bytes 61448 | tf_op jit(solution)/shard_map/ppermute | solution.py:15
Sparse Core Ops, SparseCore 0:
  106.2 54.3 reduce-scatter.1
Sparse Core Ops, SparseCore 1:
  112.0 290.7 all-reduce.2
where the time goes:
time: 417 us; the launch traced here: 414 us
  waiting for transfers between devices  262 us (63%)
  starting transfers between devices  37.1 us (9%)
  local copies, waits for them, and re-layouts  31.8 us (8%)
  between operations  31.4 us (8%)
  blocking collectives  25 us (6%)
  matrix products  20.6 us (5%)
  other arithmetic  5.83 us (1%)
    unnamed x3, waiting for transfers between devices  221 us
    reduce_scatter x1, waiting for transfers between devices, shards(): lax.psum_scatter(partial_value.astype(jnp.bfloat16), 'tensor', scatter_di...  41.7 us
    ppermute x12, starting transfers between devices, passed_along(): lax.ppermute(value, axis, [(source, source + steps) for source in range(l...  37 us
    all_gather x1, blocking collectives, shards(): hosted_full = lax.all_gather(hosted, 'tensor', axis=1, tiled=True)  25 us
    unnamed x29, local copies, waits for them, and re-layouts  12.8 us
  transfers between devices with their start and end apart: 14, of which 2 were waited for; matrix products, arithmetic and copies ran while one was open for 4% of the time, Pallas kernels for 0%

commit v1 on v0

v1 whole, which is shorter than its diff:
```python
import functools

import jax
import jax.numpy as jnp
import numpy as np
from jax import lax
from jax.experimental import pallas as pl
from jax.experimental.pallas import tpu as pltpu
from jax.sharding import PartitionSpec as P

HEADS = 16
IMG_DEV = 16
BLOCK = 64
GROUP = 4
HD = 80
D = 1280
ROWS = 1024
SLOT = 128
COLS = 480
PADDED = 6 * SLOT
N_X = 4
N_CORE = 2
Z_NEAR = 4
Z_FAR = 3
BF16 = jnp.bfloat16
F32 = jnp.float32

NT = (((1,), (1,)), ((), ()))
NN = (((1,), (0,)), ((), ()))


def column_spread():
    spread = np.zeros((COLS, PADDED), np.float32)
    for slot in range(6):
        for d in range(HD):
            spread[slot * HD + d, slot * SLOT + d] = 1
    return spread.astype(jnp.bfloat16)


def head_spread():
    spread = np.zeros((2 * HD, 2 * SLOT), np.float32)
    for head in range(2):
        for d in range(HD):
            spread[head * HD + d, head * SLOT + d] = 1
    return spread.astype(jnp.bfloat16)


def owner_order():
    order = np.zeros((512, PADDED), np.float32)
    for c in range(COLS):
        z, x, core, i = c // 40, c % 40 // 10, c % 10 // 5, c % 5
        near, far = z % Z_NEAR, z // Z_NEAR
        order[core * 256 + x * 64 + near * 16 + far * 5 + i, c // HD * SLOT + c % HD] = 1
    return order.astype(jnp.bfloat16)


def dot(a, b, dims):
    return lax.dot_general(a, b, dims, preferred_element_type=F32)


def project_kernel(x_ref, w_ref, spread_ref, qkv_ref, wide_ref):
    @pl.when(pl.program_id(0) == 0)
    def _():
        wide_ref[...] = dot(w_ref[...], spread_ref[...], NN).astype(BF16)

    qkv_ref[...] = dot(x_ref[...], wide_ref[...], NN).astype(BF16)


def project(patches, weight, spread):
    step = 256
    return pl.pallas_call(
        project_kernel,
        grid=(ROWS // step,),
        in_specs=[
            pl.BlockSpec((step, D), lambda i: (i, 0)),
            pl.BlockSpec((D, COLS), lambda i: (0, 0)),
            pl.BlockSpec((COLS, PADDED), lambda i: (0, 0)),
        ],
        out_specs=[
            pl.BlockSpec((step, PADDED), lambda i: (i, 0)),
            pl.BlockSpec((D, PADDED), lambda i: (0, 0)),
        ],
        out_shape=[
            jax.ShapeDtypeStruct((ROWS, PADDED), BF16),
            jax.ShapeDtypeStruct((D, PADDED), BF16),
        ],
        cost_estimate=pl.CostEstimate(flops=2 * ROWS * D * PADDED, bytes_accessed=8_000_000, transcendentals=0),
        name="project",
    )(patches, weight, spread)


def attention_kernel(info_ref, counts_ref, qkv_ref, grad_ref, g0_ref, g1_ref, g2_ref, g3_ref, spread_ref, ctx_ref, dqkv_ref, lent_ref, held_ref):
    step = pl.program_id(0)
    pair = 2 * BLOCK
    scaling = HD ** (-0.5)
    my_slot = info_ref[0]
    pick = info_ref[1]
    here = my_slot // 2 == step
    inside = pl.multiple_of((my_slot % 2) * BLOCK, BLOCK)
    held_ref[...] = grad_ref[...]
    for index, block_ref in enumerate((g0_ref, g1_ref, g2_ref, g3_ref)):
        @pl.when(here & (pick == index))
        def _(block_ref=block_ref):
            held_ref[pl.ds(inside, BLOCK), :] = block_ref[...]

    first = counts_ref[2 * step]
    second = counts_ref[2 * step + 1]
    key = lax.broadcasted_iota(jnp.int32, (pair, pair), 0)
    query = lax.broadcasted_iota(jnp.int32, (pair, pair), 1)
    live = (key < jnp.minimum(first, BLOCK)) | ((key >= BLOCK) & (key < second + BLOCK))
    keep = live & ((key < BLOCK) == (query < BLOCK))
    live_rows = jnp.where(live, 1.0, 0.0)
    wide_grad = dot(held_ref[...], spread_ref[...], NN)
    wide_grad = (wide_grad * jnp.concatenate([live_rows] * 2, axis=1)).astype(BF16)
    contexts = []
    for head in range(2):
        base = head * 3 * SLOT
        q = qkv_ref[:, base : base + SLOT]
        k = qkv_ref[:, base + SLOT : base + 2 * SLOT]
        v = qkv_ref[:, base + 2 * SLOT : base + 3 * SLOT]
        g = wide_grad[:, head * SLOT : (head + 1) * SLOT]
        scores = jnp.where(keep, dot(k, q, NT) * scaling, -1e30)
        top = jnp.max(scores, axis=0, keepdims=True)
        e = jnp.exp(scores - top)
        p = e / jnp.sum(e, axis=0, keepdims=True)
        p_half = p.astype(BF16)
        contexts.append((dot(p.T.astype(BF16), v, NN) * live_rows).astype(BF16))
        dv = dot(p_half, g, NN)
        dp = dot(v, g, NT)
        ds = p * (dp - jnp.sum(dp * p, axis=0, keepdims=True))
        dq = dot(ds.T.astype(BF16), k, NN) * scaling
        dk = dot(ds.astype(BF16), q, NN) * scaling
        dqkv_ref[:, base : base + SLOT] = dq.astype(BF16)
        dqkv_ref[:, base + SLOT : base + 2 * SLOT] = dk.astype(BF16)
        dqkv_ref[:, base + 2 * SLOT : base + 3 * SLOT] = dv.astype(BF16)
    ctx_ref[...] = dot(jnp.concatenate(contexts, axis=1), spread_ref[...], NT).astype(BF16)

    @pl.when(here)
    def _():
        lent_ref[...] = ctx_ref[pl.ds(inside, BLOCK), :]


def attention(info, counts, qkv, grad, blocks, spread):
    pair = 2 * BLOCK
    width = 2 * HD
    whole = lambda i: (0, 0)
    smem = pl.BlockSpec(memory_space=pltpu.SMEM)
    return pl.pallas_call(
        attention_kernel,
        grid=(ROWS // pair,),
        in_specs=[
            smem,
            smem,
            pl.BlockSpec((pair, PADDED), lambda i: (i, 0)),
            pl.BlockSpec((pair, width), lambda i: (i, 0)),
        ]
        + [pl.BlockSpec((BLOCK, width), whole)] * 4
        + [pl.BlockSpec((width, 2 * SLOT), whole)],
        out_specs=[
            pl.BlockSpec((pair, width), lambda i: (i, 0)),
            pl.BlockSpec((pair, PADDED), lambda i: (i, 0)),
            pl.BlockSpec((BLOCK, width), whole),
        ],
        out_shape=[
            jax.ShapeDtypeStruct((ROWS, width), BF16),
            jax.ShapeDtypeStruct((ROWS, PADDED), BF16),
            jax.ShapeDtypeStruct((BLOCK, width), BF16),
        ],
        scratch_shapes=[pltpu.VMEM((pair, width), BF16)],
        cost_estimate=pl.CostEstimate(flops=400_000_000, bytes_accessed=4_000_000, transcendentals=300_000),
        name="attention",
    )(info, counts, qkv, grad, *blocks, spread)


def term_kernel(wide_ref, dqkv_ref, out_ref):
    out_ref[...] = dot(wide_ref[...], dqkv_ref[...], NT).astype(BF16)


def term(wide, dqkv):
    step = 320
    return pl.pallas_call(
        term_kernel,
        grid=(D // step,),
        in_specs=[pl.BlockSpec((step, PADDED), lambda i: (i, 0)), pl.BlockSpec((ROWS, PADDED), lambda i: (0, 0))],
        out_specs=pl.BlockSpec((step, ROWS), lambda i: (i, 0)),
        out_shape=jax.ShapeDtypeStruct((D, ROWS), BF16),
        cost_estimate=pl.CostEstimate(flops=2 * ROWS * D * PADDED, bytes_accessed=6_000_000, transcendentals=0),
        name="term",
    )(wide, dqkv)


def half_kernel(info_ref, order_ref, dqkv_ref, x_ref, out_ref):
    sorted_grad = dot(order_ref[...], dqkv_ref[...], NT).astype(BF16)
    out_ref[...] = (dot(sorted_grad, x_ref[...], NN) * (1.0 / ROWS)).astype(BF16)


def own_kernel(info_ref, order_ref, dqkv_ref, x_ref, other_ref, own_ref, s1_ref, s2_ref, s3_ref, held_ref):
    sorted_grad = dot(order_ref[...], dqkv_ref[...], NT).astype(BF16)
    held_ref[...] = dot(sorted_grad, x_ref[...], NN) * (1.0 / ROWS) + other_ref[...].astype(F32)
    rank = info_ref[3]
    for index, ref in enumerate((own_ref, s1_ref, s2_ref, s3_ref)):
        start = pl.multiple_of(lax.rem(rank + index, N_X) * 64, 64)
        ref[...] = held_ref[pl.ds(start, 64), :].astype(ref.dtype)


def half_specs(flip):
    def order_map(i, info):
        core = info[2]
        return (1 - core if flip else core, 0)

    return [
        pl.BlockSpec((256, PADDED), order_map),
        pl.BlockSpec((ROWS, PADDED), lambda i, info: (0, 0)),
        pl.BlockSpec((ROWS, D), lambda i, info: (0, 0)),
    ]


HALF_COST = pl.CostEstimate(flops=2 * 256 * ROWS * (D + PADDED), bytes_accessed=6_000_000, transcendentals=0)


def other_half(info, order, dqkv, patches):
    return pl.pallas_call(
        half_kernel,
        grid_spec=pltpu.PrefetchScalarGridSpec(
            num_scalar_prefetch=1,
            grid=(1,),
            in_specs=half_specs(True),
            out_specs=pl.BlockSpec((256, D), lambda i, info: (0, 0)),
        ),
        out_shape=jax.ShapeDtypeStruct((256, D), BF16),
        cost_estimate=HALF_COST,
        name="other_half",
    )(info, order, dqkv, patches)


def own_half(info, order, dqkv, patches, received):
    whole = lambda i, info: (0, 0)
    return pl.pallas_call(
        own_kernel,
        grid_spec=pltpu.PrefetchScalarGridSpec(
            num_scalar_prefetch=1,
            grid=(1,),
            in_specs=half_specs(False) + [pl.BlockSpec((256, D), whole)],
            out_specs=[pl.BlockSpec((64, D), whole)] * 4,
            scratch_shapes=[pltpu.VMEM((256, D), F32)],
        ),
        out_shape=[jax.ShapeDtypeStruct((64, D), F32)] + [jax.ShapeDtypeStruct((64, D), BF16)] * 3,
        cost_estimate=HALF_COST,
        name="own_half",
    )(info, order, dqkv, patches, received)


VMEM = pl.BlockSpec(memory_space=pltpu.VMEM)
SMEM = pl.BlockSpec(memory_space=pltpu.SMEM)


def near_kernel(info_ref, own_ref, a_ref, b_ref, c_ref, mine_ref, s1_ref, s2_ref, s3_ref, held_ref):
    held_ref[...] = own_ref[...] + a_ref[...].astype(F32) + b_ref[...].astype(F32) + c_ref[...].astype(F32)
    rank = info_ref[4]
    for index, ref in enumerate((mine_ref, s1_ref, s2_ref, s3_ref)):
        start = pl.multiple_of(lax.rem(rank + index, Z_NEAR) * 16, 16)
        ref[...] = held_ref[pl.ds(start, 16), :].astype(ref.dtype)


def near_sums(info, own, received):
    return pl.pallas_call(
        near_kernel,
        in_specs=[SMEM] + [VMEM] * 4,
        out_specs=[VMEM] * 4,
        out_shape=[jax.ShapeDtypeStruct((16, D), F32)] + [jax.ShapeDtypeStruct((16, D), BF16)] * 3,
        scratch_shapes=[pltpu.VMEM((64, D), F32)],
        name="near_sums",
    )(info, own, *received)


def far_kernel(info_ref, own_ref, a_ref, b_ref, c_ref, mine_ref, s1_ref, s2_ref):
    total = own_ref[...] + a_ref[...].astype(F32) + b_ref[...].astype(F32) + c_ref[...].astype(F32)
    rank = info_ref[5]
    rows = [total[0:8], jnp.concatenate([total[5:10], total[0:3]], axis=0), jnp.concatenate([total[10:15], total[0:3]], axis=0)]
    for index, ref in enumerate((mine_ref, s1_ref, s2_ref)):
        far = lax.rem(rank + index, Z_FAR)
        ref[...] = jnp.where(far == 0, rows[0], jnp.where(far == 1, rows[1], rows[2])).astype(ref.dtype)


def far_sums(info, own, received):
    return pl.pallas_call(
        far_kernel,
        in_specs=[SMEM] + [VMEM] * 4,
        out_specs=[VMEM] * 3,
        out_shape=[jax.ShapeDtypeStruct((8, D), F32)] + [jax.ShapeDtypeStruct((8, D), BF16)] * 2,
        name="far_sums",
    )(info, own, *received)


def last_kernel(own_ref, a_ref, b_ref, out_ref):
    total = own_ref[...] + a_ref[...].astype(F32) + b_ref[...].astype(F32)
    out_ref[...] = total[0:5]


def last_sum(own, received):
    return pl.pallas_call(
        last_kernel,
        in_specs=[VMEM] * 3,
        out_specs=VMEM,
        out_shape=jax.ShapeDtypeStruct((5, D), F32),
        name="last_sum",
    )(own, *received)


def turn_kernel(in_ref, out_ref):
    out_ref[...] = in_ref[...].astype(F32).T.astype(BF16)


def turn(columns):
    return pl.pallas_call(
        turn_kernel,
        in_specs=[VMEM],
        out_specs=VMEM,
        out_shape=jax.ShapeDtypeStruct((ROWS, 2 * HD), BF16),
        name="turn",
    )(columns)


def moved(value, target):
    return lax.ppermute(value, "dp", [(p, target(p)) for p in range(96)])


def xor_step(step):
    return lambda p: p ^ step


def x_step(step):
    return lambda p: p // 8 * 8 + ((p % 8 // 2 + step) % N_X) * 2 + p % 2


def near_step(step):
    def target(p):
        z = p // 8
        return (z // Z_NEAR * Z_NEAR + (z % Z_NEAR + step) % Z_NEAR) * 8 + p % 8

    return target


def far_step(step):
    def target(p):
        z = p // 8
        return ((z // Z_NEAR + step) % Z_FAR * Z_NEAR + z % Z_NEAR) * 8 + p % 8

    return target


def shards(patches, qkv_weight, patch_counts, lend_dest, lend_slot, attn_grad):
    my_rank = lax.axis_index("dp").astype(jnp.int32)
    ranks = jnp.arange(96, dtype=jnp.int32)
    my_slot = lend_slot[my_rank]
    pick = lend_dest[my_rank] ^ my_rank
    source = jnp.sum(jnp.where(lend_dest == my_rank, ranks, 0))
    z = my_rank // 8
    info = jnp.stack([my_slot, pick, my_rank % 2, my_rank % 8 // 2, z % Z_NEAR, z // Z_NEAR, source ^ my_rank, my_rank])
    counts = lax.dynamic_slice_in_dim(patch_counts, my_rank * IMG_DEV, IMG_DEV, 0)
    block = lax.dynamic_slice_in_dim(attn_grad, my_slot * BLOCK, BLOCK, 0)
    blocks = [block] + [moved(block, xor_step(s)) for s in range(1, GROUP)]
    qkv, wide = project(patches, qkv_weight, jnp.asarray(column_spread()))
    context, dqkv, lent = attention(info, counts, qkv, attn_grad, blocks, jnp.asarray(head_spread()))
    terms = term(wide, dqkv)
    summed = lax.psum_scatter(terms, "tensor", scatter_dimension=0, tiled=True)
    order = jnp.asarray(owner_order())
    received = moved(other_half(info, order, dqkv, patches), xor_step(1))
    own, *sends = own_half(info, order, dqkv, patches, received)
    own, *sends = near_sums(info, own, [moved(v, x_step(s + 1)) for s, v in enumerate(sends)])
    own, *sends = far_sums(info, own, [moved(v, near_step(s + 1)) for s, v in enumerate(sends)])
    weight_grad = last_sum(own, [moved(v, far_step(s + 1)) for s, v in enumerate(sends)])
    returned = lent
    for s in range(1, GROUP):
        returned = jnp.where(info[6] == s, moved(lent, xor_step(s)), returned)
    context = lax.dynamic_update_slice_in_dim(context, returned, my_slot * BLOCK, 0)
    return (context, turn(summed), weight_grad)


def solution(mesh):
    return jax.shard_map(
        shards,
        mesh=mesh,
        in_specs=(P("dp", None), P(None, "tensor"), P(), P(), P(), P("dp", "tensor")),
        out_specs=(P("dp", "tensor"), P("dp", "tensor"), P(("tensor", "dp"), None)),
        check_vma=False,
    )
```

time: 417 us -> 143 us (0.34)
  waiting for transfers between devices: 262 us -> 15.4 us
  Pallas kernels: 0 us -> 40.5 us
  blocking collectives: 25 us -> 0 us
  matrix products: 20.6 us -> 0 us
  local copies, waits for them, and re-layouts: 31.8 us -> 14.4 us
  starting transfers between devices: 37.1 us -> 53.1 us
  between operations: 31.4 us -> 16.4 us
  other arithmetic: 5.83 us -> 0.67 us
    unnamed x3 -> x1, waiting for transfers between devices: 221 us -> 0.02 us
    reduce_scatter x1, waiting for transfers between devices: 41.7 us -> 0.01 us  [shards(): summed = lax.psum_scatter(terms, 'tensor', scatter_dimension=0, tiled=True)]
    pallas_call x0 -> x9, Pallas kernels: none -> 40.5 us  [the longest x1 9.8 us: attention(): pl.pallas_call(attention_kernel, grid=(ROWS // pair,), in_specs=[smem, sm...]
    all_gather x1 -> x0, blocking collectives: 25 us -> none  [shards(): hosted_full = lax.all_gather(hosted, 'tensor', axis=1, tiled=True)]
    dot_general x9 -> x0, matrix products: 20.6 us -> none  [the longest x1 4.64 us: shards(): lax.dot_general(grad_qkv, full_rows, (((0,), (0,)), ((), ())), preferred_...]
    ppermute x12 -> x15, starting transfers between devices: 37 us -> 53.1 us  [moved(): return lax.ppermute(value, 'dp', [(p, target(p)) for p in range(96)])]
    ppermute x12 -> x15, waiting for transfers between devices: 0.03 us -> 15.4 us  [moved(): return lax.ppermute(value, 'dp', [(p, target(p)) for p in range(96)])]
    reshape x4 -> x0, local copies, waits for them, and re-layouts: 6.58 us -> none  [the longest x1 2.84 us: attention_pass(): qkv_half = qkv_half.reshape(image_count, block_rows, head_count, 3, HD)]
  transfers between devices with their start and end apart: 14 -> 16, of which waited for: 2 -> 5; matrix products, arithmetic and copies ran while one was open for 4% -> 5% of each run, Pallas kernels for 0% -> 16%
where the time goes in v1:
time: 143 us; the launch traced here: 141 us
  starting transfers between devices  53.1 us (37%)
  Pallas kernels  40.5 us (28%)
  between operations  16.4 us (11%)
  waiting for transfers between devices  15.4 us (11%)
  local copies, waits for them, and re-layouts  14.4 us (10%)
    ppermute x15, starting transfers between devices, moved(): return lax.ppermute(value, 'dp', [(p, target(p)) for p in range(96)])  53.1 us
    ppermute x15, waiting for transfers between devices, moved(): return lax.ppermute(value, 'dp', [(p, target(p)) for p in range(96)])  15.4 us
    unnamed x38, local copies, waits for them, and re-layouts  9.81 us
    pallas_call x1, Pallas kernels, attention(): pl.pallas_call(attention_kernel, grid=(ROWS // pair,), in_specs=[smem, sm...  9.8 us
    pallas_call x1, Pallas kernels, project(): pl.pallas_call(project_kernel, grid=(ROWS // step,), in_specs=[pl.BlockSp...  7.08 us
    pallas_call x1, Pallas kernels, term(): pl.pallas_call(term_kernel, grid=(D // step,), in_specs=[pl.BlockSpec((st...  5.88 us
    pallas_call x1, Pallas kernels, own_half(): pl.pallas_call(own_kernel, grid_spec=pltpu.PrefetchScalarGridSpec(num_sca...  5.59 us
    pallas_call x1, Pallas kernels, other_half(): pl.pallas_call(half_kernel, grid_spec=pltpu.PrefetchScalarGridSpec(num_sc...  5.21 us
  transfers between devices with their start and end apart: 16, of which 5 were waited for; matrix products, arithmetic and copies ran while one was open for 5% of the time, Pallas kernels for 16%

profile of v1, /device:TPU:6, one launch (start us, length us, event | category | flops | bytes accessed | tf_op | source)
XLA Modules:
  0.0 140.5 jit_solution(1152219859904409955)
XLA Ops:
  12.3 2.7 %collective-permute-start.1 = (bf16[64,160]{1,0:T(8,128)(2,1)S(1)}, bf16[64,160]{1,0:T(8,128)(2,1)S(1)}, u32[]{:S(2)}, u32[]{:S(2)}) collective-permute-start(bf16[64,160]{1,0:T(8,128)(2,1)S(1)} %constant_dynamic-slice_fusion.g0_ref), channel_id=1, source_target_pairs={{0,16},{8,24},{16,0},{24,8},{32,48},{40,56},{48,32},{56,40},{64,80... | collective-permute-start | bytes 61448 | tf_op jit(solution)/shard_map/ppermute | solution.py:325
  15.1 2.9 %collective-permute-start.2 = (bf16[64,160]{1,0:T(8,128)(2,1)S(1)}, bf16[64,160]{1,0:T(8,128)(2,1)S(1)}, u32[]{:S(2)}, u32[]{:S(2)}) collective-permute-start(bf16[64,160]{1,0:T(8,128)(2,1)S(1)} %constant_dynamic-slice_fusion.g0_ref), channel_id=1, source_target_pairs={{0,24},{8,16},{16,8},{24,0},{32,56},{40,48},{48,40},{56,32},{64,88... | collective-permute-start | bytes 61448 | tf_op jit(solution)/shard_map/ppermute | solution.py:325
  18.0 2.4 %copy.12.w_ref = bf16[1280,480]{1,0:T(8,128)(2,1)} copy(bf16[1280,480]{0,1:T(8,128)(2,1)} %param.10) | data formatting | bytes 2457600 | tf_op args[1]
  20.4 7.1 %project.1 = (bf16[1024,768]{1,0:T(8,128)(2,1)}, bf16[1280,768]{1,0:T(8,128)(2,1)}) custom-call(bf16[1024,1280]{1,0:T(8,128)(2,1)} %x_ref.5, bf16[1280,480]{1,0:T(8,128)(2,1)} %copy.12.w_ref, bf16[480,768]{1,0:T(8,128)(2,1)} %constant.85.clone.spread_ref), custom_call_target="tpu_custom_call" | custom-call | flops 2013265920 | bytes 8000000 | tf_op jit(solution)/shard_map/project/pallas_call | solution.py:71
  33.5 9.8 %attention.1 = (bf16[1024,160]{1,0:T(8,128)(2,1)}, bf16[1024,768]{1,0:T(8,128)(2,1)}, bf16[64,160]{1,0:T(8,128)(2,1)}) custom-call(s32[8]{0:T(128)} %stack.31.info_ref, s32[16]{0:T(128)} %dynamic_slice.14.counts_ref, bf16[1024,768]{1,0:T(8,128)(2,1)} %get-tuple-element.19.qkv_ref, bf16[1024,160]{1,0:T(8,128)(2,1)} %copy-done, bf16[64,160]{1,0:T(8,128)(2,1)} %copy-done.6, ...), custom_call_target="tpu_custom_call" | custom-call | flops 400000000 | bytes 4000000 | tf_op jit(solution)/shard_map/attention/pallas_call | solution.py:148
  43.3 5.9 %term.1 = bf16[1280,1024]{1,0:T(8,128)(2,1)} custom-call(bf16[1280,768]{1,0:T(8,128)(2,1)} %get-tuple-element.22.wide_ref, bf16[1024,768]{1,0:T(8,128)(2,1)} %get-tuple-element.23.dqkv_ref), custom_call_target="tpu_custom_call" | custom-call | flops 2013265920 | bytes 6000000 | tf_op jit(solution)/shard_map/term/pallas_call | solution.py:181
  49.2 5.2 %other_half.1 = bf16[256,1280]{1,0:T(8,128)(2,1)} custom-call(s32[8]{0:T(128)} %stack.31.info_ref, bf16[512,768]{1,0:T(8,128)(2,1)} %constant.87.clone.order_ref, bf16[1024,768]{1,0:T(8,128)(2,1)} %get-tuple-element.23.dqkv_ref, bf16[1024,1280]{1,0:T(8,128)(2,1)} %x_ref.5), custom_call_target="tpu_custom_call" | custom-call | flops 1073741824 | bytes 6000000 | tf_op jit(solution)/shard_map/other_half/pallas_call | solution.py:222
  54.4 2.3 %collective-permute-start.6 = (bf16[256,1280]{1,0:T(8,128)(2,1)}, bf16[256,1280]{1,0:T(8,128)(2,1)S(1)}, u32[]{:S(2)}, u32[]{:S(2)}) collective-permute-start(bf16[256,1280]{1,0:T(8,128)(2,1)} %other_half.1), channel_id=1, source_target_pairs={{0,8},{8,0},{16,24},{24,16},{32,40},{40,32},{48,56},{56,48},{64,72... | collective-permute-start | bytes 1966088 | tf_op jit(solution)/shard_map/ppermute | solution.py:325
  56.7 2.0 %collective-permute-done.6.other_ref = bf16[256,1280]{1,0:T(8,128)(2,1)S(1)} collective-permute-done((bf16[256,1280]{1,0:T(8,128)(2,1)}, bf16[256,1280]{1,0:T(8,128)(2,1)S(1)}, u32[]{:S(2)}, u32[]{:S(2)}) %collective-permute-start.6) | collective-permute-done | bytes 655392 | tf_op jit(solution)/shard_map/ppermute | solution.py:325
  59.6 5.6 %own_half.1 = (f32[64,1280]{1,0:T(8,128)}, bf16[64,1280]{1,0:T(8,128)(2,1)}, bf16[64,1280]{1,0:T(8,128)(2,1)}, bf16[64,1280]{1,0:T(8,128)(2,1)}) custom-call(s32[8]{0:T(128)} %stack.31.info_ref, bf16[512,768]{1,0:T(8,128)(2,1)} %constant.87.clone.order_ref, bf16[1024,768]{1,0:T(8,128)(2,1)} %get-tuple-element.23.dqkv_ref, bf16[1024,1280]{1,0:T(8,128)(2,1)} %x_ref.5, ...), custom_call_target="tpu_custom_call" | custom-call | flops 1073741824 | bytes 6000000 | tf_op jit(solution)/shard_map/own_half/pallas_call | solution.py:238
  65.2 11.4 %collective-permute-start.7 = (bf16[64,1280]{1,0:T(8,128)(2,1)}, bf16[64,1280]{1,0:T(8,128)(2,1)S(1)}, u32[]{:S(2)}, u32[]{:S(2)}) collective-permute-start(bf16[64,1280]{1,0:T(8,128)(2,1)} %get-tuple-element.25), channel_id=1, source_target_pairs={{0,16},{8,24},{16,32},{24,40},{32,48},{40,56},{48,0},{56,8},{64,80... | collective-permute-start | bytes 491528 | tf_op jit(solution)/shard_map/ppermute | solution.py:325
  78.5 3.0 %collective-permute-start.9 = (bf16[64,1280]{1,0:T(8,128)(2,1)}, bf16[64,1280]{1,0:T(8,128)(2,1)S(1)}, u32[]{:S(2)}, u32[]{:S(2)}) collective-permute-start(bf16[64,1280]{1,0:T(8,128)(2,1)} %get-tuple-element.27), channel_id=1, source_target_pairs={{0,48},{8,56},{16,0},{24,8},{32,16},{40,24},{48,32},{56,40},{64,11... | collective-permute-start | bytes 491528 | tf_op jit(solution)/shard_map/ppermute | solution.py:325
  81.5 2.8 %collective-permute-done.7.a_ref = bf16[64,1280]{1,0:T(8,128)(2,1)S(1)} collective-permute-done((bf16[64,1280]{1,0:T(8,128)(2,1)}, bf16[64,1280]{1,0:T(8,128)(2,1)S(1)}, u32[]{:S(2)}, u32[]{:S(2)}) %collective-permute-start.7) | collective-permute-done | bytes 163872 | tf_op jit(solution)/shard_map/ppermute | solution.py:325
  84.3 2.9 %collective-permute-done.8.b_ref = bf16[64,1280]{1,0:T(8,128)(2,1)S(1)} collective-permute-done((bf16[64,1280]{1,0:T(8,128)(2,1)}, bf16[64,1280]{1,0:T(8,128)(2,1)S(1)}, u32[]{:S(2)}, u32[]{:S(2)}) %collective-permute-start.8) | collective-permute-done | bytes 163872 | tf_op jit(solution)/shard_map/ppermute | solution.py:325
  87.2 2.5 %collective-permute-done.9.c_ref = bf16[64,1280]{1,0:T(8,128)(2,1)S(1)} collective-permute-done((bf16[64,1280]{1,0:T(8,128)(2,1)}, bf16[64,1280]{1,0:T(8,128)(2,1)S(1)}, u32[]{:S(2)}, u32[]{:S(2)}) %collective-permute-start.9) | collective-permute-done | bytes 163872 | tf_op jit(solution)/shard_map/ppermute | solution.py:325
  90.4 2.0 %near_sums.1 = (f32[16,1280]{1,0:T(8,128)}, bf16[16,1280]{1,0:T(8,128)(2,1)}, bf16[16,1280]{1,0:T(8,128)(2,1)}, bf16[16,1280]{1,0:T(8,128)(2,1)}) custom-call(s32[8]{0:T(128)} %stack.31.info_ref, f32[64,1280]{1,0:T(8,128)} %get-tuple-element.24.own_ref, bf16[64,1280]{1,0:T(8,128)(2,1)} %copy-done.3, bf16[64,1280]{1,0:T(8,128)(2,1)} %copy-done.4, ...), custom_call_target="tpu_custom_call" | custom-call | tf_op jit(solution)/shard_map/near_sums/pallas_call | solution.py:266
  96.2 5.7 %collective-permute-start.12 = (bf16[16,1280]{1,0:T(8,128)(2,1)}, bf16[16,1280]{1,0:T(8,128)(2,1)S(1)}, u32[]{:S(2)}, u32[]{:S(2)}) collective-permute-start(bf16[16,1280]{1,0:T(8,128)(2,1)} %get-tuple-element.31), channel_id=1, source_target_pairs={{0,192},{8,200},{16,208},{24,216},{32,224},{40,232},{48,240},{56,2... | collective-permute-start | bytes 122888 | tf_op jit(solution)/shard_map/ppermute | solution.py:325
  103.9 3.1 %collective-permute-start.4 = (bf16[64,160]{1,0:T(8,128)(2,1)S(1)}, bf16[64,160]{1,0:T(8,128)(2,1)S(1)}, u32[]{:S(2)}, u32[]{:S(2)}) collective-permute-start(bf16[64,160]{1,0:T(8,128)(2,1)S(1)} %copy-done.13), channel_id=1, source_target_pairs={{0,16},{8,24},{16,0},{24,8},{32,48},{40,56},{48,32},{56,40},{64,80... | collective-permute-start | bytes 61448 | tf_op jit(solution)/shard_map/ppermute | solution.py:325
  107.0 2.6 %collective-permute-start.5 = (bf16[64,160]{1,0:T(8,128)(2,1)S(1)}, bf16[64,160]{1,0:T(8,128)(2,1)S(1)}, u32[]{:S(2)}, u32[]{:S(2)}) collective-permute-start(bf16[64,160]{1,0:T(8,128)(2,1)S(1)} %copy-done.13), channel_id=1, source_target_pairs={{0,8},{8,0},{16,24},{24,16},{32,40},{40,32},{48,56},{56,48},{64,72... | collective-permute-start | bytes 61448 | tf_op jit(solution)/shard_map/ppermute | solution.py:325
  111.9 5.4 %collective-permute-start.13 = (bf16[8,1280]{1,0:T(8,128)(2,1)}, bf16[8,1280]{1,0:T(8,128)(2,1)S(1)}, u32[]{:S(2)}, u32[]{:S(2)}) collective-permute-start(bf16[8,1280]{1,0:T(8,128)(2,1)} %get-tuple-element.33), channel_id=1, source_target_pairs={{0,256},{8,264},{16,272},{24,280},{32,288},{40,296},{48,304},{56,3... | collective-permute-start | bytes 61448 | tf_op jit(solution)/shard_map/ppermute | solution.py:325
  117.3 4.3 %collective-permute-start.14 = (bf16[8,1280]{1,0:T(8,128)(2,1)}, bf16[8,1280]{1,0:T(8,128)(2,1)S(1)}, u32[]{:S(2)}, u32[]{:S(2)}) collective-permute-start(bf16[8,1280]{1,0:T(8,128)(2,1)} %get-tuple-element.34), channel_id=1, source_target_pairs={{0,512},{8,520},{16,528},{24,536},{32,544},{40,552},{48,560},{56,5... | collective-permute-start | bytes 61448 | tf_op jit(solution)/shard_map/ppermute | solution.py:325
  122.6 5.1 %collective-permute-done.14.b_ref = bf16[8,1280]{1,0:T(8,128)(2,1)S(1)} collective-permute-done((bf16[8,1280]{1,0:T(8,128)(2,1)}, bf16[8,1280]{1,0:T(8,128)(2,1)S(1)}, u32[]{:S(2)}, u32[]{:S(2)}) %collective-permute-start.14) | collective-permute-done | bytes 20512 | tf_op jit(solution)/shard_map/ppermute | solution.py:325
  129.8 2.0 %turn.1 = bf16[1024,160]{1,0:T(8,128)(2,1)} custom-call(bf16[160,1024]{1,0:T(8,128)(2,1)} %reduce-scatter.2.cloned.1.call-done.in_ref), custom_call_target="tpu_custom_call" | custom-call | tf_op jit(solution)/shard_map/turn/pallas_call | solution.py:315
  131.7 1.9 %copy.16 = bf16[1024,160]{0,1:T(8,128)(2,1)} copy(bf16[1024,160]{1,0:T(8,128)(2,1)} %turn.1) | data formatting | bytes 655360
  (63 shorter events, 23.4 us)
Async XLA Ops:
  7.2 122.6 %reduce-scatter.2.cloned.1.call-start = ((), (), s32[]{:S(2)}) async-start(), calls=%async_computation.1 | async-start | bytes 2949120 | tf_op jit(solution)/shard_map/reduce_scatter | solution.py:366
  8.4 19.1 %copy-start = (bf16[1024,160]{1,0:T(8,128)(2,1)}, bf16[1024,160]{1,0:T(8,128)(2,1)S(1)}, u32[]{:S(2)}) copy-start(bf16[1024,160]{1,0:T(8,128)(2,1)S(1)} %copy.14.grad_ref) | copy-start | bytes 983044
  10.4 17.1 %copy-start.6 = (bf16[64,160]{1,0:T(8,128)(2,1)}, bf16[64,160]{1,0:T(8,128)(2,1)S(1)}, u32[]{:S(2)}) copy-start(bf16[64,160]{1,0:T(8,128)(2,1)S(1)} %constant_dynamic-slice_fusion.g0_ref) | copy-start | bytes 61444
  10.4 22.5 %collective-permute-start = (bf16[64,160]{1,0:T(8,128)(2,1)S(1)}, bf16[64,160]{1,0:T(8,128)(2,1)S(1)}, u32[]{:S(2)}, u32[]{:S(2)}) collective-permute-start(bf16[64,160]{1,0:T(8,128)(2,1)S(1)} %constant_dynamic-slice_fusion.g0_ref), channel_id=1, source_target_pairs={{0,8},{8,0},{16,24},{24,16},{32,40},{40,32},{48,56},{56,48},{64,72... | collective-permute-start | bytes 61448 | tf_op jit(solution)/shard_map/ppermute | solution.py:325
  12.3 20.5 %collective-permute-start.1 = (bf16[64,160]{1,0:T(8,128)(2,1)S(1)}, bf16[64,160]{1,0:T(8,128)(2,1)S(1)}, u32[]{:S(2)}, u32[]{:S(2)}) collective-permute-start(bf16[64,160]{1,0:T(8,128)(2,1)S(1)} %constant_dynamic-slice_fusion.g0_ref), channel_id=1, source_target_pairs={{0,16},{8,24},{16,0},{24,8},{32,48},{40,56},{48,32},{56,40},{64,80... | collective-permute-start | bytes 61448 | tf_op jit(solution)/shard_map/ppermute | solution.py:325
  15.1 17.8 %collective-permute-start.2 = (bf16[64,160]{1,0:T(8,128)(2,1)S(1)}, bf16[64,160]{1,0:T(8,128)(2,1)S(1)}, u32[]{:S(2)}, u32[]{:S(2)}) collective-permute-start(bf16[64,160]{1,0:T(8,128)(2,1)S(1)} %constant_dynamic-slice_fusion.g0_ref), channel_id=1, source_target_pairs={{0,24},{8,16},{16,8},{24,0},{32,56},{40,48},{48,40},{56,32},{64,88... | collective-permute-start | bytes 61448 | tf_op jit(solution)/shard_map/ppermute | solution.py:325
  20.4 7.1 %copy-start.16 = (s32[96]{0:T(128)S(1)}, s32[96]{0:T(128)}, u32[]{:S(2)}) copy-start(s32[96]{0:T(128)} %param.12) | copy-start | bytes 1156
  54.4 47.6 %copy-start.13 = (bf16[64,160]{1,0:T(8,128)(2,1)S(1)}, bf16[64,160]{1,0:T(8,128)(2,1)}, u32[]{:S(2)}) copy-start(bf16[64,160]{1,0:T(8,128)(2,1)} %get-tuple-element.21) | copy-start | bytes 61444
  54.4 67.3 %copy-start.2 = (bf16[1024,160]{1,0:T(8,128)(2,1)S(1)}, bf16[1024,160]{1,0:T(8,128)(2,1)}, u32[]{:S(2)}) copy-start(bf16[1024,160]{1,0:T(8,128)(2,1)} %get-tuple-element.20) | copy-start | bytes 983044
  54.4 4.3 %collective-permute-start.6 = (bf16[256,1280]{1,0:T(8,128)(2,1)}, bf16[256,1280]{1,0:T(8,128)(2,1)S(1)}, u32[]{:S(2)}, u32[]{:S(2)}) collective-permute-start(bf16[256,1280]{1,0:T(8,128)(2,1)} %other_half.1), channel_id=1, source_target_pairs={{0,8},{8,0},{16,24},{24,16},{32,40},{40,32},{48,56},{56,48},{64,72... | collective-permute-start | bytes 1966088 | tf_op jit(solution)/shard_map/ppermute | solution.py:325
  65.2 19.1 %collective-permute-start.7 = (bf16[64,1280]{1,0:T(8,128)(2,1)}, bf16[64,1280]{1,0:T(8,128)(2,1)S(1)}, u32[]{:S(2)}, u32[]{:S(2)}) collective-permute-start(bf16[64,1280]{1,0:T(8,128)(2,1)} %get-tuple-element.25), channel_id=1, source_target_pairs={{0,16},{8,24},{16,32},{24,40},{32,48},{40,56},{48,0},{56,8},{64,80... | collective-permute-start | bytes 491528 | tf_op jit(solution)/shard_map/ppermute | solution.py:325
  76.6 10.7 %collective-permute-start.8 = (bf16[64,1280]{1,0:T(8,128)(2,1)}, bf16[64,1280]{1,0:T(8,128)(2,1)S(1)}, u32[]{:S(2)}, u32[]{:S(2)}) collective-permute-start(bf16[64,1280]{1,0:T(8,128)(2,1)} %get-tuple-element.26), channel_id=1, source_target_pairs={{0,32},{8,40},{16,48},{24,56},{32,0},{40,8},{48,16},{56,24},{64,96... | collective-permute-start | bytes 491528 | tf_op jit(solution)/shard_map/ppermute | solution.py:325
  78.5 11.3 %collective-permute-start.9 = (bf16[64,1280]{1,0:T(8,128)(2,1)}, bf16[64,1280]{1,0:T(8,128)(2,1)S(1)}, u32[]{:S(2)}, u32[]{:S(2)}) collective-permute-start(bf16[64,1280]{1,0:T(8,128)(2,1)} %get-tuple-element.27), channel_id=1, source_target_pairs={{0,48},{8,56},{16,0},{24,8},{32,16},{40,24},{48,32},{56,40},{64,11... | collective-permute-start | bytes 491528 | tf_op jit(solution)/shard_map/ppermute | solution.py:325
  84.3 5.5 %copy-start.3 = (bf16[64,1280]{1,0:T(8,128)(2,1)}, bf16[64,1280]{1,0:T(8,128)(2,1)S(1)}, u32[]{:S(2)}) copy-start(bf16[64,1280]{1,0:T(8,128)(2,1)S(1)} %collective-permute-done.7.a_ref) | copy-start | bytes 491524
  92.4 14.6 %collective-permute-start.10 = (bf16[16,1280]{1,0:T(8,128)(2,1)}, bf16[16,1280]{1,0:T(8,128)(2,1)S(1)}, u32[]{:S(2)}, u32[]{:S(2)}) collective-permute-start(bf16[16,1280]{1,0:T(8,128)(2,1)} %get-tuple-element.29), channel_id=1, source_target_pairs={{0,64},{8,72},{16,80},{24,88},{32,96},{40,104},{48,112},{56,120},{... | collective-permute-start | bytes 122888 | tf_op jit(solution)/shard_map/ppermute | solution.py:325
  94.3 15.3 %collective-permute-start.11 = (bf16[16,1280]{1,0:T(8,128)(2,1)}, bf16[16,1280]{1,0:T(8,128)(2,1)S(1)}, u32[]{:S(2)}, u32[]{:S(2)}) collective-permute-start(bf16[16,1280]{1,0:T(8,128)(2,1)} %get-tuple-element.30), channel_id=1, source_target_pairs={{0,128},{8,136},{16,144},{24,152},{32,160},{40,168},{48,176},{56,1... | collective-permute-start | bytes 122888 | tf_op jit(solution)/shard_map/ppermute | solution.py:325
  96.2 13.4 %collective-permute-start.12 = (bf16[16,1280]{1,0:T(8,128)(2,1)}, bf16[16,1280]{1,0:T(8,128)(2,1)S(1)}, u32[]{:S(2)}, u32[]{:S(2)}) collective-permute-start(bf16[16,1280]{1,0:T(8,128)(2,1)} %get-tuple-element.31), channel_id=1, source_target_pairs={{0,192},{8,200},{16,208},{24,216},{32,224},{40,232},{48,240},{56,2... | collective-permute-start | bytes 122888 | tf_op jit(solution)/shard_map/ppermute | solution.py:325
  102.0 19.6 %collective-permute-start.3 = (bf16[64,160]{1,0:T(8,128)(2,1)S(1)}, bf16[64,160]{1,0:T(8,128)(2,1)S(1)}, u32[]{:S(2)}, u32[]{:S(2)}) collective-permute-start(bf16[64,160]{1,0:T(8,128)(2,1)S(1)} %copy-done.13), channel_id=1, source_target_pairs={{0,24},{8,16},{16,8},{24,0},{32,56},{40,48},{48,40},{56,32},{64,88... | collective-permute-start | bytes 61448 | tf_op jit(solution)/shard_map/ppermute | solution.py:325
  103.9 17.7 %collective-permute-start.4 = (bf16[64,160]{1,0:T(8,128)(2,1)S(1)}, bf16[64,160]{1,0:T(8,128)(2,1)S(1)}, u32[]{:S(2)}, u32[]{:S(2)}) collective-permute-start(bf16[64,160]{1,0:T(8,128)(2,1)S(1)} %copy-done.13), channel_id=1, source_target_pairs={{0,16},{8,24},{16,0},{24,8},{32,48},{40,56},{48,32},{56,40},{64,80... | collective-permute-start | bytes 61448 | tf_op jit(solution)/shard_map/ppermute | solution.py:325
  107.0 2.6 %copy-start.7 = (bf16[16,1280]{1,0:T(8,128)(2,1)}, bf16[16,1280]{1,0:T(8,128)(2,1)S(1)}, u32[]{:S(2)}) copy-start(bf16[16,1280]{1,0:T(8,128)(2,1)S(1)} %collective-permute-done.10.a_ref) | copy-start | bytes 122884
  107.0 14.6 %collective-permute-start.5 = (bf16[64,160]{1,0:T(8,128)(2,1)S(1)}, bf16[64,160]{1,0:T(8,128)(2,1)S(1)}, u32[]{:S(2)}, u32[]{:S(2)}) collective-permute-start(bf16[64,160]{1,0:T(8,128)(2,1)S(1)} %copy-done.13), channel_id=1, source_target_pairs={{0,8},{8,0},{16,24},{24,16},{32,40},{40,32},{48,56},{56,48},{64,72... | collective-permute-start | bytes 61448 | tf_op jit(solution)/shard_map/ppermute | solution.py:325
  111.9 10.7 %collective-permute-start.13 = (bf16[8,1280]{1,0:T(8,128)(2,1)}, bf16[8,1280]{1,0:T(8,128)(2,1)S(1)}, u32[]{:S(2)}, u32[]{:S(2)}) collective-permute-start(bf16[8,1280]{1,0:T(8,128)(2,1)} %get-tuple-element.33), channel_id=1, source_target_pairs={{0,256},{8,264},{16,272},{24,280},{32,288},{40,296},{48,304},{56,3... | collective-permute-start | bytes 61448 | tf_op jit(solution)/shard_map/ppermute | solution.py:325
  117.3 10.5 %collective-permute-start.14 = (bf16[8,1280]{1,0:T(8,128)(2,1)}, bf16[8,1280]{1,0:T(8,128)(2,1)S(1)}, u32[]{:S(2)}, u32[]{:S(2)}) collective-permute-start(bf16[8,1280]{1,0:T(8,128)(2,1)} %get-tuple-element.34), channel_id=1, source_target_pairs={{0,512},{8,520},{16,528},{24,536},{32,544},{40,552},{48,560},{56,5... | collective-permute-start | bytes 61448 | tf_op jit(solution)/shard_map/ppermute | solution.py:325
  122.6 5.1 %copy-start.14 = (bf16[8,1280]{1,0:T(8,128)(2,1)}, bf16[8,1280]{1,0:T(8,128)(2,1)S(1)}, u32[]{:S(2)}) copy-start(bf16[8,1280]{1,0:T(8,128)(2,1)S(1)} %collective-permute-done.13.a_ref) | copy-start | bytes 61444
  (9 other events, 7.7 us)
Sparse Core Ops, SparseCore 0:
  49.3 55.6 reduce-scatter.1

commit v2 on v0

v2 whole, which is shorter than its diff:
```python
import jax
import jax.numpy as jnp
import numpy as np
from jax import lax
from jax.experimental import pallas as pl
from jax.experimental.pallas import tpu as pltpu
from jax.sharding import PartitionSpec as P

N_DP = 96
IMG_DEV = 16
BLOCK = 64
GROUP = 4
HD = 80
D = 1280
ROWS = 1024
COLS = 480
WIDTH = 2 * HD
PAIR = 2 * BLOCK
STEP = 2 * PAIR
N_X = 4
N_Z = 12
PACK = 16
BF16 = jnp.bfloat16
F32 = jnp.float32

NT = (((1,), (1,)), ((), ()))
NN = (((1,), (0,)), ((), ()))
TN = (((0,), (0,)), ((), ()))

VMEM = pl.BlockSpec(memory_space=pltpu.VMEM)
SMEM = pl.BlockSpec(memory_space=pltpu.SMEM)


def owner_order():
    order = np.zeros((512, COLS), np.float32)
    for c in range(COLS):
        z, x, core, i = c // 40, c % 40 // 10, c % 10 // 5, c % 5
        order[core * 256 + x * 64 + z * 5 + i, c] = 1
    return order.astype(jnp.bfloat16)


def dot(a, b, dims):
    return lax.dot_general(a, b, dims, preferred_element_type=F32)


def pick_kernel(rank_ref, slot_ref, in_ref, out_ref):
    out_ref[...] = in_ref[...]


def pick(rank, slots, grad):
    return pl.pallas_call(
        pick_kernel,
        grid_spec=pltpu.PrefetchScalarGridSpec(
            num_scalar_prefetch=2,
            grid=(1,),
            in_specs=[pl.BlockSpec((WIDTH, PAIR), lambda i, rank, slots: (0, slots[rank[0]] // 2))],
            out_specs=pl.BlockSpec((WIDTH, PAIR), lambda i, rank, slots: (0, 0)),
        ),
        out_shape=jax.ShapeDtypeStruct((WIDTH, PAIR), BF16),
        name="pick",
    )(rank, slots, grad)


def shifted(tile, flip):
    wide = tile.astype(F32)
    return jnp.where(flip, pltpu.roll(wide, BLOCK, 1), wide)


def block_kernel(rank_ref, slot_ref, dest_ref, counts_ref, w_ref, x_ref, grad_ref, gathered_ref, ctx_ref, dqkv_ref, term_ref, turned_ref):
    step = pl.program_id(0)
    scaling = HD ** (-0.5)

    @pl.when(step == 0)
    def _():
        for start in range(0, D, 256):
            turned_ref[start : start + 256, :] = w_ref[:, start : start + 256].astype(F32).T.astype(BF16)

    me = rank_ref[0]
    slot = slot_ref[me]
    host = dest_ref[me]
    lane = lax.broadcasted_iota(jnp.int32, (WIDTH, PAIR), 1)
    tile = gathered_ref[pl.ds(pl.multiple_of(lax.rem(host, GROUP) * WIDTH, 16), WIDTH), :]
    lent = shifted(tile, lax.rem(slot_ref[host], 2) != lax.rem(slot, 2))
    lent_lanes = (lane >= BLOCK) == (lax.rem(slot, 2) == 1)

    qkv = dot(w_ref[...], x_ref[...], NT).astype(BF16)
    key = lax.broadcasted_iota(jnp.int32, (PAIR, PAIR), 0)
    query = lax.broadcasted_iota(jnp.int32, (PAIR, PAIR), 1)
    same = (key < BLOCK) == (query < BLOCK)
    for pair in range(STEP // PAIR):
        columns = slice(pair * PAIR, (pair + 1) * PAIR)
        number = step * (STEP // PAIR) + pair
        first = counts_ref[me * IMG_DEV + 2 * number]
        second = counts_ref[me * IMG_DEV + 2 * number + 1]
        keep = ((key < first) | ((key >= BLOCK) & (key < second + BLOCK))) & same
        live = (lane < first) | ((lane >= BLOCK) & (lane < second + BLOCK))
        here = slot // 2 == number
        grad = jnp.where(lent_lanes & here, lent, grad_ref[:, columns].astype(F32))
        grad = jnp.where(live, grad, 0.0).astype(BF16)
        live = live[:HD]
        for head in range(2):
            base = head * 3 * HD
            q = qkv[base : base + HD, columns]
            k = qkv[base + HD : base + 2 * HD, columns]
            v = qkv[base + 2 * HD : base + 3 * HD, columns]
            g = grad[head * HD : (head + 1) * HD]
            scores = jnp.where(keep, dot(k, q, TN) * scaling, -1e30)
            e = jnp.exp(scores - jnp.max(scores, axis=0, keepdims=True))
            p = e / jnp.sum(e, axis=0, keepdims=True)
            p_half = p.astype(BF16)
            ctx_ref[head * HD : (head + 1) * HD, columns] = jnp.where(live, dot(v, p_half, NN), 0.0).astype(BF16)
            dv = dot(g, p_half, NT)
            dp = dot(v, g, TN)
            ds = (p * (dp - jnp.sum(dp * p, axis=0, keepdims=True))).astype(BF16)
            dq = dot(k, ds, NN) * scaling
            dk = dot(q, ds, NT) * scaling
            dqkv_ref[base : base + HD, columns] = dq.astype(BF16)
            dqkv_ref[base + HD : base + 2 * HD, columns] = dk.astype(BF16)
            dqkv_ref[base + 2 * HD : base + 3 * HD, columns] = dv.astype(BF16)
    term_ref[...] = dot(turned_ref[...], dqkv_ref[...], NN).astype(BF16)


def block(rank, slots, dest, counts, weight, patches, grad, gathered):
    return pl.pallas_call(
        block_kernel,
        grid=(ROWS // STEP,),
        in_specs=[
            SMEM,
            SMEM,
            SMEM,
            SMEM,
            pl.BlockSpec((COLS, D), lambda i: (0, 0)),
            pl.BlockSpec((STEP, D), lambda i: (i, 0)),
            pl.BlockSpec((WIDTH, STEP), lambda i: (0, i)),
            pl.BlockSpec((GROUP * WIDTH, PAIR), lambda i: (0, 0)),
        ],
        out_specs=[
            pl.BlockSpec((WIDTH, STEP), lambda i: (0, i)),
            pl.BlockSpec((COLS, STEP), lambda i: (0, i)),
            pl.BlockSpec((D, STEP), lambda i: (0, i)),
        ],
        out_shape=[
            jax.ShapeDtypeStruct((WIDTH, ROWS), BF16),
            jax.ShapeDtypeStruct((COLS, ROWS), BF16),
            jax.ShapeDtypeStruct((D, ROWS), BF16),
        ],
        scratch_shapes=[pltpu.VMEM((D, COLS), BF16)],
        cost_estimate=pl.CostEstimate(flops=6_000_000_000, bytes_accessed=9_000_000, transcendentals=300_000),
        name="block",
    )(rank, slots, dest, counts, weight, patches, grad, gathered)


def other_kernel(rank_ref, slot_ref, order_ref, dqkv_ref, x_ref, ctx_ref, out_ref):
    sorted_grad = dot(order_ref[...], dqkv_ref[...], NN).astype(BF16)
    out_ref[0:256, :] = (dot(sorted_grad, x_ref[...], NN) * (1.0 / ROWS)).astype(BF16)
    slot = slot_ref[rank_ref[0]]
    lent = shifted(ctx_ref[...], lax.rem(slot, 2) == 1).astype(BF16)
    for part in range(WIDTH // PACK):
        out_ref[256 : 256 + PACK, part * PAIR : (part + 1) * PAIR] = lent[part * PACK : (part + 1) * PACK]


def own_kernel(rank_ref, slot_ref, order_ref, dqkv_ref, x_ref, ctx_ref, other_ref, out_ref):
    sorted_grad = dot(order_ref[...], dqkv_ref[...], NN).astype(BF16)
    total = dot(sorted_grad, x_ref[...], NN) * (1.0 / ROWS) + other_ref[0:256, :].astype(F32)
    for x in range(N_X):
        out_ref[x, 0:64, :] = total[64 * x : 64 * (x + 1)].astype(BF16)
    slot = slot_ref[rank_ref[0]]
    lent = shifted(ctx_ref[...], lax.rem(slot, 2) == 1)
    lane = lax.broadcasted_iota(jnp.int32, (PACK, PAIR), 1)
    for part in range(WIDTH // PACK):
        columns = slice(part * PAIR, (part + 1) * PAIR)
        partner = pltpu.roll(other_ref[256 : 256 + PACK, columns].astype(F32), BLOCK, 1)
        both = jnp.where(lane < BLOCK, lent[part * PACK : (part + 1) * PACK], partner).astype(BF16)
        for x in range(N_X):
            out_ref[x, 64 : 64 + PACK, columns] = both


HALF_COST = pl.CostEstimate(flops=2 * 256 * ROWS * (D + COLS), bytes_accessed=6_000_000, transcendentals=0)


def half(kernel, flip, rank, slots, operands, shape, name):
    whole = lambda i, rank, slots: (0, 0)
    in_specs = [
        pl.BlockSpec((256, COLS), lambda i, rank, slots: ((1 - rank[0] % 2) if flip else rank[0] % 2, 0)),
        pl.BlockSpec((COLS, ROWS), whole),
        pl.BlockSpec((ROWS, D), whole),
        pl.BlockSpec((WIDTH, PAIR), lambda i, rank, slots: (0, slots[rank[0]] // 2)),
    ]
    if len(operands) == 5:
        in_specs.append(pl.BlockSpec((256 + PACK, D), whole))
    return pl.pallas_call(
        kernel,
        grid_spec=pltpu.PrefetchScalarGridSpec(
            num_scalar_prefetch=2,
            grid=(1,),
            in_specs=in_specs,
            out_specs=pl.BlockSpec(shape, lambda i, rank, slots: (0,) * len(shape)),
        ),
        out_shape=jax.ShapeDtypeStruct(shape, BF16),
        cost_estimate=HALF_COST,
        name=name,
    )(rank, slots, *operands)


def spread_kernel(rank_ref, slot_ref, dest_ref, in_ref, ctx_ref, out_ref, ctx_out_ref, held_ref):
    total = in_ref[0, 0:64, :].astype(F32)
    for x in range(1, N_X):
        total = total + in_ref[x, 0:64, :].astype(F32)
    held_ref[...] = total
    for z in range(N_Z):
        out_ref[z] = held_ref[5 * z : 5 * z + 8, :].astype(BF16)
    me = rank_ref[0]
    base = me // GROUP * GROUP
    source = base
    for k in range(1, GROUP):
        source = jnp.where(dest_ref[base + k] == me, base + k, source)
    slot = slot_ref[me]
    flip = (lax.rem(source, 2) != lax.rem(me, 2)) != (lax.rem(slot, 2) == 1)
    lane = lax.broadcasted_iota(jnp.int32, (PACK, PAIR), 1)
    mine = (lane >= BLOCK) == (lax.rem(slot, 2) == 1)
    x_source = lax.rem(source, 2 * N_X) // 2
    for part in range(WIDTH // PACK):
        rows = slice(part * PACK, (part + 1) * PACK)
        block_in = shifted(in_ref[x_source, 64 : 64 + PACK, part * PAIR : (part + 1) * PAIR], flip)
        ctx_out_ref[rows, :] = jnp.where(mine, block_in, ctx_ref[rows, :].astype(F32)).astype(BF16)


def spread(rank, slots, dest, received, ctx):
    tile = lambda i, rank, slots, dest: (0, slots[rank[0]] // 2)
    return pl.pallas_call(
        spread_kernel,
        grid_spec=pltpu.PrefetchScalarGridSpec(
            num_scalar_prefetch=3,
            grid=(1,),
            in_specs=[
                pl.BlockSpec((N_X, 64 + PACK, D), lambda i, rank, slots, dest: (0, 0, 0)),
                pl.BlockSpec((WIDTH, PAIR), tile),
            ],
            out_specs=[
                pl.BlockSpec((N_Z, 8, D), lambda i, rank, slots, dest: (0, 0, 0)),
                pl.BlockSpec((WIDTH, PAIR), tile),
            ],
            scratch_shapes=[pltpu.VMEM((64, D), F32)],
        ),
        out_shape=[jax.ShapeDtypeStruct((N_Z, 8, D), BF16), jax.ShapeDtypeStruct((WIDTH, ROWS), BF16)],
        input_output_aliases={4: 1},
        name="spread",
    )(rank, slots, dest, received, ctx)


def last_kernel(in_ref, out_ref):
    total = in_ref[0].astype(F32)
    for z in range(1, N_Z):
        total = total + in_ref[z].astype(F32)
    out_ref[...] = total[0:5]


def last_sum(received):
    return pl.pallas_call(
        last_kernel,
        in_specs=[VMEM],
        out_specs=VMEM,
        out_shape=jax.ShapeDtypeStruct((5, D), F32),
        name="last_sum",
    )(received)


def shards(patches, qkv_weight, patch_counts, lend_dest, lend_slot, attn_grad):
    rank = lax.axis_index("dp").astype(jnp.int32).reshape(1)
    grad = attn_grad.T
    weight = qkv_weight.T
    groups = [[base + k for k in range(GROUP)] for base in range(0, N_DP, GROUP)]
    x_groups = [[z * 8 + x * 2 + core for x in range(N_X)] for z in range(N_Z) for core in range(2)]
    z_groups = [[z * 8 + place for z in range(N_Z)] for place in range(8)]
    gathered = lax.all_gather(pick(rank, lend_slot, grad), "dp", axis=0, tiled=True, axis_index_groups=groups)
    ctx, dqkv, terms = block(rank, lend_slot, lend_dest, patch_counts, weight, patches, grad, gathered)
    summed = lax.psum_scatter(terms, "tensor", scatter_dimension=0, tiled=True)
    order = jnp.asarray(owner_order())
    operands = (order, dqkv, patches, ctx)
    sent = half(other_kernel, True, rank, lend_slot, operands, (256 + PACK, D), "other_half")
    received = lax.ppermute(sent, "dp", [(p, p ^ 1) for p in range(N_DP)])
    parts = half(own_kernel, False, rank, lend_slot, operands + (received,), (N_X, 64 + PACK, D), "own_half")
    parts = lax.all_to_all(parts, "dp", 0, 0, axis_index_groups=x_groups)
    parts, ctx = spread(rank, lend_slot, lend_dest, parts, ctx)
    parts = lax.all_to_all(parts, "dp", 0, 0, axis_index_groups=z_groups)
    return (ctx.T, summed.T, last_sum(parts))


def solution(mesh):
    return jax.shard_map(
        shards,
        mesh=mesh,
        in_specs=(P("dp", None), P(None, "tensor"), P(), P(), P(), P("dp", "tensor")),
        out_specs=(P("dp", "tensor"), P("dp", "tensor"), P(("tensor", "dp"), None)),
        check_vma=False,
    )
```

time: 417 us -> 108 us (0.26)
  the two profiles are of different devices: /device:TPU:6 before, /device:TPU:40 now
where the time goes in v2:
time: 108 us; the launch traced here: 107 us
  blocking collectives  55.3 us (51%)
  Pallas kernels  32.5 us (30%)
  between operations  14 us (13%)
  starting transfers between devices  2.3 us (2%)
  waiting for transfers between devices  2 us (2%)
    all_to_all x1, blocking collectives, shards(): parts = lax.all_to_all(parts, 'dp', 0, 0, axis_index_groups=z_groups)  30.5 us
    all_to_all x1, blocking collectives, shards(): parts = lax.all_to_all(parts, 'dp', 0, 0, axis_index_groups=x_groups)  17.7 us
    pallas_call x1, Pallas kernels, block(): pl.pallas_call(block_kernel, grid=(ROWS // STEP,), in_specs=[SMEM, SMEM,...  16.2 us
    pallas_call x2, Pallas kernels, half(): pl.pallas_call(kernel, grid_spec=pltpu.PrefetchScalarGridSpec(num_scalar_...  9.98 us
    all_gather x1, blocking collectives, shards(): lax.all_gather(pick(rank, lend_slot, grad), 'dp', axis=0, tiled=True, axi...  7.03 us
    pallas_call x1, Pallas kernels, spread(): pl.pallas_call(spread_kernel, grid_spec=pltpu.PrefetchScalarGridSpec(num_...  2.7 us
    ppermute x1, starting transfers between devices, shards(): received = lax.ppermute(sent, 'dp', [(p, p ^ 1) for p in range(N_DP)])  2.26 us
  transfers between devices with their start and end apart: 2, of which 1 were waited for; matrix products, arithmetic and copies ran while one was open for 0% of the time, Pallas kernels for 13%

profile of v2, /device:TPU:40, one launch (start us, length us, event | category | flops | bytes accessed | tf_op | source)
XLA Modules:
  0.0 107.0 jit_solution(14380638830623826642)
XLA Ops:
  7.2 0.0 reduce-scatter.2.cloned.1.call-start
  7.2 2.1 %pick.1 = bf16[160,128]{1,0:T(8,128)(2,1)} custom-call(s32[1]{0:T(128)} %bitcast.rank_ref, s32[96]{0:T(128)} %slot_ref.9, bf16[160,1024]{1,0:T(8,128)(2,1)} %bitcast.6), custom_call_target="tpu_custom_call" | custom-call | tf_op jit(solution)/shard_map/pick/pallas_call | solution.py:51
  9.3 7.0 %all_gather.3.gathered_ref = bf16[640,128]{1,0:T(8,128)(2,1)} all-gather(bf16[160,128]{1,0:T(8,128)(2,1)} %pick.1), channel_id=1, replica_groups={{0,8,16,24},{32,40,48,56},{64,72,80,88},{96,104,112,120},{128,136,144,1..., dimensions={0}, use_global_device_ids=true | all-gather | bytes 204800 | tf_op jit(solution)/shard_map/all_gather | solution.py:275
  16.3 16.2 %block.1 = (bf16[160,1024]{1,0:T(8,128)(2,1)}, bf16[480,1024]{1,0:T(8,128)(2,1)}, bf16[1280,1024]{1,0:T(8,128)(2,1)}) custom-call(s32[1]{0:T(128)} %bitcast.rank_ref, s32[96]{0:T(128)} %slot_ref.9, s32[96]{0:T(128)} %dest_ref.3, s32[1536]{0:T(1024)} %counts_ref.1, bf16[480,1280]{1,0:T(8,128)(2,1)} %bitcast.8, bf16[1024,1280]{1,0:T(8,128)(2,1)} %x_ref.5, ...), custom_call_target="tpu_custom_call" | custom-call | flops 6000000000 | bytes 9000000 | tf_op jit(solution)/shard_map/block/pallas_call | solution.py:124
  32.5 0.0 reduce-scatter.2.cloned.1.call-update
  32.5 4.9 %other_half.1 = bf16[272,1280]{1,0:T(8,128)(2,1)} custom-call(s32[1]{0:T(128)} %bitcast.rank_ref, s32[96]{0:T(128)} %slot_ref.9, bf16[512,480]{1,0:T(8,128)(2,1)} %constant.7.clone.order_ref, bf16[480,1024]{1,0:T(8,128)(2,1)} %get-tuple-element.8.dqkv_ref, bf16[1024,1280]{1,0:T(8,128)(2,1)} %x_ref.5, bf16[160,1024]{1,0:T(8,128)(2,1)} %get-tuple-element.9.ctx_ref), custom_call_target="tpu_custom_call" | custom-call | flops 922746880 | bytes 6000000 | tf_op jit(solution)/shard_map/other_half/pallas_call | solution.py:191
  37.4 2.3 %collective-permute-start = (bf16[272,1280]{1,0:T(8,128)(2,1)}, bf16[272,1280]{1,0:T(8,128)(2,1)S(1)}, u32[]{:S(2)}, u32[]{:S(2)}) collective-permute-start(bf16[272,1280]{1,0:T(8,128)(2,1)} %other_half.1), channel_id=1, source_target_pairs={{0,8},{8,0},{16,24},{24,16},{32,40},{40,32},{48,56},{56,48},{64,72... | collective-permute-start | bytes 2088968 | tf_op jit(solution)/shard_map/ppermute | solution.py:281
  39.7 2.0 %collective-permute-done.other_ref = bf16[272,1280]{1,0:T(8,128)(2,1)S(1)} collective-permute-done((bf16[272,1280]{1,0:T(8,128)(2,1)}, bf16[272,1280]{1,0:T(8,128)(2,1)S(1)}, u32[]{:S(2)}, u32[]{:S(2)}) %collective-permute-start) | collective-permute-done | bytes 696352 | tf_op jit(solution)/shard_map/ppermute | solution.py:281
  41.7 0.0 copy-start
  41.7 0.9 copy-done
  42.5 5.1 %own_half.1 = bf16[4,80,1280]{2,1,0:T(8,128)(2,1)} custom-call(s32[1]{0:T(128)} %bitcast.rank_ref, s32[96]{0:T(128)} %slot_ref.9, bf16[512,480]{1,0:T(8,128)(2,1)} %constant.7.clone.order_ref, bf16[480,1024]{1,0:T(8,128)(2,1)} %get-tuple-element.8.dqkv_ref, bf16[1024,1280]{1,0:T(8,128)(2,1)} %x_ref.5, bf16[160,1024]{1,0:T(8,128)(2,1)} %get-tuple-element.9.ctx_ref, ...), custom_call_target="tpu_custom_call" | custom-call | flops 922746880 | bytes 6000000 | tf_op jit(solution)/shard_map/own_half/pallas_call | solution.py:191
  47.6 17.7 %all_to_all.10.in_ref = bf16[4,80,1280]{2,1,0:T(8,128)(2,1)} all-to-all(bf16[4,80,1280]{2,1,0:T(8,128)(2,1)} %own_half.1), channel_id=1, replica_groups={{0,16,32,48},{8,24,40,56},{64,80,96,112},{72,88,104,120},{128,144,160,1..., dimensions={0} | all-to-all | bytes 1638400 | tf_op jit(solution)/shard_map/all_to_all | solution.py:283
  65.3 2.7 %spread.1 = (bf16[12,8,1280]{2,1,0:T(8,128)(2,1)}, bf16[160,1024]{1,0:T(8,128)(2,1)}) custom-call(s32[1]{0:T(128)} %bitcast.rank_ref, s32[96]{0:T(128)} %slot_ref.9, s32[96]{0:T(128)} %dest_ref.3, bf16[4,80,1280]{2,1,0:T(8,128)(2,1)} %all_to_all.10.in_ref, bf16[160,1024]{1,0:T(8,128)(2,1)} %get-tuple-element.9.ctx_ref), custom_call_target="tpu_custom_call", output_to_operand_aliasing={{1}: (4, {})} | custom-call | tf_op jit(solution)/shard_map/spread/pallas_call | solution.py:230
  68.0 30.5 %all_to_all.11.in_ref = bf16[12,8,1280]{2,1,0:T(8,128)(2,1)} all-to-all(bf16[12,8,1280]{2,1,0:T(8,128)(2,1)} %get-tuple-element.12), channel_id=1, replica_groups={{0,64,128,192,256,320,384,448,512,576,640,704},{8,72,136,200,264,328,39..., dimensions={0} | all-to-all | bytes 491520 | tf_op jit(solution)/shard_map/all_to_all | solution.py:285
  98.6 1.6 %last_sum.1 = f32[5,1280]{1,0:T(8,128)} custom-call(bf16[12,8,1280]{2,1,0:T(8,128)(2,1)} %all_to_all.11.in_ref), custom_call_target="tpu_custom_call" | custom-call | tf_op jit(solution)/shard_map/last_sum/pallas_call | solution.py:259
  100.2 0.0 reduce-scatter.2.cloned.1.call-done
Async XLA Ops:
  7.2 93.0 %reduce-scatter.2.cloned.1.call-start = ((), (), s32[]{:S(2)}) async-start(), calls=%async_computation.3 | async-start | bytes 2949120 | tf_op jit(solution)/shard_map/reduce_scatter | solution.py:277
  37.4 4.2 %collective-permute-start = (bf16[272,1280]{1,0:T(8,128)(2,1)}, bf16[272,1280]{1,0:T(8,128)(2,1)S(1)}, u32[]{:S(2)}, u32[]{:S(2)}) collective-permute-start(bf16[272,1280]{1,0:T(8,128)(2,1)} %other_half.1), channel_id=1, source_target_pairs={{0,8},{8,0},{16,24},{24,16},{32,40},{40,32},{48,56},{56,48},{64,72... | collective-permute-start | bytes 2088968 | tf_op jit(solution)/shard_map/ppermute | solution.py:281
  41.7 0.9 copy-start
Sparse Core Ops, SparseCore 0:
  32.6 53.6 reduce-scatter.1

commit v3 on v2

v3 whole, which is shorter than its diff:
```python
import jax
import jax.numpy as jnp
import numpy as np
from jax import lax
from jax.experimental import pallas as pl
from jax.experimental.pallas import tpu as pltpu
from jax.sharding import PartitionSpec as P

N_DP = 96
IMG_DEV = 16
BLOCK = 64
GROUP = 4
HD = 80
D = 1280
ROWS = 1024
COLS = 480
WIDTH = 2 * HD
PAIR = 2 * BLOCK
STEP = 4 * PAIR
N_X = 4
N_Z = 12
PACK = 16
WIDE = 7 * PAIR
BF16 = jnp.bfloat16
F32 = jnp.float32

NT = (((1,), (1,)), ((), ()))
NN = (((1,), (0,)), ((), ()))
TN = (((0,), (0,)), ((), ()))

VMEM = pl.BlockSpec(memory_space=pltpu.VMEM)
SMEM = pl.BlockSpec(memory_space=pltpu.SMEM)
SMALL = pltpu.CompilerParams(vmem_limit_bytes=16 * 2**20)


def owner_order():
    order = np.zeros((512, COLS), np.float32)
    for c in range(COLS):
        z, x, core, i = c // 40, c % 40 // 10, c % 10 // 5, c % 5
        order[core * 256 + x * 64 + z * 5 + i, c] = 1
    return order.astype(jnp.bfloat16)


def dot(a, b, dims):
    return lax.dot_general(a, b, dims, preferred_element_type=F32)


def pick_kernel(rank_ref, slot_ref, in_ref, out_ref):
    out_ref[...] = in_ref[...]


def pick(rank, slots, grad):
    return pl.pallas_call(
        pick_kernel,
        grid_spec=pltpu.PrefetchScalarGridSpec(
            num_scalar_prefetch=2,
            grid=(1,),
            in_specs=[pl.BlockSpec((WIDTH, PAIR), lambda i, rank, slots: (0, slots[rank[0]] // 2))],
            out_specs=pl.BlockSpec((WIDTH, PAIR), lambda i, rank, slots: (0, 0)),
        ),
        out_shape=jax.ShapeDtypeStruct((WIDTH, PAIR), BF16),
        name="pick",
    )(rank, slots, grad)


def shifted(tile, flip):
    wide = tile.astype(F32)
    return jnp.where(flip, pltpu.roll(wide, BLOCK, 1), wide)


def block_kernel(rank_ref, slot_ref, dest_ref, counts_ref, w_ref, x_ref, grad_ref, gathered_ref, order_ref, ctx_ref, term_ref, own_ref, send_ref, dqkv_ref, turned_ref, sum_ref):
    step = pl.program_id(0)
    scaling = HD ** (-0.5)

    @pl.when(step == 0)
    def _():
        for start in range(0, D, 256):
            turned_ref[start : start + 256, :] = w_ref[:, start : start + 256].astype(F32).T.astype(BF16)

    me = rank_ref[0]
    slot = slot_ref[me]
    host = dest_ref[me]
    lane = lax.broadcasted_iota(jnp.int32, (WIDTH, PAIR), 1)
    tile = gathered_ref[pl.ds(pl.multiple_of(lax.rem(host, GROUP) * WIDTH, 16), WIDTH), :]
    lent = shifted(tile, lax.rem(slot_ref[host], 2) != lax.rem(slot, 2))
    lent_lanes = (lane >= BLOCK) == (lax.rem(slot, 2) == 1)

    qkv = dot(w_ref[...], x_ref[...], NT).astype(BF16)
    key = lax.broadcasted_iota(jnp.int32, (PAIR, PAIR), 0)
    query = lax.broadcasted_iota(jnp.int32, (PAIR, PAIR), 1)
    same = (key < BLOCK) == (query < BLOCK)
    keeps, lives, grads = [], [], []
    for pair in range(STEP // PAIR):
        columns = slice(pair * PAIR, (pair + 1) * PAIR)
        number = step * (STEP // PAIR) + pair
        first = counts_ref[me * IMG_DEV + 2 * number]
        second = counts_ref[me * IMG_DEV + 2 * number + 1]
        keeps.append(((key < first) | ((key >= BLOCK) & (key < second + BLOCK))) & same)
        live = (lane < first) | ((lane >= BLOCK) & (lane < second + BLOCK))
        here = slot // 2 == number
        grad = jnp.where(lent_lanes & here, lent, grad_ref[:, columns].astype(F32))
        grads.append(jnp.where(live, grad, 0.0).astype(BF16))
        lives.append(live[:HD])
    chains = [(pair, head) for pair in range(STEP // PAIR) for head in range(2)]

    def part(pair, head, which):
        base = head * 3 * HD + which * HD
        return qkv[base : base + HD, pair * PAIR : (pair + 1) * PAIR]

    q = [part(*c, 0) for c in chains]
    k = [part(*c, 1) for c in chains]
    v = [part(*c, 2) for c in chains]
    g = [grads[pair][head * HD : (head + 1) * HD] for pair, head in chains]
    many = range(len(chains))
    scores = [dot(k[c], q[c], TN) for c in many]
    dp = [dot(v[c], g[c], TN) for c in many]
    scores = [jnp.where(keeps[chains[c][0]], scores[c] * scaling, -1e30) for c in many]
    e = [jnp.exp(s - jnp.max(s, axis=0, keepdims=True)) for s in scores]
    p = [x / jnp.sum(x, axis=0, keepdims=True) for x in e]
    p_half = [x.astype(BF16) for x in p]
    ds = [(p[c] * (dp[c] - jnp.sum(dp[c] * p[c], axis=0, keepdims=True))).astype(BF16) for c in many]
    ctx = [dot(v[c], p_half[c], NN) for c in many]
    dv = [dot(g[c], p_half[c], NT) for c in many]
    dq = [dot(k[c], ds[c], NN) * scaling for c in many]
    dk = [dot(q[c], ds[c], NT) * scaling for c in many]
    for c, (pair, head) in enumerate(chains):
        columns = slice(pair * PAIR, (pair + 1) * PAIR)
        base = head * 3 * HD
        ctx_ref[head * HD : (head + 1) * HD, columns] = jnp.where(lives[pair], ctx[c], 0.0).astype(BF16)
        dqkv_ref[base : base + HD, columns] = dq[c].astype(BF16)
        dqkv_ref[base + HD : base + 2 * HD, columns] = dk[c].astype(BF16)
        dqkv_ref[base + 2 * HD : base + 3 * HD, columns] = dv[c].astype(BF16)
    term_ref[...] = dot(turned_ref[...], dqkv_ref[...], NN).astype(BF16)
    sorted_grad = dot(order_ref[...], dqkv_ref[...], NN).astype(BF16)
    part_sum = dot(sorted_grad, x_ref[...], NN)

    @pl.when(slot // (2 * STEP // PAIR) == step)
    def _():
        start = pl.multiple_of(lax.rem(slot // 2, STEP // PAIR) * PAIR, PAIR)
        mine = shifted(ctx_ref[:, pl.ds(start, PAIR)], lax.rem(slot, 2) == 1).astype(BF16)
        for piece in range(WIDTH // PACK):
            send_ref[256 : 256 + PACK, piece * PAIR : (piece + 1) * PAIR] = mine[piece * PACK : (piece + 1) * PACK]

    @pl.when(step == 0)
    def _():
        sum_ref[...] = part_sum

    @pl.when(step == 1)
    def _():
        sum_ref[...] = (sum_ref[...] + part_sum) * (1.0 / ROWS)
        core = lax.rem(me, 2)
        own_ref[...] = sum_ref[pl.ds(pl.multiple_of(core * 256, 256), 256), :].astype(BF16)
        send_ref[0:256, :] = sum_ref[pl.ds(pl.multiple_of((1 - core) * 256, 256), 256), :].astype(BF16)


def block(rank, slots, dest, counts, weight, patches, grad, gathered, order):
    whole = lambda i: (0, 0)
    return pl.pallas_call(
        block_kernel,
        grid=(ROWS // STEP,),
        in_specs=[
            SMEM,
            SMEM,
            SMEM,
            SMEM,
            pl.BlockSpec((COLS, D), whole),
            pl.BlockSpec((STEP, D), lambda i: (i, 0)),
            pl.BlockSpec((WIDTH, STEP), lambda i: (0, i)),
            pl.BlockSpec((GROUP * WIDTH, PAIR), whole),
            pl.BlockSpec((512, COLS), whole),
        ],
        out_specs=[
            pl.BlockSpec((WIDTH, STEP), lambda i: (0, i)),
            pl.BlockSpec((D, STEP), lambda i: (0, i)),
            pl.BlockSpec((256, D), whole),
            pl.BlockSpec((256 + PACK, D), whole),
        ],
        out_shape=[
            jax.ShapeDtypeStruct((WIDTH, ROWS), BF16),
            jax.ShapeDtypeStruct((D, ROWS), BF16),
            jax.ShapeDtypeStruct((256, D), BF16),
            jax.ShapeDtypeStruct((256 + PACK, D), BF16),
        ],
        scratch_shapes=[pltpu.VMEM((COLS, STEP), BF16), pltpu.VMEM((D, COLS), BF16), pltpu.VMEM((512, D), F32)],
        cost_estimate=pl.CostEstimate(flops=8_000_000_000, bytes_accessed=9_000_000, transcendentals=300_000),
        compiler_params=pltpu.CompilerParams(vmem_limit_bytes=57 * 2**20),
        name="block",
    )(rank, slots, dest, counts, weight, patches, grad, gathered, order)


def own_kernel(own_ref, sent_ref, other_ref, out_ref):
    for x in range(N_X):
        rows = slice(64 * x, 64 * (x + 1))
        out_ref[x, 0:64, :] = (own_ref[rows, :].astype(F32) + other_ref[rows, :].astype(F32)).astype(BF16)
    lane = lax.broadcasted_iota(jnp.int32, (PACK, PAIR), 1)
    for piece in range(WIDTH // PACK):
        columns = slice(piece * PAIR, (piece + 1) * PAIR)
        partner = pltpu.roll(other_ref[256 : 256 + PACK, columns].astype(F32), BLOCK, 1)
        both = jnp.where(lane < BLOCK, sent_ref[256 : 256 + PACK, columns].astype(F32), partner).astype(BF16)
        for x in range(N_X):
            out_ref[x, 64 : 64 + PACK, columns] = both


def own_half(own, sent, other):
    return pl.pallas_call(
        own_kernel,
        in_specs=[VMEM] * 3,
        out_specs=VMEM,
        out_shape=jax.ShapeDtypeStruct((N_X, 64 + PACK, D), BF16),
        compiler_params=SMALL,
        name="own_half",
    )(own, sent, other)


def spread_kernel(rank_ref, slot_ref, dest_ref, in_ref, ctx_ref, out_ref, ctx_out_ref, held_ref):
    total = in_ref[0, 0:64, :].astype(F32)
    for x in range(1, N_X):
        total = total + in_ref[x, 0:64, :].astype(F32)
    held_ref[...] = total
    upper = lax.broadcasted_iota(jnp.int32, (8, PAIR), 0) < 5
    for z in range(N_Z):
        rows = held_ref[5 * z : 5 * z + 8, :]
        late = rows[:, WIDE:]
        low, high = pltpu.roll(late, 5, 0), pltpu.roll(late, 2, 0)
        for piece in range(WIDE // PAIR):
            front = rows[:, piece * PAIR : (piece + 1) * PAIR]
            if piece < 6:
                source_piece = (high if piece % 2 else low)[:, piece // 2 * PAIR : (piece // 2 + 1) * PAIR]
                front = jnp.where(upper, front, source_piece)
            out_ref[z, :, piece * PAIR : (piece + 1) * PAIR] = front.astype(BF16)
    me = rank_ref[0]
    base = me // GROUP * GROUP
    source = base
    for k in range(1, GROUP):
        source = jnp.where(dest_ref[base + k] == me, base + k, source)
    slot = slot_ref[me]
    flip = (lax.rem(source, 2) != lax.rem(me, 2)) != (lax.rem(slot, 2) == 1)
    lane = lax.broadcasted_iota(jnp.int32, (PACK, PAIR), 1)
    mine = (lane >= BLOCK) == (lax.rem(slot, 2) == 1)
    x_source = lax.rem(source, 2 * N_X) // 2
    for part in range(WIDTH // PACK):
        rows = slice(part * PACK, (part + 1) * PACK)
        block_in = shifted(in_ref[x_source, 64 : 64 + PACK, part * PAIR : (part + 1) * PAIR], flip)
        ctx_out_ref[rows, :] = jnp.where(mine, block_in, ctx_ref[rows, :].astype(F32)).astype(BF16)


def spread(rank, slots, dest, received, ctx):
    tile = lambda i, rank, slots, dest: (0, slots[rank[0]] // 2)
    return pl.pallas_call(
        spread_kernel,
        grid_spec=pltpu.PrefetchScalarGridSpec(
            num_scalar_prefetch=3,
            grid=(1,),
            in_specs=[
                pl.BlockSpec((N_X, 64 + PACK, D), lambda i, rank, slots, dest: (0, 0, 0)),
                pl.BlockSpec((WIDTH, PAIR), tile),
            ],
            out_specs=[
                pl.BlockSpec((N_Z, 8, WIDE), lambda i, rank, slots, dest: (0, 0, 0)),
                pl.BlockSpec((WIDTH, PAIR), tile),
            ],
            scratch_shapes=[pltpu.VMEM((64, D), F32)],
        ),
        out_shape=[jax.ShapeDtypeStruct((N_Z, 8, WIDE), BF16), jax.ShapeDtypeStruct((WIDTH, ROWS), BF16)],
        input_output_aliases={4: 1},
        compiler_params=SMALL,
        name="spread",
    )(rank, slots, dest, received, ctx)


def last_kernel(in_ref, out_ref):
    total = in_ref[0].astype(F32)
    for z in range(1, N_Z):
        total = total + in_ref[z].astype(F32)
    out_ref[:, 0:WIDE] = total[0:5]
    upper = lax.broadcasted_iota(jnp.int32, (8, PAIR), 0) < 3
    for piece in range(3):
        low = pltpu.roll(total[:, 2 * piece * PAIR : (2 * piece + 1) * PAIR], 3, 0)
        high = pltpu.roll(total[:, (2 * piece + 1) * PAIR : (2 * piece + 2) * PAIR], 6, 0)
        out_ref[:, WIDE + piece * PAIR : WIDE + (piece + 1) * PAIR] = jnp.where(upper, low, high)[0:5]


def last_sum(received):
    return pl.pallas_call(
        last_kernel,
        in_specs=[VMEM],
        out_specs=VMEM,
        out_shape=jax.ShapeDtypeStruct((5, D), F32),
        compiler_params=SMALL,
        name="last_sum",
    )(received)


def shards(patches, qkv_weight, patch_counts, lend_dest, lend_slot, attn_grad):
    rank = lax.axis_index("dp").astype(jnp.int32).reshape(1)
    grad = attn_grad.T
    weight = qkv_weight.T
    groups = [[base + k for k in range(GROUP)] for base in range(0, N_DP, GROUP)]
    x_groups = [[z * 8 + x * 2 + core for x in range(N_X)] for z in range(N_Z) for core in range(2)]
    z_groups = [[z * 8 + place for z in range(N_Z)] for place in range(8)]
    gathered = lax.all_gather(pick(rank, lend_slot, grad), "dp", axis=0, tiled=True, axis_index_groups=groups)
    order = jnp.asarray(owner_order())
    ctx, terms, own, sent = block(rank, lend_slot, lend_dest, patch_counts, weight, patches, grad, gathered, order)
    summed = lax.psum_scatter(terms, "tensor", scatter_dimension=0, tiled=True)
    received = lax.ppermute(sent, "dp", [(p, p ^ 1) for p in range(N_DP)])
    parts = own_half(own, sent, received)
    parts = lax.all_to_all(parts, "dp", 0, 0, axis_index_groups=x_groups)
    parts, ctx = spread(rank, lend_slot, lend_dest, parts, ctx)
    parts = lax.all_to_all(parts, "dp", 0, 0, axis_index_groups=z_groups)
    return (ctx.T, summed.T, last_sum(parts))


def solution(mesh):
    return jax.shard_map(
        shards,
        mesh=mesh,
        in_specs=(P("dp", None), P(None, "tensor"), P(), P(), P(), P("dp", "tensor")),
        out_specs=(P("dp", "tensor"), P("dp", "tensor"), P(("tensor", "dp"), None)),
        check_vma=False,
    )
```

time: 108 us -> 91.3 us (0.85)
  the two profiles are of different devices: /device:TPU:40 before, /device:TPU:6 now
where the time goes in v3:
time: 91.3 us; the launch traced here: 90.9 us
  blocking collectives  50 us (55%)
  Pallas kernels  17.1 us (19%)
  between operations  14.1 us (15%)
  waiting for transfers between devices  6.37 us (7%)
  starting transfers between devices  2.29 us (3%)
  local copies, waits for them, and re-layouts  1.05 us (1%)
    all_to_all x1, blocking collectives, shards(): parts = lax.all_to_all(parts, 'dp', 0, 0, axis_index_groups=x_groups)  23.1 us
    all_to_all x1, blocking collectives, shards(): parts = lax.all_to_all(parts, 'dp', 0, 0, axis_index_groups=z_groups)  20.6 us
    pallas_call x1, Pallas kernels, block(): pl.pallas_call(block_kernel, grid=(ROWS // STEP,), in_specs=[SMEM, SMEM,...  12 us
    all_gather x1, blocking collectives, shards(): lax.all_gather(pick(rank, lend_slot, grad), 'dp', axis=0, tiled=True, axi...  6.34 us
    reduce_scatter x1, waiting for transfers between devices, shards(): summed = lax.psum_scatter(terms, 'tensor', scatter_dimension=0, tiled=True)  4.57 us
    ppermute x1, starting transfers between devices, shards(): received = lax.ppermute(sent, 'dp', [(p, p ^ 1) for p in range(N_DP)])  2.25 us
    pallas_call x1, Pallas kernels, spread(): pl.pallas_call(spread_kernel, grid_spec=pltpu.PrefetchScalarGridSpec(num_...  2.17 us
    pallas_call x1, Pallas kernels, pick(): pl.pallas_call(pick_kernel, grid_spec=pltpu.PrefetchScalarGridSpec(num_sc...  2.07 us
  transfers between devices with their start and end apart: 2, of which 2 were waited for; matrix products, arithmetic and copies ran while one was open for 0% of the time, Pallas kernels for 3%

profile of v3, /device:TPU:6, one launch (start us, length us, event | category | flops | bytes accessed | tf_op | source)
XLA Modules:
  0.0 90.9 jit_solution(2843835063180895926)
XLA Ops:
  7.2 0.0 reduce-scatter.2.cloned.1.call-start
  7.2 2.1 %pick.1 = bf16[160,128]{1,0:T(8,128)(2,1)} custom-call(s32[1]{0:T(128)} %bitcast.rank_ref, s32[96]{0:T(128)} %slot_ref.5, bf16[160,1024]{1,0:T(8,128)(2,1)} %bitcast.6), custom_call_target="tpu_custom_call" | custom-call | tf_op jit(solution)/shard_map/pick/pallas_call | solution.py:53
  9.3 6.3 %all_gather.3.gathered_ref = bf16[640,128]{1,0:T(8,128)(2,1)} all-gather(bf16[160,128]{1,0:T(8,128)(2,1)} %pick.1), channel_id=1, replica_groups={{0,8,16,24},{32,40,48,56},{64,72,80,88},{96,104,112,120},{128,136,144,1..., dimensions={0}, use_global_device_ids=true | all-gather | bytes 204800 | tf_op jit(solution)/shard_map/all_gather | solution.py:301
  15.6 12.0 %block.1 = (bf16[160,1024]{1,0:T(8,128)(2,1)}, bf16[1280,1024]{1,0:T(8,128)(2,1)}, bf16[256,1280]{1,0:T(8,128)(2,1)}, bf16[272,1280]{1,0:T(8,128)(2,1)}) custom-call(s32[1]{0:T(128)} %bitcast.rank_ref, s32[96]{0:T(128)} %slot_ref.5, s32[96]{0:T(128)} %dest_ref.3, s32[1536]{0:T(1024)} %counts_ref.1, bf16[480,1280]{1,0:T(8,128)(2,1)} %bitcast.8, ...), custom_call_target="tpu_custom_call" | custom-call | flops 8000000000 | bytes 9000000 | tf_op jit(solution)/shard_map/block/pallas_call | solution.py:158
  27.6 0.0 copy-start
  27.6 0.0 copy-start.1
  27.6 0.0 reduce-scatter.2.cloned.1.call-update
  27.7 0.0 copy-start.2
  27.7 0.0 copy-start.3
  27.7 1.0 %copy-done = bf16[272,1280]{1,0:T(8,128)(2,1)S(1)} copy-done((bf16[272,1280]{1,0:T(8,128)(2,1)S(1)}, bf16[272,1280]{1,0:T(8,128)(2,1)}, u32[]{:S(2)}) %copy-start) | copy-done | bytes 696344
  28.7 2.3 %collective-permute-start = (bf16[272,1280]{1,0:T(8,128)(2,1)S(1)}, bf16[272,1280]{1,0:T(8,128)(2,1)S(1)}, u32[]{:S(2)}, u32[]{:S(2)}) collective-permute-start(bf16[272,1280]{1,0:T(8,128)(2,1)S(1)} %copy-done), channel_id=1, source_target_pairs={{0,8},{8,0},{16,24},{24,16},{32,40},{40,32},{48,56},{56,48},{64,72... | collective-permute-start | bytes 2088968 | tf_op jit(solution)/shard_map/ppermute | solution.py:305
  31.0 1.8 %collective-permute-done.other_ref = bf16[272,1280]{1,0:T(8,128)(2,1)S(1)} collective-permute-done((bf16[272,1280]{1,0:T(8,128)(2,1)S(1)}, bf16[272,1280]{1,0:T(8,128)(2,1)S(1)}, u32[]{:S(2)}, u32[]{:S(2)}) %collective-permute-start) | collective-permute-done | bytes 696352 | tf_op jit(solution)/shard_map/ppermute | solution.py:305
  32.8 0.0 copy-done.1
  32.8 0.3 own_half.1
  33.0 23.1 %all_to_all.10.in_ref = bf16[4,80,1280]{2,1,0:T(8,128)(2,1)S(1)} all-to-all(bf16[4,80,1280]{2,1,0:T(8,128)(2,1)S(1)} %own_half.1), channel_id=1, replica_groups={{0,16,32,48},{8,24,40,56},{64,80,96,112},{72,88,104,120},{128,144,160,1..., dimensions={0} | all-to-all | bytes 1638400 | tf_op jit(solution)/shard_map/all_to_all | solution.py:307
  56.1 0.0 copy-done.2
  56.1 0.0 copy-done.3
  56.1 2.2 %spread.1 = (bf16[12,8,896]{2,1,0:T(8,128)(2,1)S(1)}, bf16[160,1024]{1,0:T(8,128)(2,1)}) custom-call(s32[1]{0:T(128)} %bitcast.rank_ref, s32[96]{0:T(128)S(1)} %copy-done.2, s32[96]{0:T(128)S(1)} %copy-done.3, bf16[4,80,1280]{2,1,0:T(8,128)(2,1)S(1)} %all_to_all.10.in_ref, bf16[160,1024]{1,0:T(8,128)(2,1)} %get-tuple-element.11.ctx_ref), custom_call_target="tpu_custom_call", output_to_operand_aliasing={{1}: (4, {})} | custom-call | tf_op jit(solution)/shard_map/spread/pallas_call | solution.py:249
  58.3 20.6 %all_to_all.11.in_ref = bf16[12,8,896]{2,1,0:T(8,128)(2,1)S(1)} all-to-all(bf16[12,8,896]{2,1,0:T(8,128)(2,1)S(1)} %get-tuple-element.14), channel_id=1, replica_groups={{0,64,128,192,256,320,384,448,512,576,640,704},{8,72,136,200,264,328,39..., dimensions={0} | all-to-all | bytes 344064 | tf_op jit(solution)/shard_map/all_to_all | solution.py:309
  78.8 0.6 last_sum.1
  79.5 4.6 %reduce-scatter.2.cloned.1.call-done = bf16[160,1024]{1,0:T(8,128)(2,1)} async-done(((bf16[1280,1024]{1,0:T(8,128)(2,1)}), bf16[160,1024]{1,0:T(8,128)(2,1)}) %reduce-scatter.2.cloned.1.call-update) | async-done | bytes 327696 | tf_op jit(solution)/shard_map/reduce_scatter | solution.py:304
Async XLA Ops:
  7.2 76.9 %reduce-scatter.2.cloned.1.call-start = ((), (), s32[]{:S(2)}) async-start(), calls=%async_computation.3 | async-start | bytes 2949120 | tf_op jit(solution)/shard_map/reduce_scatter | solution.py:304
  27.6 1.1 %copy-start = (bf16[272,1280]{1,0:T(8,128)(2,1)S(1)}, bf16[272,1280]{1,0:T(8,128)(2,1)}, u32[]{:S(2)}) copy-start(bf16[272,1280]{1,0:T(8,128)(2,1)} %get-tuple-element.10.sent_ref) | copy-start | bytes 2088964
  27.6 5.1 %copy-start.1 = (bf16[256,1280]{1,0:T(8,128)(2,1)S(1)}, bf16[256,1280]{1,0:T(8,128)(2,1)}, u32[]{:S(2)}) copy-start(bf16[256,1280]{1,0:T(8,128)(2,1)} %get-tuple-element.9.own_ref) | copy-start | bytes 1966084
  27.7 28.4 %copy-start.2 = (s32[96]{0:T(128)S(1)}, s32[96]{0:T(128)}, u32[]{:S(2)}) copy-start(s32[96]{0:T(128)} %slot_ref.5) | copy-start | bytes 1156
  27.7 28.4 %copy-start.3 = (s32[96]{0:T(128)S(1)}, s32[96]{0:T(128)}, u32[]{:S(2)}) copy-start(s32[96]{0:T(128)} %dest_ref.3) | copy-start | bytes 1156
  28.7 4.0 %collective-permute-start = (bf16[272,1280]{1,0:T(8,128)(2,1)S(1)}, bf16[272,1280]{1,0:T(8,128)(2,1)S(1)}, u32[]{:S(2)}, u32[]{:S(2)}) collective-permute-start(bf16[272,1280]{1,0:T(8,128)(2,1)S(1)} %copy-done), channel_id=1, source_target_pairs={{0,8},{8,0},{16,24},{24,16},{32,40},{40,32},{48,56},{56,48},{64,72... | collective-permute-start | bytes 2088968 | tf_op jit(solution)/shard_map/ppermute | solution.py:305
Sparse Core Ops, SparseCore 0:
  27.8 56.2 reduce-scatter.1

commit v4 on v3

--- a/solution.py
+++ b/solution.py
@@ -68,7 +68,7 @@
     return jnp.where(flip, pltpu.roll(wide, BLOCK, 1), wide)
 
 
-def block_kernel(rank_ref, slot_ref, dest_ref, counts_ref, w_ref, x_ref, grad_ref, gathered_ref, order_ref, ctx_ref, term_ref, own_ref, send_ref, dqkv_ref, turned_ref, sum_ref):
+def block_kernel(rank_ref, slot_ref, dest_ref, counts_ref, w_ref, x_ref, grad_ref, gathered_ref, ctx_ref, term_ref, dqkv_ref, pack_ref, turned_ref):
     step = pl.program_id(0)
     scaling = HD ** (-0.5)
 
@@ -131,29 +131,16 @@
         dqkv_ref[base + HD : base + 2 * HD, columns] = dk[c].astype(BF16)
         dqkv_ref[base + 2 * HD : base + 3 * HD, columns] = dv[c].astype(BF16)
     term_ref[...] = dot(turned_ref[...], dqkv_ref[...], NN).astype(BF16)
-    sorted_grad = dot(order_ref[...], dqkv_ref[...], NN).astype(BF16)
-    part_sum = dot(sorted_grad, x_ref[...], NN)
 
     @pl.when(slot // (2 * STEP // PAIR) == step)
     def _():
         start = pl.multiple_of(lax.rem(slot // 2, STEP // PAIR) * PAIR, PAIR)
         mine = shifted(ctx_ref[:, pl.ds(start, PAIR)], lax.rem(slot, 2) == 1).astype(BF16)
         for piece in range(WIDTH // PACK):
-            send_ref[256 : 256 + PACK, piece * PAIR : (piece + 1) * PAIR] = mine[piece * PACK : (piece + 1) * PACK]
-
-    @pl.when(step == 0)
-    def _():
-        sum_ref[...] = part_sum
-
-    @pl.when(step == 1)
-    def _():
-        sum_ref[...] = (sum_ref[...] + part_sum) * (1.0 / ROWS)
-        core = lax.rem(me, 2)
-        own_ref[...] = sum_ref[pl.ds(pl.multiple_of(core * 256, 256), 256), :].astype(BF16)
-        send_ref[0:256, :] = sum_ref[pl.ds(pl.multiple_of((1 - core) * 256, 256), 256), :].astype(BF16)
-
-
-def block(rank, slots, dest, counts, weight, patches, grad, gathered, order):
+            pack_ref[:, piece * PAIR : (piece + 1) * PAIR] = mine[piece * PACK : (piece + 1) * PACK]
+
+
+def block(rank, slots, dest, counts, weight, patches, grad, gathered):
     whole = lambda i: (0, 0)
     return pl.pallas_call(
         block_kernel,
@@ -167,28 +154,48 @@
             pl.BlockSpec((STEP, D), lambda i: (i, 0)),
             pl.BlockSpec((WIDTH, STEP), lambda i: (0, i)),
             pl.BlockSpec((GROUP * WIDTH, PAIR), whole),
-            pl.BlockSpec((512, COLS), whole),
         ],
         out_specs=[
             pl.BlockSpec((WIDTH, STEP), lambda i: (0, i)),
             pl.BlockSpec((D, STEP), lambda i: (0, i)),
-            pl.BlockSpec((256, D), whole),
-            pl.BlockSpec((256 + PACK, D), whole),
+            pl.BlockSpec((COLS, STEP), lambda i: (0, i)),
+            pl.BlockSpec((PACK, D), whole),
         ],
         out_shape=[
             jax.ShapeDtypeStruct((WIDTH, ROWS), BF16),
             jax.ShapeDtypeStruct((D, ROWS), BF16),
-            jax.ShapeDtypeStruct((256, D), BF16),
-            jax.ShapeDtypeStruct((256 + PACK, D), BF16),
+            jax.ShapeDtypeStruct((COLS, ROWS), BF16),
+            jax.ShapeDtypeStruct((PACK, D), BF16),
         ],
-        scratch_shapes=[pltpu.VMEM((COLS, STEP), BF16), pltpu.VMEM((D, COLS), BF16), pltpu.VMEM((512, D), F32)],
-        cost_estimate=pl.CostEstimate(flops=8_000_000_000, bytes_accessed=9_000_000, transcendentals=300_000),
+        scratch_shapes=[pltpu.VMEM((D, COLS), BF16)],
+        cost_estimate=pl.CostEstimate(flops=6_000_000_000, bytes_accessed=9_000_000, transcendentals=300_000),
         compiler_params=pltpu.CompilerParams(vmem_limit_bytes=57 * 2**20),
         name="block",
-    )(rank, slots, dest, counts, weight, patches, grad, gathered, order)
-
-
-def own_kernel(own_ref, sent_ref, other_ref, out_ref):
+    )(rank, slots, dest, counts, weight, patches, grad, gathered)
+
+
+def sums_kernel(rank_ref, order_ref, dqkv_ref, x_ref, pack_ref, own_ref, send_ref):
+    core = lax.rem(rank_ref[0], 2)
+    for which, ref in ((1 - core, send_ref), (core, own_ref)):
+        order = order_ref[pl.ds(pl.multiple_of(which * 256, 256), 256), :]
+        sorted_grad = dot(order, dqkv_ref[...], NN).astype(BF16)
+        ref[0:256, :] = (dot(sorted_grad, x_ref[...], NN) * (1.0 / ROWS)).astype(BF16)
+    send_ref[256 : 256 + PACK, :] = pack_ref[...]
+
+
+def sums(rank, order, dqkv, patches, pack):
+    return pl.pallas_call(
+        sums_kernel,
+        in_specs=[SMEM] + [VMEM] * 4,
+        out_specs=[VMEM] * 2,
+        out_shape=[jax.ShapeDtypeStruct((256, D), BF16), jax.ShapeDtypeStruct((256 + PACK, D), BF16)],
+        cost_estimate=pl.CostEstimate(flops=2_000_000_000, bytes_accessed=6_000_000, transcendentals=0),
+        compiler_params=SMALL,
+        name="sums",
+    )(rank, order, dqkv, patches, pack)
+
+
+def own_kernel(own_ref, pack_ref, other_ref, out_ref):
     for x in range(N_X):
         rows = slice(64 * x, 64 * (x + 1))
         out_ref[x, 0:64, :] = (own_ref[rows, :].astype(F32) + other_ref[rows, :].astype(F32)).astype(BF16)
@@ -196,12 +203,12 @@
     for piece in range(WIDTH // PACK):
         columns = slice(piece * PAIR, (piece + 1) * PAIR)
         partner = pltpu.roll(other_ref[256 : 256 + PACK, columns].astype(F32), BLOCK, 1)
-        both = jnp.where(lane < BLOCK, sent_ref[256 : 256 + PACK, columns].astype(F32), partner).astype(BF16)
+        both = jnp.where(lane < BLOCK, pack_ref[:, columns].astype(F32), partner).astype(BF16)
         for x in range(N_X):
             out_ref[x, 64 : 64 + PACK, columns] = both
 
 
-def own_half(own, sent, other):
+def own_half(own, pack, other):
     return pl.pallas_call(
         own_kernel,
         in_specs=[VMEM] * 3,
@@ -209,7 +216,7 @@
         out_shape=jax.ShapeDtypeStruct((N_X, 64 + PACK, D), BF16),
         compiler_params=SMALL,
         name="own_half",
-    )(own, sent, other)
+    )(own, pack, other)
 
 
 def spread_kernel(rank_ref, slot_ref, dest_ref, in_ref, ctx_ref, out_ref, ctx_out_ref, held_ref):
@@ -299,11 +306,11 @@
     x_groups = [[z * 8 + x * 2 + core for x in range(N_X)] for z in range(N_Z) for core in range(2)]
     z_groups = [[z * 8 + place for z in range(N_Z)] for place in range(8)]
     gathered = lax.all_gather(pick(rank, lend_slot, grad), "dp", axis=0, tiled=True, axis_index_groups=groups)
-    order = jnp.asarray(owner_order())
-    ctx, terms, own, sent = block(rank, lend_slot, lend_dest, patch_counts, weight, patches, grad, gathered, order)
+    ctx, terms, dqkv, pack = block(rank, lend_slot, lend_dest, patch_counts, weight, patches, grad, gathered)
     summed = lax.psum_scatter(terms, "tensor", scatter_dimension=0, tiled=True)
+    own, sent = sums(rank, jnp.asarray(owner_order()), dqkv, patches, pack)
     received = lax.ppermute(sent, "dp", [(p, p ^ 1) for p in range(N_DP)])
-    parts = own_half(own, sent, received)
+    parts = own_half(own, pack, received)
     parts = lax.all_to_all(parts, "dp", 0, 0, axis_index_groups=x_groups)
     parts, ctx = spread(rank, lend_slot, lend_dest, parts, ctx)
     parts = lax.all_to_all(parts, "dp", 0, 0, axis_index_groups=z_groups)

time: 91.3 us -> 88.7 us (0.972)
  waiting for transfers between devices: 6.37 us -> 2.8 us
  local copies, waits for them, and re-layouts: 1.05 us -> 2.24 us
    reduce_scatter x1, waiting for transfers between devices: 4.57 us -> 1 us  [shards(): summed = lax.psum_scatter(terms, 'tensor', scatter_dimension=0, tiled=True)]
    pallas_call x1, Pallas kernels: 12 us -> 8.92 us  [block(): pl.pallas_call(block_kernel, grid=(ROWS // STEP,), in_specs=[SMEM, SMEM,...]
    pallas_call x0 -> x1, Pallas kernels: none -> 2.23 us  [sums(): pl.pallas_call(sums_kernel, in_specs=[SMEM] + [VMEM] * 4, out_specs=[VMEM...]
    unnamed x8 -> x12, local copies, waits for them, and re-layouts: 1.05 us -> 2.24 us
  transfers between devices with their start and end apart: 2 -> 2, of which waited for: 2 -> 2; matrix products, arithmetic and copies ran while one was open for 0% -> 0% of each run, Pallas kernels for 3% -> 6%
where the time goes in v4:
time: 88.7 us; the launch traced here: 87.7 us
  blocking collectives  49.9 us (56%)
  Pallas kernels  16.3 us (18%)
  between operations  14.1 us (16%)
  waiting for transfers between devices  2.8 us (3%)
  starting transfers between devices  2.3 us (3%)
  local copies, waits for them, and re-layouts  2.24 us (3%)
    all_to_all x1, blocking collectives, shards(): parts = lax.all_to_all(parts, 'dp', 0, 0, axis_index_groups=x_groups)  23.1 us
    all_to_all x1, blocking collectives, shards(): parts = lax.all_to_all(parts, 'dp', 0, 0, axis_index_groups=z_groups)  20.6 us
    pallas_call x1, Pallas kernels, block(): pl.pallas_call(block_kernel, grid=(ROWS // STEP,), in_specs=[SMEM, SMEM,...  8.92 us
    all_gather x1, blocking collectives, shards(): lax.all_gather(pick(rank, lend_slot, grad), 'dp', axis=0, tiled=True, axi...  6.34 us
    ppermute x1, starting transfers between devices, shards(): received = lax.ppermute(sent, 'dp', [(p, p ^ 1) for p in range(N_DP)])  2.26 us
    unnamed x12, local copies, waits for them, and re-layouts  2.24 us
    pallas_call x1, Pallas kernels, sums(): pl.pallas_call(sums_kernel, in_specs=[SMEM] + [VMEM] * 4, out_specs=[VMEM...  2.23 us
    pallas_call x1, Pallas kernels, spread(): pl.pallas_call(spread_kernel, grid_spec=pltpu.PrefetchScalarGridSpec(num_...  2.17 us
  transfers between devices with their start and end apart: 2, of which 2 were waited for; matrix products, arithmetic and copies ran while one was open for 0% of the time, Pallas kernels for 6%

profile of v4, /device:TPU:6, one launch (start us, length us, event | category | flops | bytes accessed | tf_op | source)
XLA Modules:
  0.0 87.7 jit_solution(9982752379479367319)
XLA Ops:
  7.2 0.0 reduce-scatter.2.cloned.1.call-start
  7.2 2.1 %pick.1 = bf16[160,128]{1,0:T(8,128)(2,1)} custom-call(s32[1]{0:T(128)} %bitcast.rank_ref, s32[96]{0:T(128)} %slot_ref.5, bf16[160,1024]{1,0:T(8,128)(2,1)} %bitcast.6), custom_call_target="tpu_custom_call" | custom-call | tf_op jit(solution)/shard_map/pick/pallas_call | solution.py:53
  9.3 6.3 %all_gather.3.gathered_ref = bf16[640,128]{1,0:T(8,128)(2,1)} all-gather(bf16[160,128]{1,0:T(8,128)(2,1)} %pick.1), channel_id=1, replica_groups={{0,8,16,24},{32,40,48,56},{64,72,80,88},{96,104,112,120},{128,136,144,1..., dimensions={0}, use_global_device_ids=true | all-gather | bytes 204800 | tf_op jit(solution)/shard_map/all_gather | solution.py:308
  15.6 0.0 copy-start.3
  15.6 8.9 %block.1 = (bf16[160,1024]{1,0:T(8,128)(2,1)}, bf16[1280,1024]{1,0:T(8,128)(2,1)}, bf16[480,1024]{1,0:T(8,128)(2,1)}, bf16[16,1280]{1,0:T(8,128)(2,1)}) custom-call(s32[1]{0:T(128)} %bitcast.rank_ref, s32[96]{0:T(128)} %slot_ref.5, s32[96]{0:T(128)} %dest_ref.3, s32[1536]{0:T(1024)} %counts_ref.1, bf16[480,1280]{1,0:T(8,128)(2,1)} %bitcast.8, ...), custom_call_target="tpu_custom_call" | custom-call | flops 6000000000 | bytes 9000000 | tf_op jit(solution)/shard_map/block/pallas_call | solution.py:145
  24.6 0.0 copy-start.4
  24.6 0.0 reduce-scatter.2.cloned.1.call-update
  24.6 0.0 copy-done.3
  24.6 0.7 copy-done
  25.3 0.3 copy-done.4
  25.6 1.2 %copy-done.5 = bf16[480,1024]{1,0:T(8,128)(2,1)S(1)} copy-done((bf16[480,1024]{1,0:T(8,128)(2,1)S(1)}, bf16[480,1024]{1,0:T(8,128)(2,1)}, u32[]{:S(2)}) %copy-start.5) | copy-done | bytes 983064
  26.8 2.2 %sums.1 = (bf16[256,1280]{1,0:T(8,128)(2,1)S(1)}, bf16[272,1280]{1,0:T(8,128)(2,1)S(1)}) custom-call(s32[1]{0:T(128)} %bitcast.rank_ref, bf16[512,480]{1,0:T(8,128)(2,1)S(1)} %copy-done.4, bf16[480,1024]{1,0:T(8,128)(2,1)S(1)} %copy-done.5, bf16[1024,1280]{1,0:T(8,128)(2,1)S(1)} %copy-done.3, bf16[16,1280]{1,0:T(8,128)(2,1)S(1)} %copy-done), custom_call_target="tpu_custom_call" | custom-call | flops 2000000000 | bytes 6000000 | tf_op jit(solution)/shard_map/sums/pallas_call | solution.py:187
  29.1 0.0 copy-start.1
  29.1 0.0 copy-start.2
  29.1 2.3 %collective-permute-start = (bf16[272,1280]{1,0:T(8,128)(2,1)S(1)}, bf16[272,1280]{1,0:T(8,128)(2,1)S(1)}, u32[]{:S(2)}, u32[]{:S(2)}) collective-permute-start(bf16[272,1280]{1,0:T(8,128)(2,1)S(1)} %get-tuple-element.14), channel_id=1, source_target_pairs={{0,8},{8,0},{16,24},{24,16},{32,40},{40,32},{48,56},{56,48},{64,72... | collective-permute-start | bytes 2088968 | tf_op jit(solution)/shard_map/ppermute | solution.py:312
  31.3 1.8 %collective-permute-done.other_ref = bf16[272,1280]{1,0:T(8,128)(2,1)S(1)} collective-permute-done((bf16[272,1280]{1,0:T(8,128)(2,1)S(1)}, bf16[272,1280]{1,0:T(8,128)(2,1)S(1)}, u32[]{:S(2)}, u32[]{:S(2)}) %collective-permute-start) | collective-permute-done | bytes 696352 | tf_op jit(solution)/shard_map/ppermute | solution.py:312
  33.1 0.3 own_half.1
  33.4 23.1 %all_to_all.10.in_ref = bf16[4,80,1280]{2,1,0:T(8,128)(2,1)S(1)} all-to-all(bf16[4,80,1280]{2,1,0:T(8,128)(2,1)S(1)} %own_half.1), channel_id=1, replica_groups={{0,16,32,48},{8,24,40,56},{64,80,96,112},{72,88,104,120},{128,144,160,1..., dimensions={0} | all-to-all | bytes 1638400 | tf_op jit(solution)/shard_map/all_to_all | solution.py:314
  56.4 0.0 copy-done.1
  56.5 0.0 copy-done.2
  56.5 2.2 %spread.1 = (bf16[12,8,896]{2,1,0:T(8,128)(2,1)S(1)}, bf16[160,1024]{1,0:T(8,128)(2,1)}) custom-call(s32[1]{0:T(128)} %bitcast.rank_ref, s32[96]{0:T(128)S(1)} %copy-done.1, s32[96]{0:T(128)S(1)} %copy-done.2, bf16[4,80,1280]{2,1,0:T(8,128)(2,1)S(1)} %all_to_all.10.in_ref, bf16[160,1024]{1,0:T(8,128)(2,1)} %get-tuple-element.15.ctx_ref), custom_call_target="tpu_custom_call", output_to_operand_aliasing={{1}: (4, {})} | custom-call | tf_op jit(solution)/shard_map/spread/pallas_call | solution.py:256
  58.6 20.6 %all_to_all.11.in_ref = bf16[12,8,896]{2,1,0:T(8,128)(2,1)S(1)} all-to-all(bf16[12,8,896]{2,1,0:T(8,128)(2,1)S(1)} %get-tuple-element.18), channel_id=1, replica_groups={{0,64,128,192,256,320,384,448,512,576,640,704},{8,72,136,200,264,328,39..., dimensions={0} | all-to-all | bytes 344064 | tf_op jit(solution)/shard_map/all_to_all | solution.py:316
  79.2 0.6 last_sum.1
  79.8 1.0 %reduce-scatter.2.cloned.1.call-done = bf16[160,1024]{1,0:T(8,128)(2,1)} async-done(((bf16[1280,1024]{1,0:T(8,128)(2,1)}), bf16[160,1024]{1,0:T(8,128)(2,1)}) %reduce-scatter.2.cloned.1.call-update) | async-done | bytes 327696 | tf_op jit(solution)/shard_map/reduce_scatter | solution.py:310
  (2 shorter events, 0.0 us)
Async XLA Ops:
  7.2 73.7 %reduce-scatter.2.cloned.1.call-start = ((), (), s32[]{:S(2)}) async-start(), calls=%async_computation.3 | async-start | bytes 2949120 | tf_op jit(solution)/shard_map/reduce_scatter | solution.py:310
  15.6 9.0 %copy-start.3 = (bf16[1024,1280]{1,0:T(8,128)(2,1)S(1)}, bf16[1024,1280]{1,0:T(8,128)(2,1)}, u32[]{:S(2)}) copy-start(bf16[1024,1280]{1,0:T(8,128)(2,1)} %x_ref.3) | copy-start | bytes 7864324
  24.6 0.8 copy-start
  24.6 1.1 %copy-start.4 = (bf16[512,480]{1,0:T(8,128)(2,1)S(1)}, bf16[512,480]{1,0:T(8,128)(2,1)}, u32[]{:S(2)}) copy-start(bf16[512,480]{1,0:T(8,128)(2,1)} %constant.7.clone.order_ref) | copy-start | bytes 1474564
  25.6 1.2 %copy-start.5 = (bf16[480,1024]{1,0:T(8,128)(2,1)S(1)}, bf16[480,1024]{1,0:T(8,128)(2,1)}, u32[]{:S(2)}) copy-start(bf16[480,1024]{1,0:T(8,128)(2,1)} %get-tuple-element.11.dqkv_ref) | copy-start | bytes 2949124
  29.1 27.4 %copy-start.1 = (s32[96]{0:T(128)S(1)}, s32[96]{0:T(128)}, u32[]{:S(2)}) copy-start(s32[96]{0:T(128)} %slot_ref.5) | copy-start | bytes 1156
  29.1 27.4 %copy-start.2 = (s32[96]{0:T(128)S(1)}, s32[96]{0:T(128)}, u32[]{:S(2)}) copy-start(s32[96]{0:T(128)} %dest_ref.3) | copy-start | bytes 1156
  29.1 4.1 %collective-permute-start = (bf16[272,1280]{1,0:T(8,128)(2,1)S(1)}, bf16[272,1280]{1,0:T(8,128)(2,1)S(1)}, u32[]{:S(2)}, u32[]{:S(2)}) collective-permute-start(bf16[272,1280]{1,0:T(8,128)(2,1)S(1)} %get-tuple-element.14), channel_id=1, source_target_pairs={{0,8},{8,0},{16,24},{24,16},{32,40},{40,32},{48,56},{56,48},{64,72... | collective-permute-start | bytes 2088968 | tf_op jit(solution)/shard_map/ppermute | solution.py:312
Sparse Core Ops, SparseCore 0:
  24.7 56.0 reduce-scatter.1

commit v5 on v4

--- a/solution.py
+++ b/solution.py
@@ -17,6 +17,7 @@
 WIDTH = 2 * HD
 PAIR = 2 * BLOCK
 STEP = 4 * PAIR
+CUT = 256
 N_X = 4
 N_Z = 12
 PACK = 16
@@ -30,6 +31,7 @@
 
 VMEM = pl.BlockSpec(memory_space=pltpu.VMEM)
 SMEM = pl.BlockSpec(memory_space=pltpu.SMEM)
+HBM = pl.BlockSpec(memory_space=pltpu.HBM)
 SMALL = pltpu.CompilerParams(vmem_limit_bytes=16 * 2**20)
 
 
@@ -46,7 +48,11 @@
 
 
 def pick_kernel(rank_ref, slot_ref, in_ref, out_ref):
-    out_ref[...] = in_ref[...]
+    upper = lax.rem(slot_ref[rank_ref[0]], 2) == 1
+    lane = lax.broadcasted_iota(jnp.int32, (HD, PAIR), 1)
+    left = shifted(in_ref[0:HD, :], upper)
+    right = shifted(in_ref[HD:WIDTH, :], jnp.logical_not(upper))
+    out_ref[...] = jnp.where(lane < BLOCK, left, right).astype(BF16)
 
 
 def pick(rank, slots, grad):
@@ -56,9 +62,11 @@
             num_scalar_prefetch=2,
             grid=(1,),
             in_specs=[pl.BlockSpec((WIDTH, PAIR), lambda i, rank, slots: (0, slots[rank[0]] // 2))],
-            out_specs=pl.BlockSpec((WIDTH, PAIR), lambda i, rank, slots: (0, 0)),
+            out_specs=pl.BlockSpec((HD, PAIR), lambda i, rank, slots: (0, 0)),
         ),
-        out_shape=jax.ShapeDtypeStruct((WIDTH, PAIR), BF16),
+        out_shape=jax.ShapeDtypeStruct((HD, PAIR), BF16),
+        cost_estimate=pl.CostEstimate(flops=20_000_000_000, bytes_accessed=40_000_000, transcendentals=0),
+        compiler_params=pltpu.CompilerParams(vmem_limit_bytes=60400 * 1024),
         name="pick",
     )(rank, slots, grad)
 
@@ -68,44 +76,30 @@
     return jnp.where(flip, pltpu.roll(wide, BLOCK, 1), wide)
 
 
-def block_kernel(rank_ref, slot_ref, dest_ref, counts_ref, w_ref, x_ref, grad_ref, gathered_ref, ctx_ref, term_ref, dqkv_ref, pack_ref, turned_ref):
-    step = pl.program_id(0)
+def attend(me, slot, group, lent, counts_ref, grad_buf, qkv_buf, ctx_buf, dqkv_buf):
     scaling = HD ** (-0.5)
-
-    @pl.when(step == 0)
-    def _():
-        for start in range(0, D, 256):
-            turned_ref[start : start + 256, :] = w_ref[:, start : start + 256].astype(F32).T.astype(BF16)
-
-    me = rank_ref[0]
-    slot = slot_ref[me]
-    host = dest_ref[me]
     lane = lax.broadcasted_iota(jnp.int32, (WIDTH, PAIR), 1)
-    tile = gathered_ref[pl.ds(pl.multiple_of(lax.rem(host, GROUP) * WIDTH, 16), WIDTH), :]
-    lent = shifted(tile, lax.rem(slot_ref[host], 2) != lax.rem(slot, 2))
     lent_lanes = (lane >= BLOCK) == (lax.rem(slot, 2) == 1)
-
-    qkv = dot(w_ref[...], x_ref[...], NT).astype(BF16)
     key = lax.broadcasted_iota(jnp.int32, (PAIR, PAIR), 0)
     query = lax.broadcasted_iota(jnp.int32, (PAIR, PAIR), 1)
     same = (key < BLOCK) == (query < BLOCK)
-    keeps, lives, grads = [], [], []
-    for pair in range(STEP // PAIR):
+    pairs = range(group * (STEP // PAIR), (group + 1) * (STEP // PAIR))
+    keeps, lives, grads = {}, {}, {}
+    for pair in pairs:
         columns = slice(pair * PAIR, (pair + 1) * PAIR)
-        number = step * (STEP // PAIR) + pair
-        first = counts_ref[me * IMG_DEV + 2 * number]
-        second = counts_ref[me * IMG_DEV + 2 * number + 1]
-        keeps.append(((key < first) | ((key >= BLOCK) & (key < second + BLOCK))) & same)
+        first = counts_ref[me * IMG_DEV + 2 * pair]
+        second = counts_ref[me * IMG_DEV + 2 * pair + 1]
+        keeps[pair] = ((key < first) | ((key >= BLOCK) & (key < second + BLOCK))) & same
         live = (lane < first) | ((lane >= BLOCK) & (lane < second + BLOCK))
-        here = slot // 2 == number
-        grad = jnp.where(lent_lanes & here, lent, grad_ref[:, columns].astype(F32))
-        grads.append(jnp.where(live, grad, 0.0).astype(BF16))
-        lives.append(live[:HD])
-    chains = [(pair, head) for pair in range(STEP // PAIR) for head in range(2)]
+        here = slot // 2 == pair
+        grad = jnp.where(lent_lanes & here, lent, grad_buf[:, columns].astype(F32))
+        grads[pair] = jnp.where(live, grad, 0.0).astype(BF16)
+        lives[pair] = live[:HD]
+    chains = [(pair, head) for pair in pairs for head in range(2)]
 
     def part(pair, head, which):
         base = head * 3 * HD + which * HD
-        return qkv[base : base + HD, pair * PAIR : (pair + 1) * PAIR]
+        return qkv_buf[base : base + HD, pair * PAIR : (pair + 1) * PAIR]
 
     q = [part(*c, 0) for c in chains]
     k = [part(*c, 1) for c in chains]
@@ -126,50 +120,73 @@
     for c, (pair, head) in enumerate(chains):
         columns = slice(pair * PAIR, (pair + 1) * PAIR)
         base = head * 3 * HD
-        ctx_ref[head * HD : (head + 1) * HD, columns] = jnp.where(lives[pair], ctx[c], 0.0).astype(BF16)
-        dqkv_ref[base : base + HD, columns] = dq[c].astype(BF16)
-        dqkv_ref[base + HD : base + 2 * HD, columns] = dk[c].astype(BF16)
-        dqkv_ref[base + 2 * HD : base + 3 * HD, columns] = dv[c].astype(BF16)
-    term_ref[...] = dot(turned_ref[...], dqkv_ref[...], NN).astype(BF16)
-
-    @pl.when(slot // (2 * STEP // PAIR) == step)
-    def _():
-        start = pl.multiple_of(lax.rem(slot // 2, STEP // PAIR) * PAIR, PAIR)
-        mine = shifted(ctx_ref[:, pl.ds(start, PAIR)], lax.rem(slot, 2) == 1).astype(BF16)
-        for piece in range(WIDTH // PACK):
-            pack_ref[:, piece * PAIR : (piece + 1) * PAIR] = mine[piece * PACK : (piece + 1) * PACK]
+        ctx_buf[head * HD : (head + 1) * HD, columns] = jnp.where(lives[pair], ctx[c], 0.0).astype(BF16)
+        dqkv_buf[base : base + HD, columns] = dq[c].astype(BF16)
+        dqkv_buf[base + HD : base + 2 * HD, columns] = dk[c].astype(BF16)
+        dqkv_buf[base + 2 * HD : base + 3 * HD, columns] = dv[c].astype(BF16)
+
+
+def block_kernel(
+    rank_ref, slot_ref, dest_ref, counts_ref, w_ref, x_ref, grad_ref, gathered_ref, ctx_ref, term_ref, dqkv_ref, pack_ref,
+    qkv_buf, turned_buf, ctx_buf, dqkv_buf, term_buf, out_sems,
+):
+    me = rank_ref[0]
+    slot = slot_ref[me]
+    host = dest_ref[me]
+    for start in range(0, D, 256):
+        turned_buf[start : start + 256, :] = w_ref[:, start : start + 256].astype(F32).T.astype(BF16)
+
+    def project(group):
+        rows = slice(group * STEP, (group + 1) * STEP)
+        qkv_buf[:, rows] = dot(w_ref[...], x_ref[rows, :], NT).astype(BF16)
+
+    tile = gathered_ref[pl.ds(pl.multiple_of(lax.rem(host, GROUP) * HD, 16), HD), :]
+    upper = lax.rem(slot, 2) == 1
+    lent = jnp.concatenate([shifted(tile, upper), shifted(tile, jnp.logical_not(upper))], axis=0)
+    for group in range(ROWS // STEP):
+        project(group)
+    for group in range(ROWS // STEP):
+        attend(me, slot, group, lent, counts_ref, grad_ref, qkv_buf, ctx_buf, dqkv_buf)
+    stores = [
+        pltpu.make_async_copy(ctx_buf, ctx_ref, out_sems.at[0]),
+        pltpu.make_async_copy(dqkv_buf, dqkv_ref, out_sems.at[1]),
+    ]
+    stores[0].start()
+    stores[1].start()
+    for piece in range(D // CUT):
+        rows = pl.ds(piece * CUT, CUT)
+        term_buf[rows, :] = dot(turned_buf[rows, :], dqkv_buf[...], NN).astype(BF16)
+        stores.append(pltpu.make_async_copy(term_buf.at[rows], term_ref.at[rows], out_sems.at[2 + piece]))
+        stores[-1].start()
+    mine = ctx_buf[:, pl.ds(pl.multiple_of(slot // 2 * PAIR, PAIR), PAIR)]
+    mine = shifted(mine, upper).astype(BF16)
+    for piece in range(WIDTH // PACK):
+        pack_ref[:, piece * PAIR : (piece + 1) * PAIR] = mine[piece * PACK : (piece + 1) * PACK]
+    for store in stores:
+        store.wait()
 
 
 def block(rank, slots, dest, counts, weight, patches, grad, gathered):
-    whole = lambda i: (0, 0)
     return pl.pallas_call(
         block_kernel,
-        grid=(ROWS // STEP,),
-        in_specs=[
-            SMEM,
-            SMEM,
-            SMEM,
-            SMEM,
-            pl.BlockSpec((COLS, D), whole),
-            pl.BlockSpec((STEP, D), lambda i: (i, 0)),
-            pl.BlockSpec((WIDTH, STEP), lambda i: (0, i)),
-            pl.BlockSpec((GROUP * WIDTH, PAIR), whole),
-        ],
-        out_specs=[
-            pl.BlockSpec((WIDTH, STEP), lambda i: (0, i)),
-            pl.BlockSpec((D, STEP), lambda i: (0, i)),
-            pl.BlockSpec((COLS, STEP), lambda i: (0, i)),
-            pl.BlockSpec((PACK, D), whole),
-        ],
+        in_specs=[SMEM] * 4 + [VMEM] * 4,
+        out_specs=[HBM] * 3 + [VMEM],
         out_shape=[
             jax.ShapeDtypeStruct((WIDTH, ROWS), BF16),
             jax.ShapeDtypeStruct((D, ROWS), BF16),
             jax.ShapeDtypeStruct((COLS, ROWS), BF16),
             jax.ShapeDtypeStruct((PACK, D), BF16),
         ],
-        scratch_shapes=[pltpu.VMEM((D, COLS), BF16)],
+        scratch_shapes=[
+            pltpu.VMEM((COLS, ROWS), BF16),
+            pltpu.VMEM((D, COLS), BF16),
+            pltpu.VMEM((WIDTH, ROWS), BF16),
+            pltpu.VMEM((COLS, ROWS), BF16),
+            pltpu.VMEM((D, ROWS), BF16),
+            pltpu.SemaphoreType.DMA((2 + D // CUT,)),
+        ],
         cost_estimate=pl.CostEstimate(flops=6_000_000_000, bytes_accessed=9_000_000, transcendentals=300_000),
-        compiler_params=pltpu.CompilerParams(vmem_limit_bytes=57 * 2**20),
+        compiler_params=pltpu.CompilerParams(vmem_limit_bytes=32 * 2**20),
         name="block",
     )(rank, slots, dest, counts, weight, patches, grad, gathered)
 

time: 88.7 us -> 86.8 us (0.979)
  Pallas kernels: 16.3 us -> 14.7 us
  blocking collectives: 49.9 us -> 48.7 us
  local copies, waits for them, and re-layouts: 2.24 us -> 3.19 us
    pallas_call x1, Pallas kernels: 8.92 us -> 6.72 us  [block(): pl.pallas_call(block_kernel, in_specs=[SMEM] * 4 + [VMEM] * 4, out_specs=...]
    unnamed x12 -> x18, local copies, waits for them, and re-layouts: 2.24 us -> 3.19 us
where the time goes in v5:
time: 86.8 us; the launch traced here: 86 us
  blocking collectives  48.7 us (56%)
  Pallas kernels  14.7 us (17%)
  between operations  14.2 us (16%)
  local copies, waits for them, and re-layouts  3.19 us (4%)
  waiting for transfers between devices  3 us (3%)
  starting transfers between devices  2.29 us (3%)
    all_to_all x1, blocking collectives, shards(): parts = lax.all_to_all(parts, 'dp', 0, 0, axis_index_groups=x_groups)  23.2 us
    all_to_all x1, blocking collectives, shards(): parts = lax.all_to_all(parts, 'dp', 0, 0, axis_index_groups=z_groups)  20 us
    pallas_call x1, Pallas kernels, block(): pl.pallas_call(block_kernel, in_specs=[SMEM] * 4 + [VMEM] * 4, out_specs=...  6.72 us
    all_gather x1, blocking collectives, shards(): lax.all_gather(pick(rank, lend_slot, grad), 'dp', axis=0, tiled=True, axi...  5.49 us
    unnamed x18, local copies, waits for them, and re-layouts  3.19 us
    pallas_call x1, Pallas kernels, pick(): pl.pallas_call(pick_kernel, grid_spec=pltpu.PrefetchScalarGridSpec(num_sc...  2.69 us
    ppermute x1, starting transfers between devices, shards(): received = lax.ppermute(sent, 'dp', [(p, p ^ 1) for p in range(N_DP)])  2.25 us
    pallas_call x1, Pallas kernels, sums(): pl.pallas_call(sums_kernel, in_specs=[SMEM] + [VMEM] * 4, out_specs=[VMEM...  2.21 us
  transfers between devices with their start and end apart: 2, of which 2 were waited for; matrix products, arithmetic and copies ran while one was open for 0% of the time, Pallas kernels for 6%

profile of v5, /device:TPU:6, one launch (start us, length us, event | category | flops | bytes accessed | tf_op | source)
XLA Modules:
  0.0 86.0 jit_solution(4394253998120282614)
XLA Ops:
  7.2 0.0 reduce-scatter.2.cloned.1.call-start
  7.2 0.0 copy-start
  7.2 0.0 copy-start.1
  7.2 0.0 copy-start.2
  7.2 0.0 copy-start.3
  7.3 0.0 copy-start.4
  7.3 0.0 copy-start.5
  7.3 2.7 %pick.1 = bf16[80,128]{1,0:T(8,128)(2,1)} custom-call(s32[1]{0:T(128)} %bitcast.rank_ref, s32[96]{0:T(128)} %slot_ref.5, bf16[160,1024]{1,0:T(8,128)(2,1)} %bitcast.6), custom_call_target="tpu_custom_call" | custom-call | flops 20000000000 | bytes 40000000 | tf_op jit(solution)/shard_map/pick/pallas_call | solution.py:59
  10.0 5.5 %all_gather.3.gathered_ref = bf16[320,128]{1,0:T(8,128)(2,1)S(1)} all-gather(bf16[80,128]{1,0:T(8,128)(2,1)} %pick.1), channel_id=1, replica_groups={{0,8,16,24},{32,40,48,56},{64,72,80,88},{96,104,112,120},{128,136,144,1..., dimensions={0}, use_global_device_ids=true | all-gather | bytes 102400 | tf_op jit(solution)/shard_map/all_gather | solution.py:325
  15.5 0.0 copy-done.1
  15.5 6.7 %block.1 = (bf16[160,1024]{1,0:T(8,128)(2,1)}, bf16[1280,1024]{1,0:T(8,128)(2,1)}, bf16[480,1024]{1,0:T(8,128)(2,1)S(1)}, bf16[16,1280]{1,0:T(8,128)(2,1)S(1)}) custom-call(s32[1]{0:T(128)} %bitcast.rank_ref, s32[96]{0:T(128)S(1)} %copy-done, s32[96]{0:T(128)S(1)} %copy-done.1, s32[1536]{0:T(1024)S(1)} %copy-done.5, bf16[480,1280]{1,0:T(8,128)(2,1)S(1)} %bitcast.5, ...), custom_call_target="tpu_custom_call" | custom-call | flops 6000000000 | bytes 9000000 | tf_op jit(solution)/shard_map/block/pallas_call | solution.py:170
  22.2 0.9 %copy-done.7 = bf16[480,1024]{1,0:T(8,128)(2,1)} copy-done((bf16[480,1024]{1,0:T(8,128)(2,1)}, bf16[480,1024]{1,0:T(8,128)(2,1)S(1)}, u32[]{:S(2)}) %copy-start.7) | copy-done | bytes 983064
  23.2 0.0 reduce-scatter.2.cloned.1.call-update
  23.2 1.0 %copy-done.6 = bf16[512,480]{1,0:T(8,128)(2,1)S(1)} copy-done((bf16[512,480]{1,0:T(8,128)(2,1)S(1)}, bf16[512,480]{1,0:T(8,128)(2,1)}, u32[]{:S(2)}) %copy-start.6) | copy-done | bytes 491544
  24.2 1.2 %copy-done.8 = bf16[480,1024]{1,0:T(8,128)(2,1)S(1)} copy-done((bf16[480,1024]{1,0:T(8,128)(2,1)S(1)}, bf16[480,1024]{1,0:T(8,128)(2,1)}, u32[]{:S(2)}) %copy-start.8) | copy-done | bytes 983064
  25.4 2.2 %sums.1 = (bf16[256,1280]{1,0:T(8,128)(2,1)S(1)}, bf16[272,1280]{1,0:T(8,128)(2,1)S(1)}) custom-call(s32[1]{0:T(128)} %bitcast.rank_ref, bf16[512,480]{1,0:T(8,128)(2,1)S(1)} %copy-done.6, bf16[480,1024]{1,0:T(8,128)(2,1)S(1)} %copy-done.8, bf16[1024,1280]{1,0:T(8,128)(2,1)S(1)} %copy-done.2, bf16[16,1280]{1,0:T(8,128)(2,1)S(1)} %get-tuple-element.12.pack_ref), custom_call_target="tpu_custom_call" | custom-call | flops 2000000000 | bytes 6000000 | tf_op jit(solution)/shard_map/sums/pallas_call | solution.py:204
  27.6 2.2 %collective-permute-start = (bf16[272,1280]{1,0:T(8,128)(2,1)S(1)}, bf16[272,1280]{1,0:T(8,128)(2,1)S(1)}, u32[]{:S(2)}, u32[]{:S(2)}) collective-permute-start(bf16[272,1280]{1,0:T(8,128)(2,1)S(1)} %get-tuple-element.14), channel_id=1, source_target_pairs={{0,8},{8,0},{16,24},{24,16},{32,40},{40,32},{48,56},{56,48},{64,72... | collective-permute-start | bytes 2088968 | tf_op jit(solution)/shard_map/ppermute | solution.py:329
  29.9 1.8 %collective-permute-done.other_ref = bf16[272,1280]{1,0:T(8,128)(2,1)S(1)} collective-permute-done((bf16[272,1280]{1,0:T(8,128)(2,1)S(1)}, bf16[272,1280]{1,0:T(8,128)(2,1)S(1)}, u32[]{:S(2)}, u32[]{:S(2)}) %collective-permute-start) | collective-permute-done | bytes 696352 | tf_op jit(solution)/shard_map/ppermute | solution.py:329
  31.7 0.3 own_half.1
  31.9 23.2 %all_to_all.10.in_ref = bf16[4,80,1280]{2,1,0:T(8,128)(2,1)S(1)} all-to-all(bf16[4,80,1280]{2,1,0:T(8,128)(2,1)S(1)} %own_half.1), channel_id=1, replica_groups={{0,16,32,48},{8,24,40,56},{64,80,96,112},{72,88,104,120},{128,144,160,1..., dimensions={0} | all-to-all | bytes 1638400 | tf_op jit(solution)/shard_map/all_to_all | solution.py:331
  55.2 2.2 %spread.1 = (bf16[12,8,896]{2,1,0:T(8,128)(2,1)S(1)}, bf16[160,1024]{1,0:T(8,128)(2,1)}) custom-call(s32[1]{0:T(128)} %bitcast.rank_ref, s32[96]{0:T(128)S(1)} %copy-done, s32[96]{0:T(128)S(1)} %copy-done.1, bf16[4,80,1280]{2,1,0:T(8,128)(2,1)S(1)} %all_to_all.10.in_ref, bf16[160,1024]{1,0:T(8,128)(2,1)} %get-tuple-element.15.ctx_ref), custom_call_target="tpu_custom_call", output_to_operand_aliasing={{1}: (4, {})} | custom-call | tf_op jit(solution)/shard_map/spread/pallas_call | solution.py:273
  57.3 20.0 %all_to_all.11.in_ref = bf16[12,8,896]{2,1,0:T(8,128)(2,1)S(1)} all-to-all(bf16[12,8,896]{2,1,0:T(8,128)(2,1)S(1)} %get-tuple-element.18), channel_id=1, replica_groups={{0,64,128,192,256,320,384,448,512,576,640,704},{8,72,136,200,264,328,39..., dimensions={0} | all-to-all | bytes 344064 | tf_op jit(solution)/shard_map/all_to_all | solution.py:333
  77.3 0.6 last_sum.1
  78.0 1.2 %reduce-scatter.2.cloned.1.call-done = bf16[160,1024]{1,0:T(8,128)(2,1)} async-done(((bf16[1280,1024]{1,0:T(8,128)(2,1)}), bf16[160,1024]{1,0:T(8,128)(2,1)}) %reduce-scatter.2.cloned.1.call-update) | async-done | bytes 327696 | tf_op jit(solution)/shard_map/reduce_scatter | solution.py:327
  (8 shorter events, 0.0 us)
Async XLA Ops:
  7.2 72.0 %reduce-scatter.2.cloned.1.call-start = ((), (), s32[]{:S(2)}) async-start(), calls=%async_computation.3 | async-start | bytes 2949120 | tf_op jit(solution)/shard_map/reduce_scatter | solution.py:327
  7.2 8.2 %copy-start = (s32[96]{0:T(128)S(1)}, s32[96]{0:T(128)}, u32[]{:S(2)}) copy-start(s32[96]{0:T(128)} %slot_ref.5) | copy-start | bytes 1156
  7.2 8.2 %copy-start.1 = (s32[96]{0:T(128)S(1)}, s32[96]{0:T(128)}, u32[]{:S(2)}) copy-start(s32[96]{0:T(128)} %dest_ref.3) | copy-start | bytes 1156
  7.2 8.2 %copy-start.2 = (bf16[1024,1280]{1,0:T(8,128)(2,1)S(1)}, bf16[1024,1280]{1,0:T(8,128)(2,1)}, u32[]{:S(2)}) copy-start(bf16[1024,1280]{1,0:T(8,128)(2,1)} %x_ref.3) | copy-start | bytes 7864324
  7.2 8.2 %copy-start.3 = (bf16[1280,480]{0,1:T(8,128)(2,1)S(1)}, bf16[1280,480]{0,1:T(8,128)(2,1)}, u32[]{:S(2)}) copy-start(bf16[1280,480]{0,1:T(8,128)(2,1)} %param.8) | copy-start | bytes 3686404
  7.3 8.2 %copy-start.4 = (bf16[1024,160]{0,1:T(8,128)(2,1)S(1)}, bf16[1024,160]{0,1:T(8,128)(2,1)}, u32[]{:S(2)}) copy-start(bf16[1024,160]{0,1:T(8,128)(2,1)} %param.12) | copy-start | bytes 983044
  7.3 8.2 %copy-start.5 = (s32[1536]{0:T(1024)S(1)}, s32[1536]{0:T(1024)}, u32[]{:S(2)}) copy-start(s32[1536]{0:T(1024)} %counts_ref.1) | copy-start | bytes 18436
  22.2 1.0 %copy-start.7 = (bf16[480,1024]{1,0:T(8,128)(2,1)}, bf16[480,1024]{1,0:T(8,128)(2,1)S(1)}, u32[]{:S(2)}) copy-start(bf16[480,1024]{1,0:T(8,128)(2,1)S(1)} %get-tuple-element.11.dqkv_ref) | copy-start | bytes 2949124
  23.2 1.0 %copy-start.6 = (bf16[512,480]{1,0:T(8,128)(2,1)S(1)}, bf16[512,480]{1,0:T(8,128)(2,1)}, u32[]{:S(2)}) copy-start(bf16[512,480]{1,0:T(8,128)(2,1)} %constant.7.clone.order_ref) | copy-start | bytes 1474564
  24.2 1.2 %copy-start.8 = (bf16[480,1024]{1,0:T(8,128)(2,1)S(1)}, bf16[480,1024]{1,0:T(8,128)(2,1)}, u32[]{:S(2)}) copy-start(bf16[480,1024]{1,0:T(8,128)(2,1)} %copy-done.7) | copy-start | bytes 2949124
  27.6 4.1 %collective-permute-start = (bf16[272,1280]{1,0:T(8,128)(2,1)S(1)}, bf16[272,1280]{1,0:T(8,128)(2,1)S(1)}, u32[]{:S(2)}, u32[]{:S(2)}) collective-permute-start(bf16[272,1280]{1,0:T(8,128)(2,1)S(1)} %get-tuple-element.14), channel_id=1, source_target_pairs={{0,8},{8,0},{16,24},{24,16},{32,40},{40,32},{48,56},{56,48},{64,72... | collective-permute-start | bytes 2088968 | tf_op jit(solution)/shard_map/ppermute | solution.py:329
Sparse Core Ops, SparseCore 0:
  23.3 55.8 reduce-scatter.1

commit v6 on v5

--- a/solution.py
+++ b/solution.py
@@ -1,6 +1,5 @@
 import jax
 import jax.numpy as jnp
-import numpy as np
 from jax import lax
 from jax.experimental import pallas as pl
 from jax.experimental.pallas import tpu as pltpu
@@ -18,6 +17,7 @@
 PAIR = 2 * BLOCK
 STEP = 4 * PAIR
 CUT = 256
+PARTS = 6
 N_X = 4
 N_Z = 12
 PACK = 16
@@ -35,12 +35,13 @@
 SMALL = pltpu.CompilerParams(vmem_limit_bytes=16 * 2**20)
 
 
-def owner_order():
-    order = np.zeros((512, COLS), np.float32)
-    for c in range(COLS):
-        z, x, core, i = c // 40, c % 40 // 10, c % 10 // 5, c % 5
-        order[core * 256 + x * 64 + z * 5 + i, c] = 1
-    return order.astype(jnp.bfloat16)
+def owner_order(core):
+    row = lax.broadcasted_iota(jnp.int32, (256, COLS), 0)
+    column = lax.broadcasted_iota(jnp.int32, (256, COLS), 1)
+    place = row & 63
+    z = (place * 205) >> 10
+    source = z * 35 + place + (row >> 6) * 10 + core * 5
+    return jnp.where((source == column) & (place < 5 * N_Z), 1.0, 0.0).astype(BF16)
 
 
 def dot(a, b, dims):
@@ -126,10 +127,8 @@
         dqkv_buf[base + 2 * HD : base + 3 * HD, columns] = dv[c].astype(BF16)
 
 
-def block_kernel(
-    rank_ref, slot_ref, dest_ref, counts_ref, w_ref, x_ref, grad_ref, gathered_ref, ctx_ref, term_ref, dqkv_ref, pack_ref,
-    qkv_buf, turned_buf, ctx_buf, dqkv_buf, term_buf, out_sems,
-):
+def block_kernel(rank_ref, slot_ref, dest_ref, counts_ref, w_ref, x_ref, grad_ref, gathered_ref, ctx_ref, term_ref, pack_ref, *more):
+    dqkv_refs, (qkv_buf, turned_buf, ctx_buf, dqkv_buf, term_buf, out_sems) = more[:PARTS], more[PARTS:]
     me = rank_ref[0]
     slot = slot_ref[me]
     host = dest_ref[me]
@@ -147,16 +146,15 @@
         project(group)
     for group in range(ROWS // STEP):
         attend(me, slot, group, lent, counts_ref, grad_ref, qkv_buf, ctx_buf, dqkv_buf)
-    stores = [
-        pltpu.make_async_copy(ctx_buf, ctx_ref, out_sems.at[0]),
-        pltpu.make_async_copy(dqkv_buf, dqkv_ref, out_sems.at[1]),
-    ]
-    stores[0].start()
-    stores[1].start()
+    stores = [pltpu.make_async_copy(ctx_buf, ctx_ref, out_sems.at[0])]
+    for part, dqkv_ref in enumerate(dqkv_refs):
+        stores.append(pltpu.make_async_copy(dqkv_buf.at[part * HD : (part + 1) * HD], dqkv_ref, out_sems.at[1 + part]))
+    for store in stores:
+        store.start()
     for piece in range(D // CUT):
         rows = pl.ds(piece * CUT, CUT)
         term_buf[rows, :] = dot(turned_buf[rows, :], dqkv_buf[...], NN).astype(BF16)
-        stores.append(pltpu.make_async_copy(term_buf.at[rows], term_ref.at[rows], out_sems.at[2 + piece]))
+        stores.append(pltpu.make_async_copy(term_buf.at[rows], term_ref.at[rows], out_sems.at[1 + PARTS + piece]))
         stores[-1].start()
     mine = ctx_buf[:, pl.ds(pl.multiple_of(slot // 2 * PAIR, PAIR), PAIR)]
     mine = shifted(mine, upper).astype(BF16)
@@ -170,20 +168,20 @@
     return pl.pallas_call(
         block_kernel,
         in_specs=[SMEM] * 4 + [VMEM] * 4,
-        out_specs=[HBM] * 3 + [VMEM],
+        out_specs=[HBM] * 2 + [VMEM] + [HBM] * PARTS,
         out_shape=[
             jax.ShapeDtypeStruct((WIDTH, ROWS), BF16),
             jax.ShapeDtypeStruct((D, ROWS), BF16),
-            jax.ShapeDtypeStruct((COLS, ROWS), BF16),
             jax.ShapeDtypeStruct((PACK, D), BF16),
-        ],
+        ]
+        + [jax.ShapeDtypeStruct((HD, ROWS), BF16)] * PARTS,
         scratch_shapes=[
             pltpu.VMEM((COLS, ROWS), BF16),
             pltpu.VMEM((D, COLS), BF16),
             pltpu.VMEM((WIDTH, ROWS), BF16),
             pltpu.VMEM((COLS, ROWS), BF16),
             pltpu.VMEM((D, ROWS), BF16),
-            pltpu.SemaphoreType.DMA((2 + D // CUT,)),
+            pltpu.SemaphoreType.DMA((1 + PARTS + D // CUT,)),
         ],
         cost_estimate=pl.CostEstimate(flops=6_000_000_000, bytes_accessed=9_000_000, transcendentals=300_000),
         compiler_params=pltpu.CompilerParams(vmem_limit_bytes=32 * 2**20),
@@ -191,25 +189,28 @@
     )(rank, slots, dest, counts, weight, patches, grad, gathered)
 
 
-def sums_kernel(rank_ref, order_ref, dqkv_ref, x_ref, pack_ref, own_ref, send_ref):
+def sums_kernel(rank_ref, x_ref, pack_ref, *more):
+    dqkv_refs, (own_ref, send_ref, dqkv_buf) = more[:PARTS], more[PARTS:]
+    for part, dqkv_ref in enumerate(dqkv_refs):
+        dqkv_buf[part * HD : (part + 1) * HD, :] = dqkv_ref[...]
     core = lax.rem(rank_ref[0], 2)
     for which, ref in ((1 - core, send_ref), (core, own_ref)):
-        order = order_ref[pl.ds(pl.multiple_of(which * 256, 256), 256), :]
-        sorted_grad = dot(order, dqkv_ref[...], NN).astype(BF16)
+        sorted_grad = dot(owner_order(which), dqkv_buf[...], NN).astype(BF16)
         ref[0:256, :] = (dot(sorted_grad, x_ref[...], NN) * (1.0 / ROWS)).astype(BF16)
     send_ref[256 : 256 + PACK, :] = pack_ref[...]
 
 
-def sums(rank, order, dqkv, patches, pack):
+def sums(rank, patches, pack, dqkv):
     return pl.pallas_call(
         sums_kernel,
-        in_specs=[SMEM] + [VMEM] * 4,
+        in_specs=[SMEM] + [VMEM] * (2 + PARTS),
         out_specs=[VMEM] * 2,
         out_shape=[jax.ShapeDtypeStruct((256, D), BF16), jax.ShapeDtypeStruct((256 + PACK, D), BF16)],
+        scratch_shapes=[pltpu.VMEM((COLS, ROWS), BF16)],
         cost_estimate=pl.CostEstimate(flops=2_000_000_000, bytes_accessed=6_000_000, transcendentals=0),
         compiler_params=SMALL,
         name="sums",
-    )(rank, order, dqkv, patches, pack)
+    )(rank, patches, pack, *dqkv)
 
 
 def own_kernel(own_ref, pack_ref, other_ref, out_ref):
@@ -323,9 +324,9 @@
     x_groups = [[z * 8 + x * 2 + core for x in range(N_X)] for z in range(N_Z) for core in range(2)]
     z_groups = [[z * 8 + place for z in range(N_Z)] for place in range(8)]
     gathered = lax.all_gather(pick(rank, lend_slot, grad), "dp", axis=0, tiled=True, axis_index_groups=groups)
-    ctx, terms, dqkv, pack = block(rank, lend_slot, lend_dest, patch_counts, weight, patches, grad, gathered)
+    ctx, terms, pack, *dqkv = block(rank, lend_slot, lend_dest, patch_counts, weight, patches, grad, gathered)
     summed = lax.psum_scatter(terms, "tensor", scatter_dimension=0, tiled=True)
-    own, sent = sums(rank, jnp.asarray(owner_order()), dqkv, patches, pack)
+    own, sent = sums(rank, patches, pack, dqkv)
     received = lax.ppermute(sent, "dp", [(p, p ^ 1) for p in range(N_DP)])
     parts = own_half(own, pack, received)
     parts = lax.all_to_all(parts, "dp", 0, 0, axis_index_groups=x_groups)

time: 86.8 us -> 87 us (level)
  local copies, waits for them, and re-layouts: 3.19 us -> 1.59 us
  waiting for transfers between devices: 3 us -> 4.18 us
  Pallas kernels: 14.7 us -> 15.7 us
    unnamed x18 -> x16, local copies, waits for them, and re-layouts: 3.19 us -> 1.59 us
    reduce_scatter x1, waiting for transfers between devices: 1.19 us -> 2.38 us  [shards(): summed = lax.psum_scatter(terms, 'tensor', scatter_dimension=0, tiled=True)]
    pallas_call x1, Pallas kernels: 6.72 us -> 7.7 us  [block(): pl.pallas_call(block_kernel, in_specs=[SMEM] * 4 + [VMEM] * 4, out_specs=...]
where the time goes in v6:
time: 87 us; the launch traced here: 86.6 us
  blocking collectives  48.7 us (56%)
  Pallas kernels  15.7 us (18%)
  between operations  14.2 us (16%)
  waiting for transfers between devices  4.18 us (5%)
  starting transfers between devices  2.29 us (3%)
  local copies, waits for them, and re-layouts  1.59 us (2%)
    all_to_all x1, blocking collectives, shards(): parts = lax.all_to_all(parts, 'dp', 0, 0, axis_index_groups=x_groups)  23.2 us
    all_to_all x1, blocking collectives, shards(): parts = lax.all_to_all(parts, 'dp', 0, 0, axis_index_groups=z_groups)  20 us
    pallas_call x1, Pallas kernels, block(): pl.pallas_call(block_kernel, in_specs=[SMEM] * 4 + [VMEM] * 4, out_specs=...  7.7 us
    all_gather x1, blocking collectives, shards(): lax.all_gather(pick(rank, lend_slot, grad), 'dp', axis=0, tiled=True, axi...  5.49 us
    pallas_call x1, Pallas kernels, pick(): pl.pallas_call(pick_kernel, grid_spec=pltpu.PrefetchScalarGridSpec(num_sc...  2.69 us
    reduce_scatter x1, waiting for transfers between devices, shards(): summed = lax.psum_scatter(terms, 'tensor', scatter_dimension=0, tiled=True)  2.38 us
    ppermute x1, starting transfers between devices, shards(): received = lax.ppermute(sent, 'dp', [(p, p ^ 1) for p in range(N_DP)])  2.26 us
    pallas_call x1, Pallas kernels, sums(): pl.pallas_call(sums_kernel, in_specs=[SMEM] + [VMEM] * (2 + PARTS), out_s...  2.2 us
  transfers between devices with their start and end apart: 2, of which 2 were waited for; matrix products, arithmetic and copies ran while one was open for 0% of the time, Pallas kernels for 6%

profile of v6, /device:TPU:6, one launch (start us, length us, event | category | flops | bytes accessed | tf_op | source)
XLA Modules:
  0.0 86.6 jit_solution(12289749895937820640)
XLA Ops:
  7.2 0.0 reduce-scatter.2.cloned.1.call-start
  7.2 0.0 copy-start
  7.2 0.0 copy-start.1
  7.2 0.0 copy-start.2
  7.2 0.0 copy-start.3
  7.3 0.0 copy-start.4
  7.3 0.0 copy-start.5
  7.3 2.7 %pick.1 = bf16[80,128]{1,0:T(8,128)(2,1)} custom-call(s32[1]{0:T(128)} %bitcast.rank_ref, s32[96]{0:T(128)} %slot_ref.5, bf16[160,1024]{1,0:T(8,128)(2,1)} %bitcast.6), custom_call_target="tpu_custom_call" | custom-call | flops 20000000000 | bytes 40000000 | tf_op jit(solution)/shard_map/pick/pallas_call | solution.py:60
  10.0 5.5 %all_gather.3.gathered_ref = bf16[320,128]{1,0:T(8,128)(2,1)S(1)} all-gather(bf16[80,128]{1,0:T(8,128)(2,1)} %pick.1), channel_id=1, replica_groups={{0,8,16,24},{32,40,48,56},{64,72,80,88},{96,104,112,120},{128,136,144,1..., dimensions={0}, use_global_device_ids=true | all-gather | bytes 102400 | tf_op jit(solution)/shard_map/all_gather | solution.py:326
  15.5 0.0 copy-done
  15.5 0.0 copy-done.1
  15.5 7.7 %block.1 = (bf16[160,1024]{1,0:T(8,128)(2,1)}, bf16[1280,1024]{1,0:T(8,128)(2,1)}, bf16[16,1280]{1,0:T(8,128)(2,1)S(1)}, bf16[80,1024]{1,0:T(8,128)(2,1)S(1)}, b...) custom-call(s32[1]{0:T(128)} %bitcast.rank_ref, ...), custom_call_target="tpu_custom_call" | custom-call | flops 6000000000 | bytes 9000000 | tf_op jit(solution)/shard_map/block/pallas_call | solution.py:168
  23.2 0.7 copy-done.6
  23.9 0.0 reduce-scatter.2.cloned.1.call-update
  23.9 0.9 %copy-done.7 = bf16[80,1024]{1,0:T(8,128)(2,1)S(1)} copy-done((bf16[80,1024]{1,0:T(8,128)(2,1)S(1)}, bf16[80,1024]{1,0:T(8,128)(2,1)}, u32[]{:S(2)}) %copy-start.7) | copy-done | bytes 163864
  24.8 2.2 %sums.1 = (bf16[256,1280]{1,0:T(8,128)(2,1)S(1)}, bf16[272,1280]{1,0:T(8,128)(2,1)S(1)}) custom-call(s32[1]{0:T(128)} %bitcast.rank_ref, bf16[1024,1280]{1,0:T(8,128)(2,1)S(1)} %copy-done.2, bf16[16,1280]{1,0:T(8,128)(2,1)S(1)} %get-tuple-element.16.pack_ref, bf16[80,1024]{1,0:T(8,128)(2,1)S(1)} %get-tuple-element.17.more_0_, ...), custom_call_target="tpu_custom_call" | custom-call | flops 2000000000 | bytes 6000000 | tf_op jit(solution)/shard_map/sums/pallas_call | solution.py:204
  27.0 2.3 %collective-permute-start = (bf16[272,1280]{1,0:T(8,128)(2,1)S(1)}, bf16[272,1280]{1,0:T(8,128)(2,1)S(1)}, u32[]{:S(2)}, u32[]{:S(2)}) collective-permute-start(bf16[272,1280]{1,0:T(8,128)(2,1)S(1)} %get-tuple-element.24), channel_id=1, source_target_pairs={{0,8},{8,0},{16,24},{24,16},{32,40},{40,32},{48,56},{56,48},{64,72... | collective-permute-start | bytes 2088968 | tf_op jit(solution)/shard_map/ppermute | solution.py:330
  29.3 1.8 %collective-permute-done.other_ref = bf16[272,1280]{1,0:T(8,128)(2,1)S(1)} collective-permute-done((bf16[272,1280]{1,0:T(8,128)(2,1)S(1)}, bf16[272,1280]{1,0:T(8,128)(2,1)S(1)}, u32[]{:S(2)}, u32[]{:S(2)}) %collective-permute-start) | collective-permute-done | bytes 696352 | tf_op jit(solution)/shard_map/ppermute | solution.py:330
  31.1 0.3 own_half.1
  31.3 23.2 %all_to_all.10.in_ref = bf16[4,80,1280]{2,1,0:T(8,128)(2,1)S(1)} all-to-all(bf16[4,80,1280]{2,1,0:T(8,128)(2,1)S(1)} %own_half.1), channel_id=1, replica_groups={{0,16,32,48},{8,24,40,56},{64,80,96,112},{72,88,104,120},{128,144,160,1..., dimensions={0} | all-to-all | bytes 1638400 | tf_op jit(solution)/shard_map/all_to_all | solution.py:332
  54.6 2.2 %spread.1 = (bf16[12,8,896]{2,1,0:T(8,128)(2,1)S(1)}, bf16[160,1024]{1,0:T(8,128)(2,1)}) custom-call(s32[1]{0:T(128)} %bitcast.rank_ref, s32[96]{0:T(128)S(1)} %copy-done, s32[96]{0:T(128)S(1)} %copy-done.1, bf16[4,80,1280]{2,1,0:T(8,128)(2,1)S(1)} %all_to_all.10.in_ref, bf16[160,1024]{1,0:T(8,128)(2,1)} %get-tuple-element.25.ctx_ref), custom_call_target="tpu_custom_call", output_to_operand_aliasing={{1}: (4, {})} | custom-call | tf_op jit(solution)/shard_map/spread/pallas_call | solution.py:274
  56.7 20.0 %all_to_all.11.in_ref = bf16[12,8,896]{2,1,0:T(8,128)(2,1)S(1)} all-to-all(bf16[12,8,896]{2,1,0:T(8,128)(2,1)S(1)} %get-tuple-element.28), channel_id=1, replica_groups={{0,64,128,192,256,320,384,448,512,576,640,704},{8,72,136,200,264,328,39..., dimensions={0} | all-to-all | bytes 344064 | tf_op jit(solution)/shard_map/all_to_all | solution.py:334
  76.7 0.6 last_sum.1
  77.4 2.4 %reduce-scatter.2.cloned.1.call-done = bf16[160,1024]{1,0:T(8,128)(2,1)} async-done(((bf16[1280,1024]{1,0:T(8,128)(2,1)}), bf16[160,1024]{1,0:T(8,128)(2,1)}) %reduce-scatter.2.cloned.1.call-update) | async-done | bytes 327696 | tf_op jit(solution)/shard_map/reduce_scatter | solution.py:328
  (6 shorter events, 0.0 us)
Async XLA Ops:
  7.2 72.6 %reduce-scatter.2.cloned.1.call-start = ((), (), s32[]{:S(2)}) async-start(), calls=%async_computation.3 | async-start | bytes 2949120 | tf_op jit(solution)/shard_map/reduce_scatter | solution.py:328
  7.2 8.2 %copy-start = (s32[96]{0:T(128)S(1)}, s32[96]{0:T(128)}, u32[]{:S(2)}) copy-start(s32[96]{0:T(128)} %slot_ref.5) | copy-start | bytes 1156
  7.2 8.2 %copy-start.1 = (s32[96]{0:T(128)S(1)}, s32[96]{0:T(128)}, u32[]{:S(2)}) copy-start(s32[96]{0:T(128)} %dest_ref.3) | copy-start | bytes 1156
  7.2 8.2 %copy-start.2 = (bf16[1024,1280]{1,0:T(8,128)(2,1)S(1)}, bf16[1024,1280]{1,0:T(8,128)(2,1)}, u32[]{:S(2)}) copy-start(bf16[1024,1280]{1,0:T(8,128)(2,1)} %x_ref.3) | copy-start | bytes 7864324
  7.2 8.2 %copy-start.3 = (bf16[1280,480]{0,1:T(8,128)(2,1)S(1)}, bf16[1280,480]{0,1:T(8,128)(2,1)}, u32[]{:S(2)}) copy-start(bf16[1280,480]{0,1:T(8,128)(2,1)} %param.7) | copy-start | bytes 3686404
  7.3 8.2 %copy-start.4 = (bf16[1024,160]{0,1:T(8,128)(2,1)S(1)}, bf16[1024,160]{0,1:T(8,128)(2,1)}, u32[]{:S(2)}) copy-start(bf16[1024,160]{0,1:T(8,128)(2,1)} %param.11) | copy-start | bytes 983044
  7.3 8.2 %copy-start.5 = (s32[1536]{0:T(1024)S(1)}, s32[1536]{0:T(1024)}, u32[]{:S(2)}) copy-start(s32[1536]{0:T(1024)} %counts_ref.1) | copy-start | bytes 18436
  23.2 0.7 copy-start.6
  23.9 0.9 %copy-start.7 = (bf16[80,1024]{1,0:T(8,128)(2,1)S(1)}, bf16[80,1024]{1,0:T(8,128)(2,1)}, u32[]{:S(2)}) copy-start(bf16[80,1024]{1,0:T(8,128)(2,1)} %copy-done.6) | copy-start | bytes 491524
  27.0 4.1 %collective-permute-start = (bf16[272,1280]{1,0:T(8,128)(2,1)S(1)}, bf16[272,1280]{1,0:T(8,128)(2,1)S(1)}, u32[]{:S(2)}, u32[]{:S(2)}) collective-permute-start(bf16[272,1280]{1,0:T(8,128)(2,1)S(1)} %get-tuple-element.24), channel_id=1, source_target_pairs={{0,8},{8,0},{16,24},{24,16},{32,40},{40,32},{48,56},{56,48},{64,72... | collective-permute-start | bytes 2088968 | tf_op jit(solution)/shard_map/ppermute | solution.py:330
Sparse Core Ops, SparseCore 0:
  24.0 55.6 reduce-scatter.1

commit v7 on v6

--- a/solution.py
+++ b/solution.py
@@ -148,13 +148,13 @@
         attend(me, slot, group, lent, counts_ref, grad_ref, qkv_buf, ctx_buf, dqkv_buf)
     stores = [pltpu.make_async_copy(ctx_buf, ctx_ref, out_sems.at[0])]
     for part, dqkv_ref in enumerate(dqkv_refs):
-        stores.append(pltpu.make_async_copy(dqkv_buf.at[part * HD : (part + 1) * HD], dqkv_ref, out_sems.at[1 + part]))
+        dqkv_ref[...] = dqkv_buf[part * HD : (part + 1) * HD, :]
     for store in stores:
         store.start()
     for piece in range(D // CUT):
         rows = pl.ds(piece * CUT, CUT)
         term_buf[rows, :] = dot(turned_buf[rows, :], dqkv_buf[...], NN).astype(BF16)
-        stores.append(pltpu.make_async_copy(term_buf.at[rows], term_ref.at[rows], out_sems.at[1 + PARTS + piece]))
+        stores.append(pltpu.make_async_copy(term_buf.at[rows], term_ref.at[rows], out_sems.at[1 + piece]))
         stores[-1].start()
     mine = ctx_buf[:, pl.ds(pl.multiple_of(slot // 2 * PAIR, PAIR), PAIR)]
     mine = shifted(mine, upper).astype(BF16)
@@ -168,7 +168,7 @@
     return pl.pallas_call(
         block_kernel,
         in_specs=[SMEM] * 4 + [VMEM] * 4,
-        out_specs=[HBM] * 2 + [VMEM] + [HBM] * PARTS,
+        out_specs=[HBM] * 2 + [VMEM] * (1 + PARTS),
         out_shape=[
             jax.ShapeDtypeStruct((WIDTH, ROWS), BF16),
             jax.ShapeDtypeStruct((D, ROWS), BF16),
@@ -181,7 +181,7 @@
             pltpu.VMEM((WIDTH, ROWS), BF16),
             pltpu.VMEM((COLS, ROWS), BF16),
             pltpu.VMEM((D, ROWS), BF16),
-            pltpu.SemaphoreType.DMA((1 + PARTS + D // CUT,)),
+            pltpu.SemaphoreType.DMA((1 + D // CUT,)),
         ],
         cost_estimate=pl.CostEstimate(flops=6_000_000_000, bytes_accessed=9_000_000, transcendentals=300_000),
         compiler_params=pltpu.CompilerParams(vmem_limit_bytes=32 * 2**20),

time: 87 us -> 85.8 us (0.986)
  Pallas kernels: 15.7 us -> 14.4 us
    pallas_call x1, Pallas kernels: 7.7 us -> 6.42 us  [block(): pl.pallas_call(block_kernel, in_specs=[SMEM] * 4 + [VMEM] * 4, out_specs=...]
where the time goes in v7:
time: 85.8 us; the launch traced here: 85.3 us
  blocking collectives  48.7 us (57%)
  Pallas kernels  14.4 us (17%)
  between operations  14.2 us (17%)
  waiting for transfers between devices  4.18 us (5%)
  starting transfers between devices  2.3 us (3%)
  local copies, waits for them, and re-layouts  1.59 us (2%)
    all_to_all x1, blocking collectives, shards(): parts = lax.all_to_all(parts, 'dp', 0, 0, axis_index_groups=x_groups)  23.2 us
    all_to_all x1, blocking collectives, shards(): parts = lax.all_to_all(parts, 'dp', 0, 0, axis_index_groups=z_groups)  20 us
    pallas_call x1, Pallas kernels, block(): pl.pallas_call(block_kernel, in_specs=[SMEM] * 4 + [VMEM] * 4, out_specs=...  6.42 us
    all_gather x1, blocking collectives, shards(): lax.all_gather(pick(rank, lend_slot, grad), 'dp', axis=0, tiled=True, axi...  5.49 us
    pallas_call x1, Pallas kernels, pick(): pl.pallas_call(pick_kernel, grid_spec=pltpu.PrefetchScalarGridSpec(num_sc...  2.69 us
    reduce_scatter x1, waiting for transfers between devices, shards(): summed = lax.psum_scatter(terms, 'tensor', scatter_dimension=0, tiled=True)  2.38 us
    ppermute x1, starting transfers between devices, shards(): received = lax.ppermute(sent, 'dp', [(p, p ^ 1) for p in range(N_DP)])  2.26 us
    pallas_call x1, Pallas kernels, sums(): pl.pallas_call(sums_kernel, in_specs=[SMEM] + [VMEM] * (2 + PARTS), out_s...  2.2 us
  transfers between devices with their start and end apart: 2, of which 2 were waited for; matrix products, arithmetic and copies ran while one was open for 0% of the time, Pallas kernels for 6%

profile of v7, /device:TPU:6, one launch (start us, length us, event | category | flops | bytes accessed | tf_op | source)
XLA Modules:
  0.0 85.3 jit_solution(5918676736383090270)
XLA Ops:
  7.2 0.0 reduce-scatter.2.cloned.1.call-start
  7.2 0.0 copy-start
  7.2 0.0 copy-start.1
  7.2 0.0 copy-start.2
  7.2 0.0 copy-start.3
  7.3 0.0 copy-start.4
  7.3 0.0 copy-start.5
  7.3 2.7 %pick.1 = bf16[80,128]{1,0:T(8,128)(2,1)} custom-call(s32[1]{0:T(128)} %bitcast.rank_ref, s32[96]{0:T(128)} %slot_ref.5, bf16[160,1024]{1,0:T(8,128)(2,1)} %bitcast.6), custom_call_target="tpu_custom_call" | custom-call | flops 20000000000 | bytes 40000000 | tf_op jit(solution)/shard_map/pick/pallas_call | solution.py:60
  10.0 5.5 %all_gather.3.gathered_ref = bf16[320,128]{1,0:T(8,128)(2,1)S(1)} all-gather(bf16[80,128]{1,0:T(8,128)(2,1)} %pick.1), channel_id=1, replica_groups={{0,8,16,24},{32,40,48,56},{64,72,80,88},{96,104,112,120},{128,136,144,1..., dimensions={0}, use_global_device_ids=true | all-gather | bytes 102400 | tf_op jit(solution)/shard_map/all_gather | solution.py:326
  15.5 0.0 copy-done
  15.5 0.0 copy-done.1
  15.5 6.4 %block.1 = (bf16[160,1024]{1,0:T(8,128)(2,1)}, bf16[1280,1024]{1,0:T(8,128)(2,1)}, bf16[16,1280]{1,0:T(8,128)(2,1)S(1)}, bf16[80,1024]{1,0:T(8,128)(2,1)S(1)}, b...) custom-call(s32[1]{0:T(128)} %bitcast.rank_ref, ...), custom_call_target="tpu_custom_call" | custom-call | flops 6000000000 | bytes 9000000 | tf_op jit(solution)/shard_map/block/pallas_call | solution.py:168
  21.9 0.7 copy-done.6
  22.6 0.0 reduce-scatter.2.cloned.1.call-update
  22.6 0.9 %copy-done.7 = bf16[80,1024]{1,0:T(8,128)(2,1)S(1)} copy-done((bf16[80,1024]{1,0:T(8,128)(2,1)S(1)}, bf16[80,1024]{1,0:T(8,128)(2,1)}, u32[]{:S(2)}) %copy-start.7) | copy-done | bytes 163864
  23.5 2.2 %sums.1 = (bf16[256,1280]{1,0:T(8,128)(2,1)S(1)}, bf16[272,1280]{1,0:T(8,128)(2,1)S(1)}) custom-call(s32[1]{0:T(128)} %bitcast.rank_ref, bf16[1024,1280]{1,0:T(8,128)(2,1)S(1)} %copy-done.2, bf16[16,1280]{1,0:T(8,128)(2,1)S(1)} %get-tuple-element.16.pack_ref, bf16[80,1024]{1,0:T(8,128)(2,1)S(1)} %get-tuple-element.17.more_0_, ...), custom_call_target="tpu_custom_call" | custom-call | flops 2000000000 | bytes 6000000 | tf_op jit(solution)/shard_map/sums/pallas_call | solution.py:204
  25.7 2.3 %collective-permute-start = (bf16[272,1280]{1,0:T(8,128)(2,1)S(1)}, bf16[272,1280]{1,0:T(8,128)(2,1)S(1)}, u32[]{:S(2)}, u32[]{:S(2)}) collective-permute-start(bf16[272,1280]{1,0:T(8,128)(2,1)S(1)} %get-tuple-element.24), channel_id=1, source_target_pairs={{0,8},{8,0},{16,24},{24,16},{32,40},{40,32},{48,56},{56,48},{64,72... | collective-permute-start | bytes 2088968 | tf_op jit(solution)/shard_map/ppermute | solution.py:330
  28.0 1.8 %collective-permute-done.other_ref = bf16[272,1280]{1,0:T(8,128)(2,1)S(1)} collective-permute-done((bf16[272,1280]{1,0:T(8,128)(2,1)S(1)}, bf16[272,1280]{1,0:T(8,128)(2,1)S(1)}, u32[]{:S(2)}, u32[]{:S(2)}) %collective-permute-start) | collective-permute-done | bytes 696352 | tf_op jit(solution)/shard_map/ppermute | solution.py:330
  29.8 0.3 own_half.1
  30.1 23.2 %all_to_all.10.in_ref = bf16[4,80,1280]{2,1,0:T(8,128)(2,1)S(1)} all-to-all(bf16[4,80,1280]{2,1,0:T(8,128)(2,1)S(1)} %own_half.1), channel_id=1, replica_groups={{0,16,32,48},{8,24,40,56},{64,80,96,112},{72,88,104,120},{128,144,160,1..., dimensions={0} | all-to-all | bytes 1638400 | tf_op jit(solution)/shard_map/all_to_all | solution.py:332
  53.3 2.2 %spread.1 = (bf16[12,8,896]{2,1,0:T(8,128)(2,1)S(1)}, bf16[160,1024]{1,0:T(8,128)(2,1)}) custom-call(s32[1]{0:T(128)} %bitcast.rank_ref, s32[96]{0:T(128)S(1)} %copy-done, s32[96]{0:T(128)S(1)} %copy-done.1, bf16[4,80,1280]{2,1,0:T(8,128)(2,1)S(1)} %all_to_all.10.in_ref, bf16[160,1024]{1,0:T(8,128)(2,1)} %get-tuple-element.25.ctx_ref), custom_call_target="tpu_custom_call", output_to_operand_aliasing={{1}: (4, {})} | custom-call | tf_op jit(solution)/shard_map/spread/pallas_call | solution.py:274
  55.4 20.0 %all_to_all.11.in_ref = bf16[12,8,896]{2,1,0:T(8,128)(2,1)S(1)} all-to-all(bf16[12,8,896]{2,1,0:T(8,128)(2,1)S(1)} %get-tuple-element.28), channel_id=1, replica_groups={{0,64,128,192,256,320,384,448,512,576,640,704},{8,72,136,200,264,328,39..., dimensions={0} | all-to-all | bytes 344064 | tf_op jit(solution)/shard_map/all_to_all | solution.py:334
  75.5 0.6 last_sum.1
  76.1 2.4 %reduce-scatter.2.cloned.1.call-done = bf16[160,1024]{1,0:T(8,128)(2,1)} async-done(((bf16[1280,1024]{1,0:T(8,128)(2,1)}), bf16[160,1024]{1,0:T(8,128)(2,1)}) %reduce-scatter.2.cloned.1.call-update) | async-done | bytes 327696 | tf_op jit(solution)/shard_map/reduce_scatter | solution.py:328
  (6 shorter events, 0.0 us)
Async XLA Ops:
  7.2 71.3 %reduce-scatter.2.cloned.1.call-start = ((), (), s32[]{:S(2)}) async-start(), calls=%async_computation.3 | async-start | bytes 2949120 | tf_op jit(solution)/shard_map/reduce_scatter | solution.py:328
  7.2 8.2 %copy-start = (s32[96]{0:T(128)S(1)}, s32[96]{0:T(128)}, u32[]{:S(2)}) copy-start(s32[96]{0:T(128)} %slot_ref.5) | copy-start | bytes 1156
  7.2 8.2 %copy-start.1 = (s32[96]{0:T(128)S(1)}, s32[96]{0:T(128)}, u32[]{:S(2)}) copy-start(s32[96]{0:T(128)} %dest_ref.3) | copy-start | bytes 1156
  7.2 8.2 %copy-start.2 = (bf16[1024,1280]{1,0:T(8,128)(2,1)S(1)}, bf16[1024,1280]{1,0:T(8,128)(2,1)}, u32[]{:S(2)}) copy-start(bf16[1024,1280]{1,0:T(8,128)(2,1)} %x_ref.3) | copy-start | bytes 7864324
  7.2 8.2 %copy-start.3 = (bf16[1280,480]{0,1:T(8,128)(2,1)S(1)}, bf16[1280,480]{0,1:T(8,128)(2,1)}, u32[]{:S(2)}) copy-start(bf16[1280,480]{0,1:T(8,128)(2,1)} %param.7) | copy-start | bytes 3686404
  7.3 8.2 %copy-start.4 = (bf16[1024,160]{0,1:T(8,128)(2,1)S(1)}, bf16[1024,160]{0,1:T(8,128)(2,1)}, u32[]{:S(2)}) copy-start(bf16[1024,160]{0,1:T(8,128)(2,1)} %param.11) | copy-start | bytes 983044
  7.3 8.2 %copy-start.5 = (s32[1536]{0:T(1024)S(1)}, s32[1536]{0:T(1024)}, u32[]{:S(2)}) copy-start(s32[1536]{0:T(1024)} %counts_ref.1) | copy-start | bytes 18436
  21.9 0.7 copy-start.6
  22.6 0.9 %copy-start.7 = (bf16[80,1024]{1,0:T(8,128)(2,1)S(1)}, bf16[80,1024]{1,0:T(8,128)(2,1)}, u32[]{:S(2)}) copy-start(bf16[80,1024]{1,0:T(8,128)(2,1)} %copy-done.6) | copy-start | bytes 491524
  25.7 4.1 %collective-permute-start = (bf16[272,1280]{1,0:T(8,128)(2,1)S(1)}, bf16[272,1280]{1,0:T(8,128)(2,1)S(1)}, u32[]{:S(2)}, u32[]{:S(2)}) collective-permute-start(bf16[272,1280]{1,0:T(8,128)(2,1)S(1)} %get-tuple-element.24), channel_id=1, source_target_pairs={{0,8},{8,0},{16,24},{24,16},{32,40},{40,32},{48,56},{56,48},{64,72... | collective-permute-start | bytes 2088968 | tf_op jit(solution)/shard_map/ppermute | solution.py:330
Sparse Core Ops, SparseCore 0:
  22.7 55.7 reduce-scatter.1

commit v8 on v7

--- a/solution.py
+++ b/solution.py
@@ -48,28 +48,29 @@
     return lax.dot_general(a, b, dims, preferred_element_type=F32)
 
 
-def pick_kernel(rank_ref, slot_ref, in_ref, out_ref):
-    upper = lax.rem(slot_ref[rank_ref[0]], 2) == 1
+def pick_kernel(slot_ref, in_ref, out_ref, tile_ref, sem):
+    slot = slot_ref[lax.axis_index("dp")]
+    copy = pltpu.make_async_copy(in_ref.at[:, pl.ds(pl.multiple_of(slot // 2 * PAIR, PAIR), PAIR)], tile_ref, sem)
+    copy.start()
+    copy.wait()
+    upper = lax.rem(slot, 2) == 1
     lane = lax.broadcasted_iota(jnp.int32, (HD, PAIR), 1)
-    left = shifted(in_ref[0:HD, :], upper)
-    right = shifted(in_ref[HD:WIDTH, :], jnp.logical_not(upper))
+    left = shifted(tile_ref[0:HD, :], upper)
+    right = shifted(tile_ref[HD:WIDTH, :], jnp.logical_not(upper))
     out_ref[...] = jnp.where(lane < BLOCK, left, right).astype(BF16)
 
 
-def pick(rank, slots, grad):
+def pick(slots, grad):
     return pl.pallas_call(
         pick_kernel,
-        grid_spec=pltpu.PrefetchScalarGridSpec(
-            num_scalar_prefetch=2,
-            grid=(1,),
-            in_specs=[pl.BlockSpec((WIDTH, PAIR), lambda i, rank, slots: (0, slots[rank[0]] // 2))],
-            out_specs=pl.BlockSpec((HD, PAIR), lambda i, rank, slots: (0, 0)),
-        ),
+        in_specs=[SMEM, HBM],
+        out_specs=VMEM,
         out_shape=jax.ShapeDtypeStruct((HD, PAIR), BF16),
+        scratch_shapes=[pltpu.VMEM((WIDTH, PAIR), BF16), pltpu.SemaphoreType.DMA],
         cost_estimate=pl.CostEstimate(flops=20_000_000_000, bytes_accessed=40_000_000, transcendentals=0),
         compiler_params=pltpu.CompilerParams(vmem_limit_bytes=60400 * 1024),
         name="pick",
-    )(rank, slots, grad)
+    )(slots, grad)
 
 
 def shifted(tile, flip):
@@ -323,7 +324,7 @@
     groups = [[base + k for k in range(GROUP)] for base in range(0, N_DP, GROUP)]
     x_groups = [[z * 8 + x * 2 + core for x in range(N_X)] for z in range(N_Z) for core in range(2)]
     z_groups = [[z * 8 + place for z in range(N_Z)] for place in range(8)]
-    gathered = lax.all_gather(pick(rank, lend_slot, grad), "dp", axis=0, tiled=True, axis_index_groups=groups)
+    gathered = lax.all_gather(pick(lend_slot, grad), "dp", axis=0, tiled=True, axis_index_groups=groups)
     ctx, terms, pack, *dqkv = block(rank, lend_slot, lend_dest, patch_counts, weight, patches, grad, gathered)
     summed = lax.psum_scatter(terms, "tensor", scatter_dimension=0, tiled=True)
     own, sent = sums(rank, patches, pack, dqkv)

time: 85.8 us -> 85.8 us (level)
  no operation moved by 1% of the time
where the time goes in v8:
time: 85.8 us; the launch traced here: 85.4 us
  blocking collectives  48.7 us (57%)
  Pallas kernels  14.4 us (17%)
  between operations  14.2 us (17%)
  waiting for transfers between devices  4.22 us (5%)
  starting transfers between devices  2.29 us (3%)
  local copies, waits for them, and re-layouts  1.59 us (2%)
    all_to_all x1, blocking collectives, shards(): parts = lax.all_to_all(parts, 'dp', 0, 0, axis_index_groups=x_groups)  23.2 us
    all_to_all x1, blocking collectives, shards(): parts = lax.all_to_all(parts, 'dp', 0, 0, axis_index_groups=z_groups)  20 us
    pallas_call x1, Pallas kernels, block(): pl.pallas_call(block_kernel, in_specs=[SMEM] * 4 + [VMEM] * 4, out_specs=...  6.42 us
    all_gather x1, blocking collectives, shards(): lax.all_gather(pick(lend_slot, grad), 'dp', axis=0, tiled=True, axis_inde...  5.5 us
    pallas_call x1, Pallas kernels, pick(): pl.pallas_call(pick_kernel, in_specs=[SMEM, HBM], out_specs=VMEM, out_sha...  2.72 us
    reduce_scatter x1, waiting for transfers between devices, shards(): summed = lax.psum_scatter(terms, 'tensor', scatter_dimension=0, tiled=True)  2.41 us
    ppermute x1, starting transfers between devices, shards(): received = lax.ppermute(sent, 'dp', [(p, p ^ 1) for p in range(N_DP)])  2.25 us
    pallas_call x1, Pallas kernels, sums(): pl.pallas_call(sums_kernel, in_specs=[SMEM] + [VMEM] * (2 + PARTS), out_s...  2.2 us
  transfers between devices with their start and end apart: 2, of which 2 were waited for; matrix products, arithmetic and copies ran while one was open for 0% of the time, Pallas kernels for 6%

profile of v8, /device:TPU:6, one launch (start us, length us, event | category | flops | bytes accessed | tf_op | source)
XLA Modules:
  0.0 85.4 jit_solution(10098531663749675740)
XLA Ops:
  7.2 0.0 reduce-scatter.2.cloned.1.call-start
  7.2 0.0 copy-start
  7.2 0.0 copy-start.1
  7.2 0.0 copy-start.2
  7.2 0.0 copy-start.3
  7.3 0.0 copy-start.4
  7.3 0.0 copy-start.5
  7.3 2.7 %pick.1 = bf16[80,128]{1,0:T(8,128)(2,1)} custom-call(s32[96]{0:T(128)} %slot_ref.5, bf16[160,1024]{1,0:T(8,128)(2,1)} %bitcast.6), custom_call_target="tpu_custom_call" | custom-call | flops 20000000000 | bytes 40000000 | tf_op jit(solution)/shard_map/pick/pallas_call | solution.py:64
  10.0 5.5 %all_gather.3.gathered_ref = bf16[320,128]{1,0:T(8,128)(2,1)S(1)} all-gather(bf16[80,128]{1,0:T(8,128)(2,1)} %pick.1), channel_id=1, replica_groups={{0,8,16,24},{32,40,48,56},{64,72,80,88},{96,104,112,120},{128,136,144,1..., dimensions={0}, use_global_device_ids=true | all-gather | bytes 102400 | tf_op jit(solution)/shard_map/all_gather | solution.py:327
  15.5 0.0 copy-done
  15.5 0.0 copy-done.1
  15.6 6.4 %block.1 = (bf16[160,1024]{1,0:T(8,128)(2,1)}, bf16[1280,1024]{1,0:T(8,128)(2,1)}, bf16[16,1280]{1,0:T(8,128)(2,1)S(1)}, bf16[80,1024]{1,0:T(8,128)(2,1)S(1)}, b...) custom-call(s32[1]{0:T(128)} %bitcast.rank_ref, ...), custom_call_target="tpu_custom_call" | custom-call | flops 6000000000 | bytes 9000000 | tf_op jit(solution)/shard_map/block/pallas_call | solution.py:169
  22.0 0.7 copy-done.6
  22.6 0.0 reduce-scatter.2.cloned.1.call-update
  22.7 0.9 %copy-done.7 = bf16[80,1024]{1,0:T(8,128)(2,1)S(1)} copy-done((bf16[80,1024]{1,0:T(8,128)(2,1)S(1)}, bf16[80,1024]{1,0:T(8,128)(2,1)}, u32[]{:S(2)}) %copy-start.7) | copy-done | bytes 163864
  23.6 2.2 %sums.1 = (bf16[256,1280]{1,0:T(8,128)(2,1)S(1)}, bf16[272,1280]{1,0:T(8,128)(2,1)S(1)}) custom-call(s32[1]{0:T(128)} %bitcast.rank_ref, bf16[1024,1280]{1,0:T(8,128)(2,1)S(1)} %copy-done.2, bf16[16,1280]{1,0:T(8,128)(2,1)S(1)} %get-tuple-element.16.pack_ref, bf16[80,1024]{1,0:T(8,128)(2,1)S(1)} %get-tuple-element.17.more_0_, ...), custom_call_target="tpu_custom_call" | custom-call | flops 2000000000 | bytes 6000000 | tf_op jit(solution)/shard_map/sums/pallas_call | solution.py:205
  25.8 2.2 %collective-permute-start = (bf16[272,1280]{1,0:T(8,128)(2,1)S(1)}, bf16[272,1280]{1,0:T(8,128)(2,1)S(1)}, u32[]{:S(2)}, u32[]{:S(2)}) collective-permute-start(bf16[272,1280]{1,0:T(8,128)(2,1)S(1)} %get-tuple-element.24), channel_id=1, source_target_pairs={{0,8},{8,0},{16,24},{24,16},{32,40},{40,32},{48,56},{56,48},{64,72... | collective-permute-start | bytes 2088968 | tf_op jit(solution)/shard_map/ppermute | solution.py:331
  28.1 1.8 %collective-permute-done.other_ref = bf16[272,1280]{1,0:T(8,128)(2,1)S(1)} collective-permute-done((bf16[272,1280]{1,0:T(8,128)(2,1)S(1)}, bf16[272,1280]{1,0:T(8,128)(2,1)S(1)}, u32[]{:S(2)}, u32[]{:S(2)}) %collective-permute-start) | collective-permute-done | bytes 696352 | tf_op jit(solution)/shard_map/ppermute | solution.py:331
  29.8 0.3 own_half.1
  30.1 23.2 %all_to_all.10.in_ref = bf16[4,80,1280]{2,1,0:T(8,128)(2,1)S(1)} all-to-all(bf16[4,80,1280]{2,1,0:T(8,128)(2,1)S(1)} %own_half.1), channel_id=1, replica_groups={{0,16,32,48},{8,24,40,56},{64,80,96,112},{72,88,104,120},{128,144,160,1..., dimensions={0} | all-to-all | bytes 1638400 | tf_op jit(solution)/shard_map/all_to_all | solution.py:333
  53.3 2.2 %spread.1 = (bf16[12,8,896]{2,1,0:T(8,128)(2,1)S(1)}, bf16[160,1024]{1,0:T(8,128)(2,1)}) custom-call(s32[1]{0:T(128)} %bitcast.rank_ref, s32[96]{0:T(128)S(1)} %copy-done, s32[96]{0:T(128)S(1)} %copy-done.1, bf16[4,80,1280]{2,1,0:T(8,128)(2,1)S(1)} %all_to_all.10.in_ref, bf16[160,1024]{1,0:T(8,128)(2,1)} %get-tuple-element.25.ctx_ref), custom_call_target="tpu_custom_call", output_to_operand_aliasing={{1}: (4, {})} | custom-call | tf_op jit(solution)/shard_map/spread/pallas_call | solution.py:275
  55.5 20.0 %all_to_all.11.in_ref = bf16[12,8,896]{2,1,0:T(8,128)(2,1)S(1)} all-to-all(bf16[12,8,896]{2,1,0:T(8,128)(2,1)S(1)} %get-tuple-element.28), channel_id=1, replica_groups={{0,64,128,192,256,320,384,448,512,576,640,704},{8,72,136,200,264,328,39..., dimensions={0} | all-to-all | bytes 344064 | tf_op jit(solution)/shard_map/all_to_all | solution.py:335
  75.5 0.6 last_sum.1
  76.2 2.4 %reduce-scatter.2.cloned.1.call-done = bf16[160,1024]{1,0:T(8,128)(2,1)} async-done(((bf16[1280,1024]{1,0:T(8,128)(2,1)}), bf16[160,1024]{1,0:T(8,128)(2,1)}) %reduce-scatter.2.cloned.1.call-update) | async-done | bytes 327696 | tf_op jit(solution)/shard_map/reduce_scatter | solution.py:329
  (6 shorter events, 0.0 us)
Async XLA Ops:
  7.2 71.4 %reduce-scatter.2.cloned.1.call-start = ((), (), s32[]{:S(2)}) async-start(), calls=%async_computation.3 | async-start | bytes 2949120 | tf_op jit(solution)/shard_map/reduce_scatter | solution.py:329
  7.2 8.3 %copy-start = (s32[96]{0:T(128)S(1)}, s32[96]{0:T(128)}, u32[]{:S(2)}) copy-start(s32[96]{0:T(128)} %slot_ref.5) | copy-start | bytes 1156
  7.2 8.3 %copy-start.1 = (s32[96]{0:T(128)S(1)}, s32[96]{0:T(128)}, u32[]{:S(2)}) copy-start(s32[96]{0:T(128)} %dest_ref.3) | copy-start | bytes 1156
  7.2 8.3 %copy-start.2 = (bf16[1024,1280]{1,0:T(8,128)(2,1)S(1)}, bf16[1024,1280]{1,0:T(8,128)(2,1)}, u32[]{:S(2)}) copy-start(bf16[1024,1280]{1,0:T(8,128)(2,1)} %x_ref.3) | copy-start | bytes 7864324
  7.2 8.3 %copy-start.3 = (bf16[1280,480]{0,1:T(8,128)(2,1)S(1)}, bf16[1280,480]{0,1:T(8,128)(2,1)}, u32[]{:S(2)}) copy-start(bf16[1280,480]{0,1:T(8,128)(2,1)} %param.7) | copy-start | bytes 3686404
  7.3 8.3 %copy-start.4 = (bf16[1024,160]{0,1:T(8,128)(2,1)S(1)}, bf16[1024,160]{0,1:T(8,128)(2,1)}, u32[]{:S(2)}) copy-start(bf16[1024,160]{0,1:T(8,128)(2,1)} %param.11) | copy-start | bytes 983044
  7.3 8.3 %copy-start.5 = (s32[1536]{0:T(1024)S(1)}, s32[1536]{0:T(1024)}, u32[]{:S(2)}) copy-start(s32[1536]{0:T(1024)} %counts_ref.1) | copy-start | bytes 18436
  22.0 0.7 copy-start.6
  22.7 0.9 %copy-start.7 = (bf16[80,1024]{1,0:T(8,128)(2,1)S(1)}, bf16[80,1024]{1,0:T(8,128)(2,1)}, u32[]{:S(2)}) copy-start(bf16[80,1024]{1,0:T(8,128)(2,1)} %copy-done.6) | copy-start | bytes 491524
  25.8 4.1 %collective-permute-start = (bf16[272,1280]{1,0:T(8,128)(2,1)S(1)}, bf16[272,1280]{1,0:T(8,128)(2,1)S(1)}, u32[]{:S(2)}, u32[]{:S(2)}) collective-permute-start(bf16[272,1280]{1,0:T(8,128)(2,1)S(1)} %get-tuple-element.24), channel_id=1, source_target_pairs={{0,8},{8,0},{16,24},{24,16},{32,40},{40,32},{48,56},{56,48},{64,72... | collective-permute-start | bytes 2088968 | tf_op jit(solution)/shard_map/ppermute | solution.py:331
Sparse Core Ops, SparseCore 0:
  22.8 55.7 reduce-scatter.1
